TPU v7x, 256 devices: a whole 4x4x8 slice. The times are simulated.
256 devices in a mesh: gx: 16 (over z, x_lo), gy: 16 (over x_hi, y, core).
Axes of the slice: x: 4 (x_hi: 2, x_lo: 2; x = x_hi * 2 + x_lo), y: 4, z: 8, core: 2. Of those that a mesh axis runs over, the one named last changes fastest.
Arguments:
- floe_position: float32 [16, 16, 2, 4096], P('gx', 'gy'), may hold values from 0 to 1
- floe_velocity: float32 [16, 16, 2, 4096], P('gx', 'gy'), may hold values from -4 to 4
- floe_radius: float32 [16, 16, 4096], P('gx', 'gy'), may hold values from 0.08 to 0.3
- floe_thickness: float32 [16, 16, 4096], P('gx', 'gy'), may hold values from 0.5 to 2
- tracers: float32 [16, 16, 16, 4096], P('gx', 'gy'), may hold values from 0.5 to 2
- ghost_lists: int32 [16, 16, 4, 1024], P('gx', 'gy'), may hold values from 0 to 4095
- pair_first: int32 [16, 16, 8192], P('gx', 'gy'), may hold values from 0 to 4095
- pair_second: int32 [16, 16, 8192], P('gx', 'gy'), may hold values from 0 to 8191
- pair_count: int32 [16, 16], P('gx', 'gy'), may hold values from 512 to 8192, as said below
- cell_index: int32 [16, 16, 4096], P('gx', 'gy'), may hold values from 0 to 65535
Outputs:
- new_velocity: float32 [16, 16, 2, 4096], P('gx', 'gy')
- remapped: float32 [16, 4096, 4096], P(None, 'gx', 'gy')
- smoothed: float32 [16, 4096, 4096], P(None, 'gx', 'gy')
Inputs may be any that keep to these rules, and one draw needn't show every extreme that they name: Only the first pair_count slots of a block are live; some block has all 8192 slots live.
All inputs are finite; a program needn't handle non-finite values.
Results may differ from a plain program's by a relative error of at most 0.0003.
Values sent between devices are 32-bit elements; how exact they have to be, the bound alone decides.
No kernel may reach another device: no remote copies, remote signals or barrier semaphores. Data moves between devices by JAX's collectives and lax.ppermute only.
A program may use at most 64 MiB of HBM per device.

v0:
```python
import math

import jax
import jax.numpy as jnp
from jax import lax
from jax.sharding import PartitionSpec as P

CX = 256
CY = 256
HALO = 16


stiffness = 1.0
damping = 0.2
soft_width = 0.5
core_sq = 0.0025


def with_halo(cells, sides, width, closed):
    for axis, dim in sides:
        count = lax.axis_size(axis)
        ends = count if closed else count - 1
        head = lax.slice_in_dim(cells, 0, width, axis=dim)
        tail = lax.slice_in_dim(cells, cells.shape[dim] - width, cells.shape[dim], axis=dim)
        cells = jnp.concatenate(
            [
                lax.ppermute(tail, axis, [(i, (i + 1) % count) for i in range(ends)]),
                cells,
                lax.ppermute(head, axis, [((i + 1) % count, i) for i in range(ends)]),
            ],
            axis=dim,
        )
    return cells


def contact_terms(near_floes, far_floes):
    gap_x = near_floes[0] - far_floes[0]
    gap_y = near_floes[1] - far_floes[1]
    spread = jnp.sqrt(gap_x * gap_x + gap_y * gap_y + core_sq)
    normal_x = gap_x / spread
    normal_y = gap_y / spread
    intersection = near_floes[4] + far_floes[4] - spread
    eff_radius = near_floes[4] * far_floes[4] / (near_floes[4] + far_floes[4])
    closing = (near_floes[2] - far_floes[2]) * normal_x + (near_floes[3] - far_floes[3]) * normal_y
    magnitude = eff_radius * (
        stiffness * soft_width * jax.nn.softplus(intersection / soft_width) - damping * closing
    )
    return jnp.stack([magnitude * normal_x, magnitude * normal_y, magnitude * spread])


def one_hots(block_index, high_count):
    high = block_index // 128
    low = block_index - high * 128
    high_hot = (high[:, None] == lax.broadcasted_iota(jnp.int32, (1, high_count), 1)).astype(
        jnp.float32
    )
    low_hot = (low[:, None] == lax.broadcasted_iota(jnp.int32, (1, 128), 1)).astype(jnp.float32)
    return (high_hot, low_hot)


def take_columns(table, index):
    rows = table.shape[0]
    high_count = table.shape[1] // 128
    shaped = table.reshape(rows, high_count, 128)
    length = index.shape[0]
    block = math.gcd(length, 512)

    def one_block(block_index):
        high_hot, low_hot = one_hots(block_index, high_count)
        picked = jnp.einsum("ph,rhl->prl", high_hot, shaped, precision=lax.Precision.HIGHEST)
        return jnp.sum(picked * low_hot[:, None, :], axis=2).T

    pieces = lax.map(one_block, index.reshape(length // block, block))
    return jnp.transpose(pieces, (1, 0, 2)).reshape(rows, length)


def sum_columns(terms, index, width):
    rows = terms.shape[0]
    high_count = width // 128
    length = index.shape[0]
    block = math.gcd(length, 512)
    blocked_terms = jnp.transpose(terms.reshape(rows, length // block, block), (1, 0, 2))
    blocked_index = index.reshape(length // block, block)

    def add_block(total, items):
        term_block, block_index = items
        high_hot, low_hot = one_hots(block_index, high_count)
        weighted = term_block.T[:, :, None] * low_hot[:, None, :]
        return (
            total + jnp.einsum("ph,prl->rhl", high_hot, weighted, precision=lax.Precision.HIGHEST),
            None,
        )

    start = jnp.zeros((rows, high_count, 128), jnp.float32)
    total, unused = lax.scan(add_block, start, (blocked_terms, blocked_index))
    return total.reshape(rows, width)


def band_matrix(count):
    rows = lax.broadcasted_iota(jnp.int32, (count, count + 2 * HALO), 0)
    cols = lax.broadcasted_iota(jnp.int32, (count, count + 2 * HALO), 1)
    offset = (cols - rows - HALO).astype(jnp.float32)
    weights = jnp.exp(-2.0 * offset * offset / (HALO * HALO))
    tap_offsets = jnp.arange(2 * HALO + 1).astype(jnp.float32) - HALO
    total = jnp.sum(jnp.exp(-2.0 * tap_offsets * tap_offsets / (HALO * HALO)))
    inside = (cols >= rows) & (cols <= rows + 2 * HALO)
    return jnp.where(inside, weights / total, 0.0)


def filter_x(padded):
    band = band_matrix(padded.shape[1] - 2 * HALO)
    return jnp.einsum("ab,cbw->caw", band, padded, precision=lax.Precision.HIGHEST)


def filter_y(padded):
    band = band_matrix(padded.shape[2] - 2 * HALO)
    return jnp.einsum("cxb,yb->cxy", padded, band, precision=lax.Precision.HIGHEST)


def shards(
    floe_position,
    floe_velocity,
    floe_radius,
    floe_thickness,
    tracers,
    ghost_lists,
    pair_first,
    pair_second,
    pair_count,
    cell_index,
):
    own_floes = jnp.concatenate(
        [
            floe_position[0, 0],
            floe_velocity[0, 0],
            floe_radius[0, 0][None],
            floe_thickness[0, 0][None],
        ],
        axis=0,
    )
    count = own_floes.shape[1]
    send_rows = ghost_lists[0, 0]
    near_index = pair_first[0, 0]
    far_index = pair_second[0, 0]
    live = (jnp.arange(near_index.shape[0]) < pair_count[0, 0]).astype(jnp.float32)
    near_floes = take_columns(own_floes, near_index)
    ghost_count = send_rows.shape[1]
    picked_rows = take_columns(own_floes, send_rows.reshape(4 * ghost_count))
    outgoing = jnp.transpose(picked_rows.reshape(6, 4, ghost_count), (1, 0, 2))
    along_gx = with_halo(outgoing[0:2], (("gx", 0),), 1, True)
    along_gy = with_halo(outgoing[2:4], (("gy", 0),), 1, False)
    from_left = along_gx[0].at[0].add(-1.0)
    from_right = along_gx[3].at[0].add(1.0)
    from_below = along_gy[0].at[1].add(-1.0)
    from_above = along_gy[3].at[1].add(1.0)
    ghost_table = jnp.concatenate([from_left, from_right, from_below, from_above], axis=1)
    table = jnp.concatenate([own_floes, ghost_table], axis=1)
    far_floes = take_columns(table, far_index)
    sums = sum_columns(contact_terms(near_floes, far_floes) * live, near_index, count)
    radius = own_floes[4]
    velocity = own_floes[2:4] + sums[0:2] / (radius * radius * own_floes[5])
    pressure = sums[2] / (radius * radius)
    values = tracers[0, 0] * pressure
    cells = cell_index[0, 0]
    remapped = sum_columns(values, cells, CX * CY)
    remapped = remapped.reshape(values.shape[0], CX, CY)
    extended = with_halo(remapped, (("gx", 1),), HALO, True)
    along_x = filter_x(extended)
    widened = with_halo(along_x, (("gy", 2),), HALO, False)
    smoothed = filter_y(widened)
    return (velocity[None, None], remapped, smoothed)


def solution(mesh):
    placed = (
        P("gx", "gy", None, None),
        P("gx", "gy", None, None),
        P("gx", "gy", None),
        P("gx", "gy", None),
        P("gx", "gy", None, None),
        P("gx", "gy", None, None),
        P("gx", "gy", None),
        P("gx", "gy", None),
        P("gx", "gy"),
        P("gx", "gy", None),
    )
    return jax.shard_map(
        shards,
        mesh=mesh,
        in_specs=placed,
        out_specs=(P("gx", "gy", None, None), P(None, "gx", "gy"), P(None, "gx", "gy")),
        check_vma=False,
    )
```

profile of v0, /device:TPU:25, one launch (start us, length us, event | category | flops | bytes accessed | tf_op | source)
XLA Modules:
  0.0 197.3 jit_solution(11329177101839126112)
XLA Ops:
  2.9 8.0 %while.67 = (s32[]{:T(128)}, f32[8,6,512]{2,1,0:T(8,128)S(1)}, s32[8,512]{1,0:T(8,128)S(1)}, f32[6,32,128]{2,1,0:T(8,128)S(1)}, s32[]{:T(128)}) while((s32[]{:T(128)}, f32[8,6,512]{2,1,0:T(8,128)S(1)}, s32[8,512]{1,0:T(8,128)S(1)}, f32[6,32,128]{2,1,0:T(8,128)S(1)}, s32[]{:T(128)}) %tuple.166), condition=%wide.region_5.6_spmd, body=%wide.region_3.5_spmd.sunk | while | flops 151934464 | bytes 682061 | solution.py:73
  5.0 0.9 multiply_reduce_fusion.8
  7.0 0.9 multiply_reduce_fusion.8
  9.0 0.9 multiply_reduce_fusion.8
  11.0 2.7 %collective-permute-start.3 = (f32[1,6,1024]{2,1,0:T(8,128)S(1)}, f32[1,6,1024]{2,1,0:T(8,128)S(1)}, u32[]{:S(2)}, u32[]{:S(2)}) collective-permute-start(f32[1,6,1024]{2,1,0:T(8,128)S(1)} %get-tuple-element.425), channel_id=1, source_target_pairs={{1,0},{2,1},{3,2},{4,3},{5,4},{6,5},{7,6},{8,7},{9,8},{10,9},{11,1... | collective-permute-start | bytes 73736 | tf_op jit(solution)/shard_map/ppermute | solution.py:29
  13.7 6.6 %collective-permute-start.2 = (f32[1,6,1024]{2,1,0:T(8,128)S(1)}, f32[1,6,1024]{2,1,0:T(8,128)S(1)}, u32[]{:S(2)}, u32[]{:S(2)}) collective-permute-start(f32[1,6,1024]{2,1,0:T(8,128)S(1)} %get-tuple-element.426), channel_id=1, source_target_pairs={{0,1},{1,2},{2,3},{3,4},{4,5},{5,6},{6,7},{7,8},{8,9},{9,10},{10,1... | collective-permute-start | bytes 73736 | tf_op jit(solution)/shard_map/ppermute | solution.py:27
  20.3 6.6 %collective-permute-start.1 = (f32[1,6,1024]{2,1,0:T(8,128)S(1)}, f32[1,6,1024]{2,1,0:T(8,128)S(1)}, u32[]{:S(2)}, u32[]{:S(2)}) collective-permute-start(f32[1,6,1024]{2,1,0:T(8,128)S(1)} %get-tuple-element.427), channel_id=1, source_target_pairs={{16,0},{32,16},{48,32},{64,48},{80,64},{96,80},{112,96},{128,112},... | collective-permute-start | bytes 73736 | tf_op jit(solution)/shard_map/ppermute | solution.py:29
  28.9 18.0 %while.66 = (s32[]{:T(128)}, f32[16,6,512]{2,0,1:T(8,128)S(1)}, s32[16,512]{1,0:T(8,128)S(1)}, f32[6,32,128]{2,1,0:T(8,128)S(1)}, s32[]{:T(128)}, /*index=5*/s32[]{:T(128)}) while((s32[]{:T(128)}, f32[16,6,512]{2,0,1:T(8,128)S(1)}, s32[16,512]{1,0:T(8,128)S(1)}, f32[6,32,128]{2,1,0:T(8,128)S(1)}, s32[]{:T(128)}, /*index=5*/s32[]{:T(128)}) %tuple.183), condition=%wide.region_2.3_spmd, body=%wide.region_0.2_spmd.sunk | while | flops 151934464 | bytes 698453 | solution.py:73
  29.0 0.9 multiply_reduce_fusion.7
  31.3 0.9 multiply_reduce_fusion.7
  33.5 0.9 multiply_reduce_fusion.7
  34.6 0.9 multiply_reduce_fusion.7
  35.8 0.9 multiply_reduce_fusion.7
  36.9 0.9 multiply_reduce_fusion.7
  38.0 0.9 multiply_reduce_fusion.7
  39.1 0.9 multiply_reduce_fusion.7
  40.3 0.9 multiply_reduce_fusion.7
  41.4 0.9 multiply_reduce_fusion.7
  49.4 18.0 %while.68 = (s32[]{:T(128)}, f32[16,6,512]{2,0,1:T(8,128)S(1)}, s32[16,512]{1,0:T(8,128)S(1)}, f32[6,64,128]{2,1,0:T(8,128)S(1)}, s32[]{:T(128)}, /*index=5*/s32[]{:T(128)}) while((s32[]{:T(128)}, f32[16,6,512]{2,0,1:T(8,128)S(1)}, s32[16,512]{1,0:T(8,128)S(1)}, f32[6,64,128]{2,1,0:T(8,128)S(1)}, s32[]{:T(128)}, /*index=5*/s32[]{:T(128)}) %tuple.182), condition=%wide.region_8.9_spmd, body=%wide.region_6.8_spmd.sunk | while | flops 302945792 | bytes 796757 | solution.py:73
  49.4 0.9 multiply_reduce_fusion.9
  51.7 0.9 multiply_reduce_fusion.9
  53.9 0.9 multiply_reduce_fusion.9
  56.2 0.9 multiply_reduce_fusion.9
  58.4 0.9 multiply_reduce_fusion.9
  60.7 0.9 multiply_reduce_fusion.9
  62.9 0.9 multiply_reduce_fusion.9
  65.2 0.9 multiply_reduce_fusion.9
  67.5 12.0 %while.69 = (s32[]{:T(128)}, f32[3,32,128]{2,1,0:T(8,128)S(1)}, f32[16,3,512]{2,0,1:T(8,128)S(1)}, s32[16,512]{1,0:T(8,128)S(1)}, s32[]{:T(128)}, /*index=5*/s32[]{:T(128)}) while((s32[]{:T(128)}, f32[3,32,128]{2,1,0:T(8,128)S(1)}, f32[16,3,512]{2,0,1:T(8,128)S(1)}, s32[16,512]{1,0:T(8,128)S(1)}, s32[]{:T(128)}, ...), condition=%wide.region_10.11_spmd.clone, body=%wide.region_9.10_spmd.clone.sunk | while | flops 75874816 | bytes 667743 | solution.py:95
  79.6 54.7 %while.70 = (s32[]{:T(128)}, f32[16,512,128]{1,2,0:T(8,128)}, f32[8,16,512]{2,0,1:T(8,128)S(1)}, s32[8,512]{1,0:T(8,128)S(1)}, s32[]{:T(128)}, /*index=5*/s32[]{:T(128)}) while((s32[]{:T(128)}, f32[16,512,128]{1,2,0:T(8,128)}, f32[8,16,512]{2,0,1:T(8,128)S(1)}, s32[8,512]{1,0:T(8,128)S(1)}, s32[]{:T(128)}, ...), condition=%wide.region_12.13_spmd.clone, body=%wide.region_11.12_spmd.clone.sunk | while | flops 6445998592 | bytes 9091167 | solution.py:95
  79.8 5.4 %bitcast_add_fusion.2 = f32[16,512,128]{1,2,0:T(8,128)} fusion(f32[16,512,128]{1,2,0:T(8,128)} %get-tuple-element.656, pred[]{:T(512)S(6)} %compare.122, f32[512,128]{0,1:T(8,128)S(1)} %fusion.143, f32[512,16]{0,1:T(8,128)S(1)} %bitcast.146, s32[512]{0:T(512)S(1)} %get-tuple-element.579), kind=kOutput, calls=%fused_computation.67.clone.1 | convolution fusion | flops 6445858816 | bytes 8685569 | tf_op jit(solution)/shard_map/while/body/eval_jaxpr/ph,prl->rhl/dot_general | solution.py:90
  85.2 6.9 %bitcast_add_fusion.2 = f32[16,512,128]{1,2,0:T(8,128)} fusion(f32[16,512,128]{1,2,0:T(8,128)} %get-tuple-element.656, pred[]{:T(512)S(6)} %compare.122, f32[512,128]{0,1:T(8,128)S(1)} %fusion.143, f32[512,16]{0,1:T(8,128)S(1)} %bitcast.146, s32[512]{0:T(512)S(1)} %get-tuple-element.579), kind=kOutput, calls=%fused_computation.67.clone.1 | convolution fusion | flops 6445858816 | bytes 8685569 | tf_op jit(solution)/shard_map/while/body/eval_jaxpr/ph,prl->rhl/dot_general | solution.py:90
  92.3 6.9 %bitcast_add_fusion.2 = f32[16,512,128]{1,2,0:T(8,128)} fusion(f32[16,512,128]{1,2,0:T(8,128)} %get-tuple-element.656, pred[]{:T(512)S(6)} %compare.122, f32[512,128]{0,1:T(8,128)S(1)} %fusion.143, f32[512,16]{0,1:T(8,128)S(1)} %bitcast.146, s32[512]{0:T(512)S(1)} %get-tuple-element.579), kind=kOutput, calls=%fused_computation.67.clone.1 | convolution fusion | flops 6445858816 | bytes 8685569 | tf_op jit(solution)/shard_map/while/body/eval_jaxpr/ph,prl->rhl/dot_general | solution.py:90
  99.3 6.9 %bitcast_add_fusion.2 = f32[16,512,128]{1,2,0:T(8,128)} fusion(f32[16,512,128]{1,2,0:T(8,128)} %get-tuple-element.656, pred[]{:T(512)S(6)} %compare.122, f32[512,128]{0,1:T(8,128)S(1)} %fusion.143, f32[512,16]{0,1:T(8,128)S(1)} %bitcast.146, s32[512]{0:T(512)S(1)} %get-tuple-element.579), kind=kOutput, calls=%fused_computation.67.clone.1 | convolution fusion | flops 6445858816 | bytes 8685569 | tf_op jit(solution)/shard_map/while/body/eval_jaxpr/ph,prl->rhl/dot_general | solution.py:90
  106.3 6.9 %bitcast_add_fusion.2 = f32[16,512,128]{1,2,0:T(8,128)} fusion(f32[16,512,128]{1,2,0:T(8,128)} %get-tuple-element.656, pred[]{:T(512)S(6)} %compare.122, f32[512,128]{0,1:T(8,128)S(1)} %fusion.143, f32[512,16]{0,1:T(8,128)S(1)} %bitcast.146, s32[512]{0:T(512)S(1)} %get-tuple-element.579), kind=kOutput, calls=%fused_computation.67.clone.1 | convolution fusion | flops 6445858816 | bytes 8685569 | tf_op jit(solution)/shard_map/while/body/eval_jaxpr/ph,prl->rhl/dot_general | solution.py:90
  113.3 6.9 %bitcast_add_fusion.2 = f32[16,512,128]{1,2,0:T(8,128)} fusion(f32[16,512,128]{1,2,0:T(8,128)} %get-tuple-element.656, pred[]{:T(512)S(6)} %compare.122, f32[512,128]{0,1:T(8,128)S(1)} %fusion.143, f32[512,16]{0,1:T(8,128)S(1)} %bitcast.146, s32[512]{0:T(512)S(1)} %get-tuple-element.579), kind=kOutput, calls=%fused_computation.67.clone.1 | convolution fusion | flops 6445858816 | bytes 8685569 | tf_op jit(solution)/shard_map/while/body/eval_jaxpr/ph,prl->rhl/dot_general | solution.py:90
  120.4 6.9 %bitcast_add_fusion.2 = f32[16,512,128]{1,2,0:T(8,128)} fusion(f32[16,512,128]{1,2,0:T(8,128)} %get-tuple-element.656, pred[]{:T(512)S(6)} %compare.122, f32[512,128]{0,1:T(8,128)S(1)} %fusion.143, f32[512,16]{0,1:T(8,128)S(1)} %bitcast.146, s32[512]{0:T(512)S(1)} %get-tuple-element.579), kind=kOutput, calls=%fused_computation.67.clone.1 | convolution fusion | flops 6445858816 | bytes 8685569 | tf_op jit(solution)/shard_map/while/body/eval_jaxpr/ph,prl->rhl/dot_general | solution.py:90
  127.4 6.9 %bitcast_add_fusion.2 = f32[16,512,128]{1,2,0:T(8,128)} fusion(f32[16,512,128]{1,2,0:T(8,128)} %get-tuple-element.656, pred[]{:T(512)S(6)} %compare.122, f32[512,128]{0,1:T(8,128)S(1)} %fusion.143, f32[512,16]{0,1:T(8,128)S(1)} %bitcast.146, s32[512]{0:T(512)S(1)} %get-tuple-element.579), kind=kOutput, calls=%fused_computation.67.clone.1 | convolution fusion | flops 6445858816 | bytes 8685569 | tf_op jit(solution)/shard_map/while/body/eval_jaxpr/ph,prl->rhl/dot_general | solution.py:90
  134.3 5.3 %copy.20 = f32[16,512,128]{2,1,0:T(8,128)} copy(f32[16,512,128]{1,2,0:T(8,128)} %get-tuple-element.325) | data formatting | bytes 8388608 | tf_op jit(solution)/shard_map/while | solution.py:95
  139.7 5.2 %reshape_reshape.7 = f32[16,256,256]{2,1,0:T(8,128)} reshape(f32[16,512,128]{2,1,0:T(8,128)} %copy.20) | data formatting | bytes 8388608 | tf_op jit(solution)/shard_map/reshape;reshape | solution.py:166
  144.8 1.1 fusion.107
  146.0 3.8 %collective-permute-start.5 = (f32[16,16,256]{2,1,0:T(8,128)S(1)}, f32[16,16,256]{2,1,0:T(8,128)S(1)}, u32[]{:S(2)}, u32[]{:S(2)}) collective-permute-start(f32[16,16,256]{2,1,0:T(8,128)S(1)} %get-tuple-element.424), channel_id=1, source_target_pairs={{16,0},{32,16},{48,32},{64,48},{80,64},{96,80},{112,96},{128,112},... | collective-permute-start | bytes 786440 | tf_op jit(solution)/shard_map/ppermute | solution.py:29
  150.5 3.1 %collective-permute-done.4 = f32[16,16,256]{2,1,0:T(8,128)S(1)} collective-permute-done((f32[16,16,256]{2,1,0:T(8,128)S(1)}, f32[16,16,256]{2,1,0:T(8,128)S(1)}, u32[]{:S(2)}, u32[]{:S(2)}) %collective-permute-start.4) | collective-permute-done | bytes 262176 | tf_op jit(solution)/shard_map/ppermute | solution.py:27
  153.6 2.8 %collective-permute-done.5 = f32[16,16,256]{2,1,0:T(8,128)S(1)} collective-permute-done((f32[16,16,256]{2,1,0:T(8,128)S(1)}, f32[16,16,256]{2,1,0:T(8,128)S(1)}, u32[]{:S(2)}, u32[]{:S(2)}) %collective-permute-start.5) | collective-permute-done | bytes 262176 | tf_op jit(solution)/shard_map/ppermute | solution.py:29
  156.4 12.5 %fusion.52 = f32[16,256,256]{1,2,0:T(8,128)S(1)} fusion(f32[16,16,256]{2,1,0:T(8,128)S(1)} %collective-permute-done.5, f32[16,256,256]{2,1,0:T(8,128)} %reshape_reshape.7, f32[16,16,256]{2,1,0:T(8,128)S(1)} %collective-permute-done.4, f32[]{:T(128)} %fusion.92, s32[256]{0:T(256)S(1)} %iota_add_fusion), kind=kOutput, calls=%fused_computation.100 | convolution fusion | flops 3627048960 | bytes 8913924 | tf_op jit(solution)/shard_map/ab,cbw->caw/dot_general | solution.py:112
  169.0 4.6 %collective-permute-start.6 = (f32[16,256,16]{1,2,0:T(8,128)S(1)}, f32[16,256,16]{1,2,0:T(8,128)S(1)}, u32[]{:S(2)}, u32[]{:S(2)}) collective-permute-start(f32[16,256,16]{1,2,0:T(8,128)S(1)} %get-tuple-element.421), channel_id=1, source_target_pairs={{0,1},{1,2},{2,3},{3,4},{4,5},{5,6},{6,7},{7,8},{8,9},{9,10},{10,1... | collective-permute-start | bytes 786440 | tf_op jit(solution)/shard_map/ppermute | solution.py:27
  173.6 1.9 collective-permute-start.7
  176.9 8.0 %collective-permute-done.7 = f32[16,256,16]{1,2,0:T(8,128)S(1)} collective-permute-done((f32[16,256,16]{1,2,0:T(8,128)S(1)}, f32[16,256,16]{1,2,0:T(8,128)S(1)}, u32[]{:S(2)}, u32[]{:S(2)}) %collective-permute-start.7) | collective-permute-done | bytes 262176 | tf_op jit(solution)/shard_map/ppermute | solution.py:29
  184.9 12.4 %fusion.46 = f32[16,256,256]{2,1,0:T(8,128)} fusion(f32[16,256,16]{1,2,0:T(8,128)S(1)} %collective-permute-done.7, f32[16,256,256]{1,2,0:T(8,128)S(1)} %fusion.52, f32[16,256,16]{1,2,0:T(8,128)S(1)} %collective-permute-done.6, f32[]{:T(128)} %fusion.92, s32[256]{0:T(256)S(1)} %iota_add_fusion), kind=kOutput, calls=%fused_computation.94 | convolution fusion | flops 3627048960 | bytes 8913924 | tf_op jit(solution)/shard_map/cxb,yb->cxy/dot_general | solution.py:117
  (417 shorter events, 42.6 us)
Async XLA Ops:
  0.6 26.3 %copy-start.3 = (f32[1,1,4096]{2,1,0:T(1,128)S(1)}, f32[1,1,4096]{2,1,0:T(1,128)}, u32[]{:S(2)}) copy-start(f32[1,1,4096]{2,1,0:T(1,128)} %param.30) | copy-start | bytes 49156
  0.6 26.3 %copy-start.2 = (f32[1,1,4096]{2,1,0:T(1,128)S(1)}, f32[1,1,4096]{2,1,0:T(1,128)}, u32[]{:S(2)}) copy-start(f32[1,1,4096]{2,1,0:T(1,128)} %param.31) | copy-start | bytes 49156
  0.7 27.5 %copy-start.5 = (s32[1,1,8192]{2,1,0:T(1,128)S(1)}, s32[1,1,8192]{2,1,0:T(1,128)}, u32[]{:S(2)}) copy-start(s32[1,1,8192]{2,1,0:T(1,128)} %param.34) | copy-start | bytes 98308
  10.9 36.0 %copy-start = (f32[1,1,2,4096]{3,2,1,0:T(2,128)S(1)}, f32[1,1,2,4096]{3,2,1,0:T(2,128)}, u32[]{:S(2)}) copy-start(f32[1,1,2,4096]{3,2,1,0:T(2,128)} %param.29) | copy-start | bytes 98308
  10.9 36.0 %copy-start.4 = (f32[1,1,2,4096]{3,2,1,0:T(2,128)S(1)}, f32[1,1,2,4096]{3,2,1,0:T(2,128)}, u32[]{:S(2)}) copy-start(f32[1,1,2,4096]{3,2,1,0:T(2,128)} %param.28) | copy-start | bytes 98308
  11.0 36.1 %copy-start.7 = (s32[1,1,4096]{2,1,0:T(1,128)S(1)}, s32[1,1,4096]{2,1,0:T(1,128)}, u32[]{:S(2)}) copy-start(s32[1,1,4096]{2,1,0:T(1,128)} %param.37) | copy-start | bytes 49156
  11.0 36.8 %copy-start.6 = (s32[1,1,8192]{2,1,0:T(1,128)S(1)}, s32[1,1,8192]{2,1,0:T(1,128)}, u32[]{:S(2)}) copy-start(s32[1,1,8192]{2,1,0:T(1,128)} %param.35) | copy-start | bytes 98308
  11.0 37.5 %copy-start.1 = (f32[1,1,16,4096]{3,2,1,0:T(8,128)S(1)}, f32[1,1,16,4096]{3,2,1,0:T(8,128)}, u32[]{:S(2)}) copy-start(f32[1,1,16,4096]{3,2,1,0:T(8,128)} %param.32) | copy-start | bytes 786436
  11.0 37.7 %collective-permute-start.3 = (f32[1,6,1024]{2,1,0:T(8,128)S(1)}, f32[1,6,1024]{2,1,0:T(8,128)S(1)}, u32[]{:S(2)}, u32[]{:S(2)}) collective-permute-start(f32[1,6,1024]{2,1,0:T(8,128)S(1)} %get-tuple-element.425), channel_id=1, source_target_pairs={{1,0},{2,1},{3,2},{4,3},{5,4},{6,5},{7,6},{8,7},{9,8},{10,9},{11,1... | collective-permute-start | bytes 73736 | tf_op jit(solution)/shard_map/ppermute | solution.py:29
  13.7 35.0 %collective-permute-start.2 = (f32[1,6,1024]{2,1,0:T(8,128)S(1)}, f32[1,6,1024]{2,1,0:T(8,128)S(1)}, u32[]{:S(2)}, u32[]{:S(2)}) collective-permute-start(f32[1,6,1024]{2,1,0:T(8,128)S(1)} %get-tuple-element.426), channel_id=1, source_target_pairs={{0,1},{1,2},{2,3},{3,4},{4,5},{5,6},{6,7},{7,8},{8,9},{9,10},{10,1... | collective-permute-start | bytes 73736 | tf_op jit(solution)/shard_map/ppermute | solution.py:27
  20.3 28.4 %collective-permute-start.1 = (f32[1,6,1024]{2,1,0:T(8,128)S(1)}, f32[1,6,1024]{2,1,0:T(8,128)S(1)}, u32[]{:S(2)}, u32[]{:S(2)}) collective-permute-start(f32[1,6,1024]{2,1,0:T(8,128)S(1)} %get-tuple-element.427), channel_id=1, source_target_pairs={{16,0},{32,16},{48,32},{64,48},{80,64},{96,80},{112,96},{128,112},... | collective-permute-start | bytes 73736 | tf_op jit(solution)/shard_map/ppermute | solution.py:29
  26.9 22.2 %collective-permute-start = (f32[1,6,1024]{2,1,0:T(8,128)S(1)}, f32[1,6,1024]{2,1,0:T(8,128)S(1)}, u32[]{:S(2)}, u32[]{:S(2)}) collective-permute-start(f32[1,6,1024]{2,1,0:T(8,128)S(1)} %get-tuple-element.428), channel_id=1, source_target_pairs={{0,16},{16,32},{32,48},{48,64},{64,80},{80,96},{96,112},{112,128},... | collective-permute-start | bytes 73736 | tf_op jit(solution)/shard_map/ppermute | solution.py:27
  145.9 7.7 %collective-permute-start.4 = (f32[16,16,256]{2,1,0:T(8,128)S(1)}, f32[16,16,256]{2,1,0:T(8,128)S(1)}, u32[]{:S(2)}, u32[]{:S(2)}) collective-permute-start(f32[16,16,256]{2,1,0:T(8,128)S(1)} %get-tuple-element.423), channel_id=1, source_target_pairs={{0,16},{16,32},{32,48},{48,64},{64,80},{80,96},{96,112},{112,128},... | collective-permute-start | bytes 786440 | tf_op jit(solution)/shard_map/ppermute | solution.py:27
  146.0 10.4 %collective-permute-start.5 = (f32[16,16,256]{2,1,0:T(8,128)S(1)}, f32[16,16,256]{2,1,0:T(8,128)S(1)}, u32[]{:S(2)}, u32[]{:S(2)}) collective-permute-start(f32[16,16,256]{2,1,0:T(8,128)S(1)} %get-tuple-element.424), channel_id=1, source_target_pairs={{16,0},{32,16},{48,32},{64,48},{80,64},{96,80},{112,96},{128,112},... | collective-permute-start | bytes 786440 | tf_op jit(solution)/shard_map/ppermute | solution.py:29
  169.0 7.9 %collective-permute-start.6 = (f32[16,256,16]{1,2,0:T(8,128)S(1)}, f32[16,256,16]{1,2,0:T(8,128)S(1)}, u32[]{:S(2)}, u32[]{:S(2)}) collective-permute-start(f32[16,256,16]{1,2,0:T(8,128)S(1)} %get-tuple-element.421), channel_id=1, source_target_pairs={{0,1},{1,2},{2,3},{3,4},{4,5},{5,6},{6,7},{7,8},{8,9},{9,10},{10,1... | collective-permute-start | bytes 786440 | tf_op jit(solution)/shard_map/ppermute | solution.py:27
  173.6 11.3 %collective-permute-start.7 = (f32[16,256,16]{1,2,0:T(8,128)S(1)}, f32[16,256,16]{1,2,0:T(8,128)S(1)}, u32[]{:S(2)}, u32[]{:S(2)}) collective-permute-start(f32[16,256,16]{1,2,0:T(8,128)S(1)} %get-tuple-element.422), channel_id=1, source_target_pairs={{1,0},{2,1},{3,2},{4,3},{5,4},{6,5},{7,6},{8,7},{9,8},{10,9},{11,1... | collective-permute-start | bytes 786440 | tf_op jit(solution)/shard_map/ppermute | solution.py:29
where the time goes:
time: 198 us; the launch traced here: 197 us
  matrix products  123 us (62%)
  starting transfers between devices  26.3 us (13%)
  local copies, waits for them, and re-layouts  19.5 us (10%)
  waiting for transfers between devices  14.7 us (7%)
  other arithmetic  8.46 us (4%)
  loops' own time  3.49 us (2%)
    dot_general x24, matrix products, add_block(): jnp.einsum('ph,prl->rhl', high_hot, weighted, precision=lax.Precision.HIG...  62.2 us
    dot_general x40, matrix products, one_block(): jnp.einsum('ph,rhl->prl', high_hot, shaped, precision=lax.Precision.HIGHEST)  36 us
    ppermute x4, starting transfers between devices, with_halo(): lax.ppermute(head, axis, [((i + 1) % count, i) for i in range(ends)])  15 us
    dot_general x1, matrix products, filter_x(): jnp.einsum('ab,cbw->caw', band, padded, precision=lax.Precision.HIGHEST)  12.5 us
    dot_general x1, matrix products, filter_y(): jnp.einsum('cxb,yb->cxy', padded, band, precision=lax.Precision.HIGHEST)  12.4 us
    ppermute x4, starting transfers between devices, with_halo(): lax.ppermute(tail, axis, [(i, (i + 1) % count) for i in range(ends)])  11.2 us
    ppermute x4, waiting for transfers between devices, with_halo(): lax.ppermute(head, axis, [((i + 1) % count, i) for i in range(ends)])  10.8 us
    while x1, local copies, waits for them, and re-layouts, sum_columns(): total, unused = lax.scan(add_block, start, (blocked_terms, blocked_index))  5.33 us
  transfers between devices with their start and end apart: 8, of which 4 were waited for; matrix products, arithmetic and copies ran while one was open for 11% of the time, Pallas kernels for 0%

commit v1 on v0

v1 whole, which is shorter than its diff:
```python
import math

import jax
import jax.numpy as jnp
from jax import lax
from jax.experimental import pallas as pl
from jax.experimental.pallas import tpu as pltpu
from jax.sharding import PartitionSpec as P

F = 4096
G = 1024
NP = 8192
CH = 16
CX = 256
CY = 256
HALO = 16
MIB = 1024 * 1024

stiffness = 1.0
damping = 0.2
soft_width = 0.5
core_sq = 0.0025

TAP_TOTAL = sum(math.exp(-2.0 * (t - HALO) ** 2 / HALO**2) for t in range(2 * HALO + 1))

f32 = jnp.float32
bf16 = jnp.bfloat16
i32 = jnp.int32


def iota(shape, dim):
    return lax.broadcasted_iota(i32, shape, dim)


def row_block(start, size):
    return pl.ds(pl.multiple_of(start, size), size)


def split2(x):
    high = x.astype(bf16)
    return high, (x - high.astype(f32)).astype(bf16)


def dot_nn(a, b):
    return lax.dot_general(a, b, (((1,), (0,)), ((), ())), preferred_element_type=f32)


def dot_nt(a, b):
    return lax.dot_general(a, b, (((1,), (1,)), ((), ())), preferred_element_type=f32)


def dot3(a, b):
    ah, al = a
    bh, bl = b
    return dot_nn(ah, bh) + (dot_nn(ah, bl) + dot_nn(al, bh))


def taps_at(offset):
    o = offset.astype(f32)
    w = jnp.exp(o * o * (-2.0 / (HALO * HALO))) * (1.0 / TAP_TOTAL)
    return jnp.where(jnp.abs(offset) <= HALO, w, 0.0)


def lookup(row_of, rows, count, index, start=None):
    high = lax.shift_right_logical(index, 7)
    low = index & 127
    out = [jnp.zeros(index.shape, f32) for _ in range(rows)] if start is None else list(start)
    for h in range(count):
        here = high == h
        for r in range(rows):
            line = jnp.broadcast_to(row_of(r, h), index.shape)
            got = jnp.take_along_axis(line, low, axis=1, mode="promise_in_bounds")
            out[r] = jnp.where(here, got, out[r])
    return out


def floe_line(pos, vel, rad):
    def row_of(r, h):
        at = slice(128 * h, 128 * h + 128)
        if r < 2:
            return pos[0, 0, r : r + 1, at]
        if r < 4:
            return vel[0, 0, r - 2 : r - 1, at]
        return rad[0, 0:1, at]

    return row_of


def fetch(pairs, sem):
    copies = [pltpu.make_async_copy(a, b, sem.at[k]) for k, (a, b) in enumerate(pairs)]
    for copy in copies:
        copy.start()
    for copy in copies:
        copy.wait()


def outgoing_kernel(pos_h, vel_h, rad_h, lists_h, *refs):
    outs = refs[:4]
    pos, vel, rad, lists, lines, sem = refs[4:]
    fetch(((pos_h, pos), (vel_h, vel), (rad_h, rad), (lists_h, lists)), sem)
    row_of = floe_line(pos, vel, rad)
    for k in range(4):
        for s in range(8):
            lines[s : s + 1, :] = lists[0, 0, k : k + 1, 128 * s : 128 * s + 128]
        got = lookup(row_of, 5, 32, lines[...])
        for r in range(5):
            outs[k][8 * r : 8 * r + 8, :] = got[r]


def prepare_kernel(
    pos_h, vel_h, rad_h, tracers_h, first_h, second_h, cells_h,
    near, far, sorted_tracers, source, rows_out, cols_out, edges, uv,
    weighted, hot, cell_rows, pos, vel, rad, tracers, first, second, cells, sem,
):
    fetch(
        (
            (pos_h, pos), (vel_h, vel), (rad_h, rad), (tracers_h, tracers),
            (first_h, first), (second_h, second), (cells_h, cells),
        ),
        sem,
    )
    row_of = floe_line(pos, vel, rad)

    def gather_block(j, _):
        at = row_block(8 * j, 8)
        for index, dest in ((first, near), (second, far)):
            got = lookup(row_of, 5, 32, index[at, :])
            for r in range(5):
                dest[r, at, :] = got[r]
        return 0

    lax.fori_loop(0, 8, gather_block, 0)
    for h in range(32):
        at = slice(128 * h, 128 * h + 128)
        for r in range(2):
            uv[r, h : h + 1, :] = vel[0, 0, r : r + 1, at]

    cell = cells[...]
    bins = lax.shift_right_logical(cell, 12)
    hots = [jnp.where(bins == b, 1.0, 0.0).astype(f32) for b in range(16)]
    stacked = jnp.concatenate(hots, axis=0).astype(bf16)
    before = jnp.where(iota((128, 128), 0) < iota((128, 128), 1), 1.0, 0.0).astype(bf16)
    ones = jnp.ones((128, 128), bf16)
    inside = dot_nn(stacked, before)
    totals = dot_nn(stacked, ones).astype(bf16)
    lower = jnp.where(iota((512, 512), 1) < iota((512, 512), 0), 1.0, 0.0).astype(bf16)
    ahead = dot_nn(lower, totals)
    place = jnp.zeros((32, 128), f32)
    for b in range(16):
        at = slice(32 * b, 32 * b + 32)
        place = place + hots[b] * (ahead[at] + inside[at])
        edges[b : b + 1, :] = ahead[32 * b : 32 * b + 1].astype(i32)
    place = place.astype(i32)
    for q in range(32):
        at = slice(128 * q, 128 * q + 128)
        line = jnp.broadcast_to(place[q : q + 1, :], (128, 128))
        mine = lax.shift_right_logical(line[0:32], 7) == iota((32, 128), 0)
        weighted[0:32, at] = jnp.where(mine, float(q), 0.0).astype(bf16)
        weighted[32:64, at] = jnp.where(mine, iota((32, 128), 1).astype(f32), 0.0).astype(bf16)
        hot[:, at] = jnp.where((line & 127) == iota((128, 128), 0), 1.0, 0.0).astype(bf16)
    found = dot_nt(weighted[...], hot[...])
    source[...] = (found[0:32] * 128.0 + found[32:64]).astype(i32)

    cell_rows[...] = cell.astype(f32)
    for k in range(4):
        index = source[8 * k : 8 * k + 8, :]
        got = lookup(lambda r, h: cell_rows[h : h + 1, :], 1, 32, index)[0].astype(i32)
        for s in range(8):
            at = slice(1024 * k + 128 * s, 1024 * k + 128 * s + 128)
            rows_out[:, at] = lax.shift_right_logical(got[s : s + 1, :], 8)
            cols_out[:, at] = got[s : s + 1, :] & 255

    def tracer_block(q, _):
        index = jnp.broadcast_to(source[pl.ds(q, 1), :], (8, 128))
        high = lax.shift_right_logical(index, 7)
        low = index & 127
        parts = [jnp.zeros((8, 128), f32), jnp.zeros((8, 128), f32)]
        for h in range(32):
            here = high == h
            for c in range(2):
                block = tracers[0, 0, 8 * c : 8 * c + 8, 128 * h : 128 * h + 128]
                got = jnp.take_along_axis(block, low, axis=1, mode="promise_in_bounds")
                parts[c] = jnp.where(here, got, parts[c])
        for c in range(2):
            sorted_tracers[8 * c : 8 * c + 8, row_block(128 * q, 128)] = parts[c]
        return 0

    lax.fori_loop(0, 32, tracer_block, 0)


def pack_sides(cells, out, count, second):
    lane = iota((count, 128), 1)
    for g in range(2):
        head = jnp.zeros((count, 128), f32)
        tail = jnp.zeros((count, 128), f32)
        for k in range(8):
            mine = (lane >= 16 * k) & (lane < 16 * k + 16)
            left = cells[8 * g + k, :, 0:128]
            right = cells[8 * g + k, :, 128:256]
            head = jnp.where(mine, pltpu.roll(left, 16 * k, 1) if k else left, head)
            turn = (16 * k + 16) % 128
            tail = jnp.where(mine, pltpu.roll(right, turn, 1) if turn else right, tail)
        out[:, 128 * g : 128 * g + 128] = head
        out[:, second + 128 * g : second + 128 * g + 128] = tail


def scatter_step(step, b, c, values_high, values_low, rows_in, cols_in):
    at = row_block(256 * c, 256)
    local = jnp.broadcast_to(rows_in[:, at], (16, 256)) - 16 * b
    here = local == iota((16, 256), 0)
    columns = jnp.broadcast_to(cols_in[:, at], (256, 256))
    hot = jnp.where(columns == iota((256, 256), 0), 1.0, 0.0).astype(bf16)
    high, low = [], []
    for ch in range(CH):
        vh = jnp.broadcast_to(values_high[ch : ch + 1, at], (16, 256))
        vl = jnp.broadcast_to(values_low[ch : ch + 1, at], (16, 256))
        high.append(jnp.where(here, vh, 0.0).astype(bf16))
        low.append(jnp.where(here, vl, 0.0).astype(bf16))
    return dot_nt(jnp.concatenate(high, axis=0), hot) + dot_nt(jnp.concatenate(low, axis=0), hot)


def contact_kernel(
    count, edges_s,
    near, far, first, second, ghost0, ghost1, ghost2, ghost3, rad, thick, uv,
    sorted_tracers, source, rows_in, cols_in,
    new_velocity, values_high, values_low, head_rows, tail_rows, head_ends, tail_ends,
    weighted, hot, pressure_rows,
):
    ghosts = (ghost0, ghost1, ghost2, ghost3)
    shift = ((0, -1.0), (0, 1.0), (1, -1.0), (1, 1.0))
    live_count = count[0, 0]

    row = lax.axis_index("gy")
    inside = {2: row > 0, 3: row < lax.axis_size("gy") - 1}

    def ghost_line(r, h):
        k, s = h // 8, h % 8
        line = ghosts[k][8 * r + s : 8 * r + s + 1, :]
        if k in inside:
            line = jnp.where(jnp.full(line.shape, inside[k]), line, 0.0)
        return line + shift[k][1] if shift[k][0] == r else line

    def pair_block(j, _):
        at = row_block(8 * j, 8)
        index = second[at, :]
        outside = index >= F
        got = lookup(ghost_line, 5, 32, index - F)
        other = [jnp.where(outside, got[r], far[r, at, :]) for r in range(5)]
        own = [near[r, at, :] for r in range(5)]
        gap_x = own[0] - other[0]
        gap_y = own[1] - other[1]
        spread = jnp.sqrt(gap_x * gap_x + gap_y * gap_y + core_sq)
        normal_x = gap_x / spread
        normal_y = gap_y / spread
        reach = own[4] + other[4]
        depth = (reach - spread) / soft_width
        eff_radius = own[4] * other[4] / reach
        closing = (own[2] - other[2]) * normal_x + (own[3] - other[3]) * normal_y
        soft = jnp.maximum(depth, 0.0) + jnp.log1p(jnp.exp(-jnp.abs(depth)))
        magnitude = eff_radius * (stiffness * soft_width * soft - damping * closing)
        slot = 1024 * j + 128 * iota((8, 128), 0) + iota((8, 128), 1)
        magnitude = jnp.where(slot < live_count, magnitude, 0.0)
        terms = (magnitude * normal_x, magnitude * normal_y, magnitude * spread)
        halves = [split2(t) for t in terms]
        halves = [h[0].astype(f32) for h in halves] + [h[1].astype(f32) for h in halves]
        index = first[at, :]
        high = lax.shift_right_logical(index, 7)
        low = index & 127
        for s in range(8):
            lanes = row_block(1024 * j + 128 * s, 128)
            mine = jnp.broadcast_to(high[s : s + 1, :], (32, 128)) == iota((32, 128), 0)
            for t in range(6):
                spot = jnp.where(mine, jnp.broadcast_to(halves[t][s : s + 1, :], (32, 128)), 0.0)
                weighted[32 * t : 32 * t + 32, lanes] = spot.astype(bf16)
            match = jnp.broadcast_to(low[s : s + 1, :], (128, 128)) == iota((128, 128), 0)
            hot[:, lanes] = jnp.where(match, 1.0, 0.0).astype(bf16)
        return 0

    lax.fori_loop(0, 8, pair_block, 0)
    sums = dot_nt(weighted[...], hot[...])
    sums = [sums[32 * r : 32 * r + 32] + sums[96 + 32 * r : 128 + 32 * r] for r in range(3)]
    radius = rad[...]
    area = radius * radius
    for r in range(2):
        moved = uv[r] + sums[r] / (area * thick[...])
        for h in range(32):
            new_velocity[0, 0, r : r + 1, 128 * h : 128 * h + 128] = moved[h : h + 1, :]
    pressure_rows[...] = sums[2] / area

    def value_block(k, _):
        index = source[row_block(8 * k, 8), :]
        got = lookup(lambda r, h: pressure_rows[h : h + 1, :], 1, 32, index)[0]
        for s in range(8):
            at = row_block(1024 * k + 128 * s, 128)
            value = sorted_tracers[:, at] * jnp.broadcast_to(got[s : s + 1, :], (16, 128))
            top = value.astype(bf16).astype(f32)
            values_high[:, at] = top
            values_low[:, at] = (value - top).astype(bf16).astype(f32)
        return 0

    lax.fori_loop(0, 4, value_block, 0)

    for b, out, ends in ((0, head_rows, head_ends), (15, tail_rows, tail_ends)):
        begin = edges_s[b, 0]
        end = edges_s[1, 0] if b == 0 else F
        out[...] = jnp.zeros((CH, 16, CY), f32)

        def add_chunk(c, _, b=b, out=out):
            got = scatter_step(0, b, c, values_high, values_low, rows_in, cols_in)
            out[...] = out[...] + got.reshape(CH, 16, CY)
            return 0

        lax.fori_loop(
            lax.shift_right_logical(begin, 8), lax.shift_right_logical(end + 255, 8), add_chunk, 0
        )
        pack_sides(out, ends, 16, 256)


def grid_kernel(
    edges_s, values_high, values_low, rows_in, cols_in,
    field, sides,
):
    def step(i, carry):
        b, c, fresh = carry
        got = scatter_step(i, b, c, values_high, values_low, rows_in, cols_in)
        at = row_block(16 * b, 16)
        was = jnp.where(jnp.full((CH, 16, CY), fresh, i32) == 1, 0.0, field[:, at, :])
        field[:, at, :] = was + got.reshape(CH, 16, CY)
        following = jnp.where(b < 15, edges_s[jnp.minimum(b + 1, 15), 0], F + 1)
        up = (b < 15) & ((following <= 256 * c + 256) | (c == 15))
        return (
            jnp.where(up, b + 1, b),
            jnp.where(up, c, c + 1),
            jnp.where(up, 1, 0).astype(i32),
        )

    carry = (jnp.int32(0), jnp.int32(0), jnp.int32(1))
    for i in range(31):
        carry = step(i, carry)
    pack_sides(field, sides, CX, 256)


def own_filter_kernel(field, out, left_x, right_y):
    high, low = split2(taps_at(iota((CX, CX), 1) - iota((CX, CX), 0)))
    left_x[...] = jnp.concatenate([high, low, high], axis=1)
    right_y[...] = jnp.concatenate([high, low, high], axis=0)

    def two(k, _):
        for c in range(2):
            h, l = split2(field[2 * k + c])
            along = dot_nn(left_x[...], jnp.concatenate([h, h, l], axis=0))
            h, l = split2(along)
            out[2 * k + c] = dot_nn(jnp.concatenate([h, h, l], axis=1), right_y[...])
        return 0

    lax.fori_loop(0, CH // 2, two, 0)


def sides_kernel(own, side_l, side_r, out_h, work, sem):
    row = lax.axis_index("gy")
    ok_l, ok_r = row > 0, row < lax.axis_size("gy") - 1
    band = split2(taps_at(iota((CX, CX), 1) - iota((CX, CX), 0)))
    edge_up = split2(taps_at(iota((16, 16), 1) - 16 - iota((16, 16), 0)))
    edge_down = split2(taps_at(iota((16, 16), 1) + 16 - iota((16, 16), 0)))
    same = (iota((256, 256), 0) >> 4) == (iota((256, 256), 1) >> 4)
    delta = (iota((256, 256), 0) & 15) - (iota((256, 256), 1) & 15)
    parts = []
    for ref, ok, reach in ((side_l, ok_l, -16), (side_r, ok_r, 16)):
        rows = jnp.where(jnp.full((CX + 32, 256), ok), ref[...], 0.0)
        mid = dot3(band, split2(rows[16 : CX + 16]))
        top = mid[0:16] + dot3(edge_up, split2(rows[0:16]))
        low = mid[240:256] + dot3(edge_down, split2(rows[CX + 16 :]))
        along = jnp.concatenate([top, mid[16:240], low], axis=0)
        weights = split2(jnp.where(same, taps_at(delta + reach), 0.0))
        parts.append(dot3(split2(along), weights))
    lane = iota((CX, 128), 1)
    copies = []
    for ch in range(CH):
        g, k = ch // 8, ch % 8
        at = slice(128 * g, 128 * g + 128)
        left, right = parts[0][:, at], parts[1][:, at]
        turn = (128 - 16 * k) % 128
        left = pltpu.roll(left, turn, 1) if turn else left
        turn = (112 - 16 * k) % 128
        right = pltpu.roll(right, turn, 1) if turn else right
        work[ch, :, 0:128] = own[ch, :, 0:128] + jnp.where(lane < 16, left, 0.0)
        work[ch, :, 128:256] = own[ch, :, 128:256] + jnp.where(lane >= 112, right, 0.0)
        copy = pltpu.make_async_copy(work.at[ch], out_h.at[ch], sem.at[ch])
        copy.start()
        copies.append(copy)
    for copy in copies:
        copy.wait()


def ends_kernel(above, below, smoothed, out):
    g = pl.program_id(0)
    rows = jnp.where(jnp.full((CH, 16, CY), g, i32) == 0, above[...], below[...]).reshape(256, CY)
    band = split2(taps_at(iota((CY, CY), 1) - iota((CY, CY), 0)))
    across = dot3(split2(rows), band)
    same = (iota((256, 256), 0) >> 4) == (iota((256, 256), 1) >> 4)
    delta = (iota((256, 256), 1) & 15) - (iota((256, 256), 0) & 15)
    weights = split2(jnp.where(same, taps_at(delta + 32 * g - 16), 0.0))
    out[...] = smoothed[...] + dot3(weights, split2(across)).reshape(CH, 16, CY)


def vmem():
    return pl.BlockSpec(memory_space=pltpu.VMEM)


def anywhere():
    return pl.BlockSpec(memory_space=pl.ANY)


def smem():
    return pl.BlockSpec(memory_space=pltpu.SMEM)


def struct(*shape, dtype=f32):
    return jax.ShapeDtypeStruct(shape, dtype)


def params(mib):
    return pltpu.CompilerParams(vmem_limit_bytes=mib * MIB)


def cost(us, nbytes=1):
    return pl.CostEstimate(flops=int(us * 1.0e9), bytes_accessed=nbytes, transcendentals=0)


def shards(
    floe_position, floe_velocity, floe_radius, floe_thickness, tracers,
    ghost_lists, pair_first, pair_second, pair_count, cell_index,
):
    first = pair_first.reshape(64, 128)
    second = pair_second.reshape(64, 128)
    cells = cell_index.reshape(32, 128)
    radius = floe_radius.reshape(32, 128)
    thickness = floe_thickness.reshape(32, 128)
    nx, ny = lax.axis_size("gx"), lax.axis_size("gy")

    def ring(count):
        return [(i, (i + 1) % count) for i in range(count)]

    def back(count):
        return [((i + 1) % count, i) for i in range(count)]

    floe_scratch = [
        pltpu.VMEM((1, 1, 2, F), f32),
        pltpu.VMEM((1, 1, 2, F), f32),
        pltpu.VMEM((1, 1, F), f32),
    ]
    outgoing = pl.pallas_call(
        outgoing_kernel,
        in_specs=[anywhere()] * 4,
        out_shape=[struct(40, 128)] * 4,
        scratch_shapes=floe_scratch
        + [
            pltpu.VMEM((1, 1, 4, G), i32),
            pltpu.VMEM((8, 128), i32),
            pltpu.SemaphoreType.DMA((4,)),
        ],
        compiler_params=params(8),
        cost_estimate=cost(1),
        name="outgoing",
    )(floe_position, floe_velocity, floe_radius, ghost_lists)
    ghosts = [
        lax.ppermute(outgoing[1], "gx", ring(nx)),
        lax.ppermute(outgoing[0], "gx", back(nx)),
        lax.ppermute(outgoing[3], "gy", ring(ny)),
        lax.ppermute(outgoing[2], "gy", back(ny)),
    ]

    near, far, sorted_tracers, source, rows, cols, edges, uv = pl.pallas_call(
        prepare_kernel,
        in_specs=[anywhere()] * 7,
        out_shape=[
            struct(5, 64, 128),
            struct(5, 64, 128),
            struct(CH, F),
            struct(32, 128, dtype=i32),
            struct(1, F, dtype=i32),
            struct(1, F, dtype=i32),
            struct(16, 128, dtype=i32),
            struct(2, 32, 128),
        ],
        scratch_shapes=[
            pltpu.VMEM((64, F), bf16),
            pltpu.VMEM((128, F), bf16),
            pltpu.VMEM((32, 128), f32),
        ]
        + floe_scratch
        + [
            pltpu.VMEM((1, 1, CH, F), f32),
            pltpu.VMEM((64, 128), i32),
            pltpu.VMEM((64, 128), i32),
            pltpu.VMEM((32, 128), i32),
            pltpu.SemaphoreType.DMA((7,)),
        ],
        compiler_params=params(16),
        cost_estimate=cost(5),
        name="prepare",
    )(floe_position, floe_velocity, floe_radius, tracers, first, second, cells)

    new_velocity, values_high, values_low, head_rows, tail_rows, head_ends, tail_ends = pl.pallas_call(
        contact_kernel,
        in_specs=[smem(), smem()] + [vmem()] * 15,
        out_shape=[
            struct(1, 1, 2, F),
            struct(CH, F),
            struct(CH, F),
            struct(CH, 16, CY),
            struct(CH, 16, CY),
            struct(16, 512),
            struct(16, 512),
        ],
        scratch_shapes=[
            pltpu.VMEM((192, NP), bf16),
            pltpu.VMEM((128, NP), bf16),
            pltpu.VMEM((32, 128), f32),
        ],
        compiler_params=params(20),
        cost_estimate=cost(5),
        name="contact",
    )(
        pair_count, edges, near, far, first, second, *ghosts, radius, thickness, uv,
        sorted_tracers, source, rows, cols,
    )
    ends_above = lax.ppermute(tail_ends, "gx", ring(nx))
    ends_below = lax.ppermute(head_ends, "gx", back(nx))
    above = lax.ppermute(tail_rows, "gx", ring(nx))
    below = lax.ppermute(head_rows, "gx", back(nx))

    field, sides = pl.pallas_call(
        grid_kernel,
        in_specs=[smem()] + [vmem()] * 4,
        out_shape=[struct(CH, CX, CY), struct(CX, 512)],
        compiler_params=params(16),
        cost_estimate=cost(0.1),
        name="to_grid",
    )(edges, values_high, values_low, rows, cols)
    sides = jnp.concatenate([ends_above, sides, ends_below], axis=0)
    side_l = lax.ppermute(sides[:, 256:], "gy", ring(ny))
    side_r = lax.ppermute(sides[:, :256], "gy", back(ny))

    own = pl.pallas_call(
        own_filter_kernel,
        in_specs=[vmem()],
        out_specs=vmem(),
        out_shape=struct(CH, CX, CY),
        scratch_shapes=[pltpu.VMEM((CX, 3 * CX), bf16), pltpu.VMEM((3 * CY, CY), bf16)],
        compiler_params=params(12),
        cost_estimate=cost(0.1),
        name="own_filter",
    )(field)
    smoothed = pl.pallas_call(
        sides_kernel,
        in_specs=[vmem()] * 3,
        out_specs=anywhere(),
        out_shape=struct(CH, CX, CY),
        scratch_shapes=[pltpu.VMEM((CH, CX, CY), f32), pltpu.SemaphoreType.DMA((CH,))],
        compiler_params=params(14),
        cost_estimate=cost(0.1),
        name="add_sides",
    )(own, side_l, side_r)
    strip = pl.BlockSpec((CH, 16, CY), lambda g: (0, 15 * g, 0))
    smoothed = pl.pallas_call(
        ends_kernel,
        grid=(2,),
        in_specs=[pl.BlockSpec((CH, 16, CY), lambda g: (0, 0, 0))] * 2 + [strip],
        out_specs=strip,
        out_shape=struct(CH, CX, CY),
        input_output_aliases={2: 0},
        compiler_params=params(10),
        cost_estimate=cost(1),
        name="add_ends",
    )(above, below, smoothed)
    return (new_velocity, field, smoothed)


def solution(mesh):
    placed = (
        P("gx", "gy", None, None),
        P("gx", "gy", None, None),
        P("gx", "gy", None),
        P("gx", "gy", None),
        P("gx", "gy", None, None),
        P("gx", "gy", None, None),
        P("gx", "gy", None),
        P("gx", "gy", None),
        P("gx", "gy"),
        P("gx", "gy", None),
    )
    return jax.shard_map(
        shards,
        mesh=mesh,
        in_specs=placed,
        out_specs=(P("gx", "gy", None, None), P(None, "gx", "gy"), P(None, "gx", "gy")),
        check_vma=False,
    )
```

time: 198 us -> 73.2 us (0.37)
  matrix products: 123 us -> 0 us
  Pallas kernels: 0 us -> 38 us
  waiting for transfers between devices: 14.7 us -> 0.03 us
  local copies, waits for them, and re-layouts: 19.5 us -> 9.93 us
  other arithmetic: 8.46 us -> 0 us
  loops' own time: 3.49 us -> 0 us
  starting transfers between devices: 26.3 us -> 23 us
    dot_general x66 -> x0, matrix products: 123 us -> none  [the longest x24 62.2 us: add_block(): jnp.einsum('ph,prl->rhl', high_hot, weighted, precision=lax.Precision.HIG...]
    pallas_call x0 -> x7, Pallas kernels: none -> 38 us  [the longest x1 9.7 us: shards(): pl.pallas_call(prepare_kernel, in_specs=[anywhere()] * 7, out_shape=[stru...]
    ppermute x8 -> x10, waiting for transfers between devices: 14.7 us -> 0.03 us  [the longest x1 0.01 us: shards(): lax.ppermute(outgoing[1], 'gx', ring(nx))]
    unnamed x22 -> x32, local copies, waits for them, and re-layouts: 0.8 us -> 9.88 us
    another operation x7 -> x0, local copies, waits for them, and re-layouts: 5.96 us -> none  [the longest x1 5.18 us: shards(): remapped = remapped.reshape(values.shape[0], CX, CY)]
    while x1 -> x0, local copies, waits for them, and re-layouts: 5.33 us -> none  [sum_columns(): total, unused = lax.scan(add_block, start, (blocked_terms, blocked_index))]
    dynamic_update_slice x72 -> x0, local copies, waits for them, and re-layouts: 3.89 us -> none  [take_columns(): pieces = lax.map(one_block, index.reshape(length // block, block))]
    another operation x5 -> x0, loops' own time: 3.49 us -> none  [the longest x3 2.29 us: take_columns(): pieces = lax.map(one_block, index.reshape(length // block, block))]
  transfers between devices with their start and end apart: 8 -> 10, of which waited for: 4 -> 0; matrix products, arithmetic and copies ran while one was open for 11% -> 0% of each run, Pallas kernels for 0% -> 37%
where the time goes in v1:
time: 73.2 us; the launch traced here: 72.5 us
  Pallas kernels  38 us (52%)
  starting transfers between devices  23 us (31%)
  local copies, waits for them, and re-layouts  9.93 us (14%)
  between operations  1.46 us (2%)
    unnamed x32, local copies, waits for them, and re-layouts  9.88 us
    pallas_call x1, Pallas kernels, shards(): pl.pallas_call(prepare_kernel, in_specs=[anywhere()] * 7, out_shape=[stru...  9.7 us
    pallas_call x1, Pallas kernels, shards(): pl.pallas_call(contact_kernel, in_specs=[smem(), smem()] + [vmem()] * 15,...  6.77 us
    pallas_call x1, Pallas kernels, shards(): pl.pallas_call(grid_kernel, in_specs=[smem()] + [vmem()] * 4, out_shape=[...  6.73 us
    pallas_call x1, Pallas kernels, shards(): pl.pallas_call(own_filter_kernel, in_specs=[vmem()], out_specs=vmem(), ou...  6.59 us
    ppermute x1, starting transfers between devices, shards(): side_l = lax.ppermute(sides[:, 256:], 'gy', ring(ny))  5.96 us
    ppermute x1, starting transfers between devices, shards(): lax.ppermute(outgoing[0], 'gx', back(nx))  5.38 us
    pallas_call x1, Pallas kernels, shards(): pl.pallas_call(sides_kernel, in_specs=[vmem()] * 3, out_specs=anywhere(),...  4.1 us
  transfers between devices with their start and end apart: 10, of which 0 were waited for; matrix products, arithmetic and copies ran while one was open for 0% of the time, Pallas kernels for 37%

profile of v1, /device:TPU:25, one launch (start us, length us, event | category | flops | bytes accessed | tf_op | source)
XLA Modules:
  0.0 72.5 jit_solution(15794839416522317843)
XLA Ops:
  0.6 0.0 copy-start.2
  0.6 0.7 %copy-done.2 = f32[1,1,2,4096]{3,2,1,0:T(2,128)S(1)} copy-done((f32[1,1,2,4096]{3,2,1,0:T(2,128)S(1)}, f32[1,1,2,4096]{3,2,1,0:T(2,128)}, u32[]{:S(2)}) %copy-start.2) | copy-done | bytes 32792
  1.4 0.0 copy-start.4
  1.4 0.8 %copy-done.4 = f32[1,1,2,4096]{3,2,1,0:T(2,128)S(1)} copy-done((f32[1,1,2,4096]{3,2,1,0:T(2,128)S(1)}, f32[1,1,2,4096]{3,2,1,0:T(2,128)}, u32[]{:S(2)}) %copy-start.4) | copy-done | bytes 32792
  2.1 0.0 copy-start.10
  2.2 0.7 copy-done.10
  2.9 0.0 copy-start.12
  2.9 0.7 copy-done.12
  3.6 0.9 %outgoing.1 = (f32[40,128]{1,0:T(8,128)S(1)}, f32[40,128]{1,0:T(8,128)S(1)}, f32[40,128]{1,0:T(8,128)S(1)}, f32[40,128]{1,0:T(8,128)S(1)}) custom-call(f32[1,1,2,4096]{3,2,1,0:T(2,128)S(1)} %copy-done.2, f32[1,1,2,4096]{3,2,1,0:T(2,128)S(1)} %copy-done.4, f32[1,1,4096]{2,1,0:T(1,128)S(1)} %copy-done.12, s32[1,1,4,1024]{3,2,1,0:T(4,128)S(1)} %copy-done.10), custom_call_target="tpu_custom_call" | custom-call | flops 1000000000 | bytes 1 | tf_op jit(solution)/shard_map/outgoing/pallas_call | solution.py:452
  4.5 1.3 %collective-permute-start = (f32[40,128]{1,0:T(8,128)S(1)}, f32[40,128]{1,0:T(8,128)S(1)}, u32[]{:S(2)}, u32[]{:S(2)}) collective-permute-start(f32[40,128]{1,0:T(8,128)S(1)} %get-tuple-element.27), channel_id=1, source_target_pairs={{0,16},{16,32},{32,48},{48,64},{64,80},{80,96},{96,112},{112,128},... | collective-permute-start | bytes 61448 | tf_op jit(solution)/shard_map/ppermute | solution.py:467
  5.8 5.4 %collective-permute-start.1 = (f32[40,128]{1,0:T(8,128)S(1)}, f32[40,128]{1,0:T(8,128)S(1)}, u32[]{:S(2)}, u32[]{:S(2)}) collective-permute-start(f32[40,128]{1,0:T(8,128)S(1)} %get-tuple-element.28), channel_id=1, source_target_pairs={{16,0},{32,16},{48,32},{64,48},{80,64},{96,80},{112,96},{128,112},... | collective-permute-start | bytes 61448 | tf_op jit(solution)/shard_map/ppermute | solution.py:468
  11.2 2.9 %collective-permute-start.2 = (f32[40,128]{1,0:T(8,128)S(1)}, f32[40,128]{1,0:T(8,128)S(1)}, u32[]{:S(2)}, u32[]{:S(2)}) collective-permute-start(f32[40,128]{1,0:T(8,128)S(1)} %get-tuple-element.29), channel_id=1, source_target_pairs={{0,1},{1,2},{2,3},{3,4},{4,5},{5,6},{6,7},{7,8},{8,9},{9,10},{10,1... | collective-permute-start | bytes 61448 | tf_op jit(solution)/shard_map/ppermute | solution.py:469
  14.1 0.0 collective-permute-start.3
  14.1 0.0 copy-start.1
  14.1 0.9 %copy-done.1 = f32[1,1,16,4096]{3,2,1,0:T(8,128)S(1)} copy-done((f32[1,1,16,4096]{3,2,1,0:T(8,128)S(1)}, f32[1,1,16,4096]{3,2,1,0:T(8,128)}, u32[]{:S(2)}) %copy-start.1) | copy-done | bytes 262168
  15.1 0.0 copy-start.3
  15.1 0.8 %copy-done.3 = f32[1,1,2,4096]{3,2,1,0:T(2,128)S(1)} copy-done((f32[1,1,2,4096]{3,2,1,0:T(2,128)S(1)}, f32[1,1,2,4096]{3,2,1,0:T(2,128)}, u32[]{:S(2)}) %copy-start.3) | copy-done | bytes 32792
  15.8 0.8 %copy-done.5 = f32[1,1,2,4096]{3,2,1,0:T(2,128)S(1)} copy-done((f32[1,1,2,4096]{3,2,1,0:T(2,128)S(1)}, f32[1,1,2,4096]{3,2,1,0:T(2,128)}, u32[]{:S(2)}) %copy-start.5) | copy-done | bytes 32792
  16.6 0.8 %copy-done.6 = s32[1,1,8192]{2,1,0:T(1,128)S(1)} copy-done((s32[1,1,8192]{2,1,0:T(1,128)S(1)}, s32[1,1,8192]{2,1,0:T(1,128)}, u32[]{:S(2)}) %copy-start.6) | copy-done | bytes 32792
  17.3 0.8 %copy-done.8 = s32[1,1,8192]{2,1,0:T(1,128)S(1)} copy-done((s32[1,1,8192]{2,1,0:T(1,128)S(1)}, s32[1,1,8192]{2,1,0:T(1,128)}, u32[]{:S(2)}) %copy-start.8) | copy-done | bytes 32792
  18.1 0.7 copy-done.11
  18.8 9.7 %prepare.1 = (f32[5,64,128]{2,1,0:T(8,128)S(1)}, f32[5,64,128]{2,1,0:T(8,128)S(1)}, f32[16,4096]{1,0:T(8,128)S(1)}, s32[32,128]{1,0:T(8,128)S(1)}, s32[1,4096]{1...) custom-call(f32[1,1,2,4096]{3,2,1,0:T(2,128)S(1)} %copy-done.3, ...), custom_call_target="tpu_custom_call" | custom-call | flops 5000000000 | bytes 1 | tf_op jit(solution)/shard_map/prepare/pallas_call | solution.py:473
  29.2 0.0 collective-permute-done.ghost0
  29.2 0.0 collective-permute-done.1.ghost1
  29.2 0.0 collective-permute-done.2.ghost2
  29.2 0.0 collective-permute-done.3.ghost3
  29.2 0.0 copy-done.7
  29.2 0.0 copy-done.9
  29.2 0.0 copy-done.13
  29.3 0.0 copy-done.14
  29.3 6.8 %contact.1 = (f32[1,1,2,4096]{3,2,1,0:T(2,128)}, f32[16,4096]{1,0:T(8,128)S(1)}, f32[16,4096]{1,0:T(8,128)S(1)}, f32[16,16,256]{2,1,0:T(8,128)S(1)}, f32[16,16,2...) custom-call(s32[1,1]{1,0:T(1,128)S(6)} %copy.17.count, s32[16,128]{1,0:T(8,128)S(1)} %get-tuple-element.24.edges_s, ...), custom_call_target="tpu_custom_call" | custom-call | flops 5000000000 | bytes 1 | tf_op jit(solution)/shard_map/contact/pallas_call | solution.py:504
  36.0 0.0 collective-permute-start.6
  36.0 3.6 %collective-permute-start.7 = (f32[16,512]{1,0:T(8,128)S(1)}, f32[16,512]{1,0:T(8,128)S(1)}, u32[]{:S(2)}, u32[]{:S(2)}) collective-permute-start(f32[16,512]{1,0:T(8,128)S(1)} %get-tuple-element.44), channel_id=1, source_target_pairs={{16,0},{32,16},{48,32},{64,48},{80,64},{96,80},{112,96},{128,112},... | collective-permute-start | bytes 98312 | tf_op jit(solution)/shard_map/ppermute | solution.py:529
  39.6 6.7 %to_grid.1 = (f32[16,256,256]{2,1,0:T(8,128)}, f32[256,512]{1,0:T(8,128)S(1)}) custom-call(s32[16,128]{1,0:T(8,128)S(1)} %get-tuple-element.24.edges_s, f32[16,4096]{1,0:T(8,128)S(1)} %get-tuple-element.37.values_high, f32[16,4096]{1,0:T(8,128)S(1)} %get-tuple-element.38.values_low, s32[1,4096]{1,0:T(1,128)S(1)} %get-tuple-element.34.rows_in, ...), custom_call_target="tpu_custom_call" | custom-call | flops 100000000 | bytes 1 | tf_op jit(solution)/shard_map/to_grid/pallas_call | solution.py:533
  46.3 0.0 collective-permute-done.6
  46.4 0.0 collective-permute-done.7
  46.5 0.3 collective-permute-start.9
  46.8 6.0 %collective-permute-start.8 = (f32[288,256]{1,0:T(8,128)S(1)}, f32[288,256]{1,0:T(8,128)S(1)}, u32[]{:S(2)}, u32[]{:S(2)}) collective-permute-start(f32[288,256]{1,0:T(8,128)S(1)} %get-tuple-element.46), channel_id=1, source_target_pairs={{0,1},{1,2},{2,3},{3,4},{4,5},{5,6},{6,7},{7,8},{8,9},{9,10},{10,1... | collective-permute-start | bytes 884744 | tf_op jit(solution)/shard_map/ppermute | solution.py:542
  52.7 0.0 collective-permute-start.4
  52.7 3.6 %collective-permute-start.5 = (f32[16,16,256]{2,1,0:T(8,128)S(1)}, f32[16,16,256]{2,1,0:T(8,128)S(1)}, u32[]{:S(2)}, u32[]{:S(2)}) collective-permute-start(f32[16,16,256]{2,1,0:T(8,128)S(1)} %get-tuple-element.41), channel_id=1, source_target_pairs={{16,0},{32,16},{48,32},{64,48},{80,64},{96,80},{112,96},{128,112},... | collective-permute-start | bytes 786440 | tf_op jit(solution)/shard_map/ppermute | solution.py:531
  56.3 2.2 %copy-done = f32[16,256,256]{2,1,0:T(8,128)S(1)} copy-done((f32[16,256,256]{2,1,0:T(8,128)S(1)}, f32[16,256,256]{2,1,0:T(8,128)}, u32[]{:S(2)}) %copy-start) | copy-done | bytes 4194328
  58.5 6.6 %own_filter.1.own = f32[16,256,256]{2,1,0:T(8,128)S(1)} custom-call(f32[16,256,256]{2,1,0:T(8,128)S(1)} %copy-done), custom_call_target="tpu_custom_call" | custom-call | flops 100000000 | bytes 1 | tf_op jit(solution)/shard_map/own_filter/pallas_call | solution.py:545
  65.1 0.0 collective-permute-done.9.side_r
  65.1 0.0 collective-permute-done.8.side_l
  65.1 4.1 %add_sides.1.smoothed = f32[16,256,256]{2,1,0:T(8,128)} custom-call(f32[16,256,256]{2,1,0:T(8,128)S(1)} %own_filter.1.own, f32[288,256]{1,0:T(8,128)S(1)} %collective-permute-done.8.side_l, f32[288,256]{1,0:T(8,128)S(1)} %collective-permute-done.9.side_r), custom_call_target="tpu_custom_call" | custom-call | flops 100000000 | bytes 1 | tf_op jit(solution)/shard_map/add_sides/pallas_call | solution.py:555
  69.2 0.0 collective-permute-done.4.above
  69.2 0.0 collective-permute-done.5.below
  69.2 3.2 %add_ends.1 = f32[16,256,256]{2,1,0:T(8,128)} custom-call(f32[16,16,256]{2,1,0:T(8,128)S(1)} %collective-permute-done.4.above, f32[16,16,256]{2,1,0:T(8,128)S(1)} %collective-permute-done.5.below, f32[16,256,256]{2,1,0:T(8,128)} %add_sides.1.smoothed), custom_call_target="tpu_custom_call", output_to_operand_aliasing={{}: (2, {})} | custom-call | flops 1000000000 | bytes 1 | tf_op jit(solution)/shard_map/add_ends/pallas_call | solution.py:566
  (13 shorter events, 0.1 us)
Async XLA Ops:
  0.6 0.8 %copy-start.2 = (f32[1,1,2,4096]{3,2,1,0:T(2,128)S(1)}, f32[1,1,2,4096]{3,2,1,0:T(2,128)}, u32[]{:S(2)}) copy-start(f32[1,1,2,4096]{3,2,1,0:T(2,128)} %pos_h.3) | copy-start | bytes 98308
  1.4 0.8 %copy-start.4 = (f32[1,1,2,4096]{3,2,1,0:T(2,128)S(1)}, f32[1,1,2,4096]{3,2,1,0:T(2,128)}, u32[]{:S(2)}) copy-start(f32[1,1,2,4096]{3,2,1,0:T(2,128)} %vel_h.3) | copy-start | bytes 98308
  2.1 0.7 copy-start.10
  2.9 0.7 copy-start.12
  4.5 24.7 %collective-permute-start = (f32[40,128]{1,0:T(8,128)S(1)}, f32[40,128]{1,0:T(8,128)S(1)}, u32[]{:S(2)}, u32[]{:S(2)}) collective-permute-start(f32[40,128]{1,0:T(8,128)S(1)} %get-tuple-element.27), channel_id=1, source_target_pairs={{0,16},{16,32},{32,48},{48,64},{64,80},{80,96},{96,112},{112,128},... | collective-permute-start | bytes 61448 | tf_op jit(solution)/shard_map/ppermute | solution.py:467
  5.8 23.4 %collective-permute-start.1 = (f32[40,128]{1,0:T(8,128)S(1)}, f32[40,128]{1,0:T(8,128)S(1)}, u32[]{:S(2)}, u32[]{:S(2)}) collective-permute-start(f32[40,128]{1,0:T(8,128)S(1)} %get-tuple-element.28), channel_id=1, source_target_pairs={{16,0},{32,16},{48,32},{64,48},{80,64},{96,80},{112,96},{128,112},... | collective-permute-start | bytes 61448 | tf_op jit(solution)/shard_map/ppermute | solution.py:468
  11.2 18.0 %collective-permute-start.2 = (f32[40,128]{1,0:T(8,128)S(1)}, f32[40,128]{1,0:T(8,128)S(1)}, u32[]{:S(2)}, u32[]{:S(2)}) collective-permute-start(f32[40,128]{1,0:T(8,128)S(1)} %get-tuple-element.29), channel_id=1, source_target_pairs={{0,1},{1,2},{2,3},{3,4},{4,5},{5,6},{6,7},{7,8},{8,9},{9,10},{10,1... | collective-permute-start | bytes 61448 | tf_op jit(solution)/shard_map/ppermute | solution.py:469
  14.1 15.1 %collective-permute-start.3 = (f32[40,128]{1,0:T(8,128)S(1)}, f32[40,128]{1,0:T(8,128)S(1)}, u32[]{:S(2)}, u32[]{:S(2)}) collective-permute-start(f32[40,128]{1,0:T(8,128)S(1)} %get-tuple-element.30), channel_id=1, source_target_pairs={{1,0},{2,1},{3,2},{4,3},{5,4},{6,5},{7,6},{8,7},{9,8},{10,9},{11,1... | collective-permute-start | bytes 61448 | tf_op jit(solution)/shard_map/ppermute | solution.py:470
  14.1 1.0 %copy-start.1 = (f32[1,1,16,4096]{3,2,1,0:T(8,128)S(1)}, f32[1,1,16,4096]{3,2,1,0:T(8,128)}, u32[]{:S(2)}) copy-start(f32[1,1,16,4096]{3,2,1,0:T(8,128)} %tracers_h.1) | copy-start | bytes 786436
  15.1 0.8 %copy-start.3 = (f32[1,1,2,4096]{3,2,1,0:T(2,128)S(1)}, f32[1,1,2,4096]{3,2,1,0:T(2,128)}, u32[]{:S(2)}) copy-start(f32[1,1,2,4096]{3,2,1,0:T(2,128)} %pos_h.3) | copy-start | bytes 98308
  15.8 0.8 %copy-start.5 = (f32[1,1,2,4096]{3,2,1,0:T(2,128)S(1)}, f32[1,1,2,4096]{3,2,1,0:T(2,128)}, u32[]{:S(2)}) copy-start(f32[1,1,2,4096]{3,2,1,0:T(2,128)} %vel_h.3) | copy-start | bytes 98308
  16.6 0.8 %copy-start.6 = (s32[1,1,8192]{2,1,0:T(1,128)S(1)}, s32[1,1,8192]{2,1,0:T(1,128)}, u32[]{:S(2)}) copy-start(s32[1,1,8192]{2,1,0:T(1,128)} %param.16) | copy-start | bytes 98308
  17.3 0.8 %copy-start.8 = (s32[1,1,8192]{2,1,0:T(1,128)S(1)}, s32[1,1,8192]{2,1,0:T(1,128)}, u32[]{:S(2)}) copy-start(s32[1,1,8192]{2,1,0:T(1,128)} %param.17) | copy-start | bytes 98308
  18.1 0.7 copy-start.11
  18.8 10.4 %copy-start.7 = (s32[1,1,8192]{2,1,0:T(1,128)S(1)}, s32[1,1,8192]{2,1,0:T(1,128)}, u32[]{:S(2)}) copy-start(s32[1,1,8192]{2,1,0:T(1,128)} %param.16) | copy-start | bytes 98308
  18.8 10.4 %copy-start.9 = (s32[1,1,8192]{2,1,0:T(1,128)S(1)}, s32[1,1,8192]{2,1,0:T(1,128)}, u32[]{:S(2)}) copy-start(s32[1,1,8192]{2,1,0:T(1,128)} %param.17) | copy-start | bytes 98308
  18.8 10.4 %copy-start.13 = (f32[1,1,4096]{2,1,0:T(1,128)S(1)}, f32[1,1,4096]{2,1,0:T(1,128)}, u32[]{:S(2)}) copy-start(f32[1,1,4096]{2,1,0:T(1,128)} %rad_h.3) | copy-start | bytes 49156
  18.8 10.4 %copy-start.14 = (f32[1,1,4096]{2,1,0:T(1,128)S(1)}, f32[1,1,4096]{2,1,0:T(1,128)}, u32[]{:S(2)}) copy-start(f32[1,1,4096]{2,1,0:T(1,128)} %param.13) | copy-start | bytes 49156
  36.0 10.3 %collective-permute-start.6 = (f32[16,512]{1,0:T(8,128)S(1)}, f32[16,512]{1,0:T(8,128)S(1)}, u32[]{:S(2)}, u32[]{:S(2)}) collective-permute-start(f32[16,512]{1,0:T(8,128)S(1)} %get-tuple-element.42), channel_id=1, source_target_pairs={{0,16},{16,32},{32,48},{48,64},{64,80},{80,96},{96,112},{112,128},... | collective-permute-start | bytes 98312 | tf_op jit(solution)/shard_map/ppermute | solution.py:528
  36.0 10.3 %collective-permute-start.7 = (f32[16,512]{1,0:T(8,128)S(1)}, f32[16,512]{1,0:T(8,128)S(1)}, u32[]{:S(2)}, u32[]{:S(2)}) collective-permute-start(f32[16,512]{1,0:T(8,128)S(1)} %get-tuple-element.44), channel_id=1, source_target_pairs={{16,0},{32,16},{48,32},{64,48},{80,64},{96,80},{112,96},{128,112},... | collective-permute-start | bytes 98312 | tf_op jit(solution)/shard_map/ppermute | solution.py:529
  46.5 18.6 %collective-permute-start.9 = (f32[288,256]{1,0:T(8,128)S(1)}, f32[288,256]{1,0:T(8,128)S(1)}, u32[]{:S(2)}, u32[]{:S(2)}) collective-permute-start(f32[288,256]{1,0:T(8,128)S(1)} %get-tuple-element.45), channel_id=1, source_target_pairs={{1,0},{2,1},{3,2},{4,3},{5,4},{6,5},{7,6},{8,7},{9,8},{10,9},{11,1... | collective-permute-start | bytes 884744 | tf_op jit(solution)/shard_map/ppermute | solution.py:543
  46.8 18.3 %collective-permute-start.8 = (f32[288,256]{1,0:T(8,128)S(1)}, f32[288,256]{1,0:T(8,128)S(1)}, u32[]{:S(2)}, u32[]{:S(2)}) collective-permute-start(f32[288,256]{1,0:T(8,128)S(1)} %get-tuple-element.46), channel_id=1, source_target_pairs={{0,1},{1,2},{2,3},{3,4},{4,5},{5,6},{6,7},{7,8},{8,9},{9,10},{10,1... | collective-permute-start | bytes 884744 | tf_op jit(solution)/shard_map/ppermute | solution.py:542
  52.7 16.5 %collective-permute-start.4 = (f32[16,16,256]{2,1,0:T(8,128)S(1)}, f32[16,16,256]{2,1,0:T(8,128)S(1)}, u32[]{:S(2)}, u32[]{:S(2)}) collective-permute-start(f32[16,16,256]{2,1,0:T(8,128)S(1)} %get-tuple-element.40), channel_id=1, source_target_pairs={{0,16},{16,32},{32,48},{48,64},{64,80},{80,96},{96,112},{112,128},... | collective-permute-start | bytes 786440 | tf_op jit(solution)/shard_map/ppermute | solution.py:530
  52.7 16.5 %collective-permute-start.5 = (f32[16,16,256]{2,1,0:T(8,128)S(1)}, f32[16,16,256]{2,1,0:T(8,128)S(1)}, u32[]{:S(2)}, u32[]{:S(2)}) collective-permute-start(f32[16,16,256]{2,1,0:T(8,128)S(1)} %get-tuple-element.41), channel_id=1, source_target_pairs={{16,0},{32,16},{48,32},{64,48},{80,64},{96,80},{112,96},{128,112},... | collective-permute-start | bytes 786440 | tf_op jit(solution)/shard_map/ppermute | solution.py:531
  56.3 2.2 %copy-start = (f32[16,256,256]{2,1,0:T(8,128)S(1)}, f32[16,256,256]{2,1,0:T(8,128)}, u32[]{:S(2)}) copy-start(f32[16,256,256]{2,1,0:T(8,128)} %get-tuple-element.22.field) | copy-start | bytes 12582916

commit v2 on v1

--- a/solution.py
+++ b/solution.py
@@ -49,10 +49,18 @@
     return lax.dot_general(a, b, (((1,), (1,)), ((), ())), preferred_element_type=f32)
 
 
+def left3(x):
+    high, low = split2(x)
+    return jnp.concatenate([high, low, high], axis=1)
+
+
+def right3(x):
+    high, low = split2(x)
+    return jnp.concatenate([high, high, low], axis=0)
+
+
 def dot3(a, b):
-    ah, al = a
-    bh, bl = b
-    return dot_nn(ah, bh) + (dot_nn(ah, bl) + dot_nn(al, bh))
+    return dot_nn(left3(a), right3(b))
 
 
 def taps_at(offset):
@@ -107,10 +115,13 @@
             outs[k][8 * r : 8 * r + 8, :] = got[r]
 
 
+NEAR, FAR, SOURCE, UV, TRACERS, ROWS, COLS, PACKED = 0, 320, 640, 672, 736, 1248, 1280, 1312
+
+
 def prepare_kernel(
     pos_h, vel_h, rad_h, tracers_h, first_h, second_h, cells_h,
-    near, far, sorted_tracers, source, rows_out, cols_out, edges, uv,
-    weighted, hot, cell_rows, pos, vel, rad, tracers, first, second, cells, sem,
+    packed, edges,
+    weighted, hot, cell_rows, source, pos, vel, rad, tracers, first, second, cells, sem,
 ):
     fetch(
         (
@@ -122,18 +133,17 @@
     row_of = floe_line(pos, vel, rad)
 
     def gather_block(j, _):
-        at = row_block(8 * j, 8)
-        for index, dest in ((first, near), (second, far)):
-            got = lookup(row_of, 5, 32, index[at, :])
+        for index, dest in ((first, NEAR), (second, FAR)):
+            got = lookup(row_of, 5, 32, index[row_block(8 * j, 8), :])
             for r in range(5):
-                dest[r, at, :] = got[r]
+                packed[row_block(dest + 64 * r + 8 * j, 8), :] = got[r]
         return 0
 
-    lax.fori_loop(0, 8, gather_block, 0)
+    lax.fori_loop(0, 8, gather_block, 0, unroll=8)
     for h in range(32):
         at = slice(128 * h, 128 * h + 128)
         for r in range(2):
-            uv[r, h : h + 1, :] = vel[0, 0, r : r + 1, at]
+            packed[UV + 32 * r + h : UV + 32 * r + h + 1, :] = vel[0, 0, r : r + 1, at]
 
     cell = cells[...]
     bins = lax.shift_right_logical(cell, 12)
@@ -159,16 +169,16 @@
         weighted[32:64, at] = jnp.where(mine, iota((32, 128), 1).astype(f32), 0.0).astype(bf16)
         hot[:, at] = jnp.where((line & 127) == iota((128, 128), 0), 1.0, 0.0).astype(bf16)
     found = dot_nt(weighted[...], hot[...])
-    source[...] = (found[0:32] * 128.0 + found[32:64]).astype(i32)
+    found = found[0:32] * 128.0 + found[32:64]
+    source[...] = found.astype(i32)
+    packed[SOURCE : SOURCE + 32, :] = found
 
     cell_rows[...] = cell.astype(f32)
     for k in range(4):
         index = source[8 * k : 8 * k + 8, :]
         got = lookup(lambda r, h: cell_rows[h : h + 1, :], 1, 32, index)[0].astype(i32)
-        for s in range(8):
-            at = slice(1024 * k + 128 * s, 1024 * k + 128 * s + 128)
-            rows_out[:, at] = lax.shift_right_logical(got[s : s + 1, :], 8)
-            cols_out[:, at] = got[s : s + 1, :] & 255
+        packed[ROWS + 8 * k : ROWS + 8 * k + 8, :] = lax.shift_right_logical(got, 8).astype(f32)
+        packed[COLS + 8 * k : COLS + 8 * k + 8, :] = (got & 255).astype(f32)
 
     def tracer_block(q, _):
         index = jnp.broadcast_to(source[pl.ds(q, 1), :], (8, 128))
@@ -182,10 +192,10 @@
                 got = jnp.take_along_axis(block, low, axis=1, mode="promise_in_bounds")
                 parts[c] = jnp.where(here, got, parts[c])
         for c in range(2):
-            sorted_tracers[8 * c : 8 * c + 8, row_block(128 * q, 128)] = parts[c]
+            packed[row_block(TRACERS + 16 * q + 8 * c, 8), :] = parts[c]
         return 0
 
-    lax.fori_loop(0, 32, tracer_block, 0)
+    lax.fori_loop(0, 32, tracer_block, 0, unroll=8)
 
 
 def pack_sides(cells, out, count, second):
@@ -204,11 +214,15 @@
         out[:, second + 128 * g : second + 128 * g + 128] = tail
 
 
-def scatter_step(step, b, c, values_high, values_low, rows_in, cols_in):
+def lines_at(ref, base, c):
+    return jnp.concatenate([ref[pl.ds(base + 2 * c, 1), :], ref[pl.ds(base + 2 * c + 1, 1), :]], axis=1)
+
+
+def scatter_step(b, c, values_high, values_low, packed):
     at = row_block(256 * c, 256)
-    local = jnp.broadcast_to(rows_in[:, at], (16, 256)) - 16 * b
+    local = jnp.broadcast_to(lines_at(packed, ROWS, c).astype(i32) - 16 * b, (16, 256))
     here = local == iota((16, 256), 0)
-    columns = jnp.broadcast_to(cols_in[:, at], (256, 256))
+    columns = jnp.broadcast_to(lines_at(packed, COLS, c).astype(i32), (256, 256))
     hot = jnp.where(columns == iota((256, 256), 0), 1.0, 0.0).astype(bf16)
     high, low = [], []
     for ch in range(CH):
@@ -221,10 +235,9 @@
 
 def contact_kernel(
     count, edges_s,
-    near, far, first, second, ghost0, ghost1, ghost2, ghost3, rad, thick, uv,
-    sorted_tracers, source, rows_in, cols_in,
-    new_velocity, values_high, values_low, head_rows, tail_rows, head_ends, tail_ends,
-    weighted, hot, pressure_rows,
+    packed, first, second, ghost0, ghost1, ghost2, ghost3, rad, thick,
+    new_velocity, values_high, values_low, head_rows, tail_rows,
+    pressure_rows,
 ):
     ghosts = (ghost0, ghost1, ghost2, ghost3)
     shift = ((0, -1.0), (0, 1.0), (1, -1.0), (1, 1.0))
@@ -240,13 +253,14 @@
             line = jnp.where(jnp.full(line.shape, inside[k]), line, 0.0)
         return line + shift[k][1] if shift[k][0] == r else line
 
-    def pair_block(j, _):
+    def pair_block(j, total):
         at = row_block(8 * j, 8)
         index = second[at, :]
         outside = index >= F
         got = lookup(ghost_line, 5, 32, index - F)
-        other = [jnp.where(outside, got[r], far[r, at, :]) for r in range(5)]
-        own = [near[r, at, :] for r in range(5)]
+        far = [packed[row_block(FAR + 64 * r + 8 * j, 8), :] for r in range(5)]
+        other = [jnp.where(outside, got[r], far[r]) for r in range(5)]
+        own = [packed[row_block(NEAR + 64 * r + 8 * j, 8), :] for r in range(5)]
         gap_x = own[0] - other[0]
         gap_y = own[1] - other[1]
         spread = jnp.sqrt(gap_x * gap_x + gap_y * gap_y + core_sq)
@@ -266,63 +280,68 @@
         index = first[at, :]
         high = lax.shift_right_logical(index, 7)
         low = index & 127
+        spots, matches = [], []
         for s in range(8):
-            lanes = row_block(1024 * j + 128 * s, 128)
             mine = jnp.broadcast_to(high[s : s + 1, :], (32, 128)) == iota((32, 128), 0)
-            for t in range(6):
-                spot = jnp.where(mine, jnp.broadcast_to(halves[t][s : s + 1, :], (32, 128)), 0.0)
-                weighted[32 * t : 32 * t + 32, lanes] = spot.astype(bf16)
+            spot = [
+                jnp.where(mine, jnp.broadcast_to(h[s : s + 1, :], (32, 128)), 0.0).astype(bf16)
+                for h in halves
+            ]
+            spots.append(jnp.concatenate(spot, axis=0))
             match = jnp.broadcast_to(low[s : s + 1, :], (128, 128)) == iota((128, 128), 0)
-            hot[:, lanes] = jnp.where(match, 1.0, 0.0).astype(bf16)
-        return 0
-
-    lax.fori_loop(0, 8, pair_block, 0)
-    sums = dot_nt(weighted[...], hot[...])
+            matches.append(jnp.where(match, 1.0, 0.0).astype(bf16))
+        return total + dot_nt(jnp.concatenate(spots, axis=1), jnp.concatenate(matches, axis=1))
+
+    sums = lax.fori_loop(0, 8, pair_block, jnp.zeros((192, 128), f32), unroll=8)
     sums = [sums[32 * r : 32 * r + 32] + sums[96 + 32 * r : 128 + 32 * r] for r in range(3)]
     radius = rad[...]
     area = radius * radius
     for r in range(2):
-        moved = uv[r] + sums[r] / (area * thick[...])
+        moved = packed[UV + 32 * r : UV + 32 * r + 32, :] + sums[r] / (area * thick[...])
         for h in range(32):
             new_velocity[0, 0, r : r + 1, 128 * h : 128 * h + 128] = moved[h : h + 1, :]
     pressure_rows[...] = sums[2] / area
 
     def value_block(k, _):
-        index = source[row_block(8 * k, 8), :]
+        index = packed[row_block(SOURCE + 8 * k, 8), :].astype(i32)
         got = lookup(lambda r, h: pressure_rows[h : h + 1, :], 1, 32, index)[0]
         for s in range(8):
             at = row_block(1024 * k + 128 * s, 128)
-            value = sorted_tracers[:, at] * jnp.broadcast_to(got[s : s + 1, :], (16, 128))
+            tracer = packed[row_block(TRACERS + 128 * k + 16 * s, 16), :]
+            value = tracer * jnp.broadcast_to(got[s : s + 1, :], (16, 128))
             top = value.astype(bf16).astype(f32)
             values_high[:, at] = top
             values_low[:, at] = (value - top).astype(bf16).astype(f32)
         return 0
 
-    lax.fori_loop(0, 4, value_block, 0)
-
-    for b, out, ends in ((0, head_rows, head_ends), (15, tail_rows, tail_ends)):
-        begin = edges_s[b, 0]
-        end = edges_s[1, 0] if b == 0 else F
-        out[...] = jnp.zeros((CH, 16, CY), f32)
-
-        def add_chunk(c, _, b=b, out=out):
-            got = scatter_step(0, b, c, values_high, values_low, rows_in, cols_in)
-            out[...] = out[...] + got.reshape(CH, 16, CY)
-            return 0
-
-        lax.fori_loop(
-            lax.shift_right_logical(begin, 8), lax.shift_right_logical(end + 255, 8), add_chunk, 0
-        )
-        pack_sides(out, ends, 16, 256)
+    lax.fori_loop(0, 4, value_block, 0, unroll=4)
+
+    def both_ends(i):
+        ends = ((head_rows, 0, i), (tail_rows, 15, 15 - i))
+        return [(out, scatter_step(b, c, values_high, values_low, packed).reshape(CH, 16, CY)) for out, b, c in ends]
+
+    for (out, one), (_, two) in zip(both_ends(0), both_ends(1), strict=True):
+        out[...] = one + two
+
+    def add_chunk(i, _):
+        for out, got in both_ends(i):
+            out[...] = out[...] + got
+        return 0
+
+    chunks = jnp.maximum(
+        lax.shift_right_logical(edges_s[1, 0] + 255, 8), 16 - lax.shift_right_logical(edges_s[15, 0], 8)
+    )
+    lax.fori_loop(2, chunks, add_chunk, 0)
 
 
 def grid_kernel(
-    edges_s, values_high, values_low, rows_in, cols_in,
-    field, sides,
+    edges_s, values_high, values_low, packed,
+    field_h, along, sides,
+    field, left_x, sem,
 ):
     def step(i, carry):
         b, c, fresh = carry
-        got = scatter_step(i, b, c, values_high, values_low, rows_in, cols_in)
+        got = scatter_step(b, c, values_high, values_low, packed)
         at = row_block(16 * b, 16)
         was = jnp.where(jnp.full((CH, 16, CY), fresh, i32) == 1, 0.0, field[:, at, :])
         field[:, at, :] = was + got.reshape(CH, 16, CY)
@@ -337,42 +356,57 @@
     carry = (jnp.int32(0), jnp.int32(0), jnp.int32(1))
     for i in range(31):
         carry = step(i, carry)
-    pack_sides(field, sides, CX, 256)
-
-
-def own_filter_kernel(field, out, left_x, right_y):
-    high, low = split2(taps_at(iota((CX, CX), 1) - iota((CX, CX), 0)))
-    left_x[...] = jnp.concatenate([high, low, high], axis=1)
-    right_y[...] = jnp.concatenate([high, low, high], axis=0)
-
-    def two(k, _):
-        for c in range(2):
-            h, l = split2(field[2 * k + c])
-            along = dot_nn(left_x[...], jnp.concatenate([h, h, l], axis=0))
-            h, l = split2(along)
-            out[2 * k + c] = dot_nn(jnp.concatenate([h, h, l], axis=1), right_y[...])
+    keep = pltpu.make_async_copy(field, field_h, sem)
+    keep.start()
+    left_x[...] = left3(taps_at(iota((CX, CX), 1) - iota((CX, CX), 0)))
+
+    def some(k, _):
+        for c in range(4):
+            along[4 * k + c] = dot_nn(left_x[...], right3(field[4 * k + c]))
         return 0
 
-    lax.fori_loop(0, CH // 2, two, 0)
-
-
-def sides_kernel(own, side_l, side_r, out_h, work, sem):
+    lax.fori_loop(0, CH // 4, some, 0)
+    pack_sides(along, sides, CX, 256)
+    keep.wait()
+
+
+def blocks_of_16(reach):
+    same = (iota((256, 256), 0) >> 4) == (iota((256, 256), 1) >> 4)
+    delta = (iota((256, 256), 0) & 15) - (iota((256, 256), 1) & 15)
+    return jnp.where(same, taps_at(delta + reach), 0.0)
+
+
+def fix_kernel(along, above, below, sides, top, low, head_cols, tail_cols, ends):
+    for ref, reach, begin, out in ((above, -16, 0, top), (below, 16, CX - 16, low)):
+        more = dot3(blocks_of_16(reach).T, ref[...].reshape(256, CY)).reshape(CH, 16, CY)
+        out[...] = along[:, begin : begin + 16, :] + more
+        pack_sides(out, ends, 16, 256)
+        head_cols[begin : begin + 16, :] = ends[:, :256]
+        tail_cols[begin : begin + 16, :] = ends[:, 256:]
+    head_cols[16 : CX - 16, :] = sides[16 : CX - 16, :256]
+    tail_cols[16 : CX - 16, :] = sides[16 : CX - 16, 256:]
+
+
+def own_y_kernel(along, top, low, out, right_y):
+    right_y[...] = right3(taps_at(iota((CY, CY), 1) - iota((CY, CY), 0)))
+
+    def some(k, _):
+        for c in range(4):
+            ch = 4 * k + c
+            rows = jnp.concatenate([top[ch], along[ch, 16 : CX - 16, :], low[ch]], axis=0)
+            out[ch] = dot_nn(left3(rows), right_y[...])
+        return 0
+
+    lax.fori_loop(0, CH // 4, some, 0)
+
+
+def finish_kernel(own, side_l, side_r, out_h, work, sem):
     row = lax.axis_index("gy")
     ok_l, ok_r = row > 0, row < lax.axis_size("gy") - 1
-    band = split2(taps_at(iota((CX, CX), 1) - iota((CX, CX), 0)))
-    edge_up = split2(taps_at(iota((16, 16), 1) - 16 - iota((16, 16), 0)))
-    edge_down = split2(taps_at(iota((16, 16), 1) + 16 - iota((16, 16), 0)))
-    same = (iota((256, 256), 0) >> 4) == (iota((256, 256), 1) >> 4)
-    delta = (iota((256, 256), 0) & 15) - (iota((256, 256), 1) & 15)
     parts = []
     for ref, ok, reach in ((side_l, ok_l, -16), (side_r, ok_r, 16)):
-        rows = jnp.where(jnp.full((CX + 32, 256), ok), ref[...], 0.0)
-        mid = dot3(band, split2(rows[16 : CX + 16]))
-        top = mid[0:16] + dot3(edge_up, split2(rows[0:16]))
-        low = mid[240:256] + dot3(edge_down, split2(rows[CX + 16 :]))
-        along = jnp.concatenate([top, mid[16:240], low], axis=0)
-        weights = split2(jnp.where(same, taps_at(delta + reach), 0.0))
-        parts.append(dot3(split2(along), weights))
+        columns = jnp.where(jnp.full((CX, 256), ok), ref[...], 0.0)
+        parts.append(dot3(columns, blocks_of_16(reach)))
     lane = iota((CX, 128), 1)
     copies = []
     for ch in range(CH):
@@ -392,23 +426,16 @@
         copy.wait()
 
 
-def ends_kernel(above, below, smoothed, out):
-    g = pl.program_id(0)
-    rows = jnp.where(jnp.full((CH, 16, CY), g, i32) == 0, above[...], below[...]).reshape(256, CY)
-    band = split2(taps_at(iota((CY, CY), 1) - iota((CY, CY), 0)))
-    across = dot3(split2(rows), band)
-    same = (iota((256, 256), 0) >> 4) == (iota((256, 256), 1) >> 4)
-    delta = (iota((256, 256), 1) & 15) - (iota((256, 256), 0) & 15)
-    weights = split2(jnp.where(same, taps_at(delta + 32 * g - 16), 0.0))
-    out[...] = smoothed[...] + dot3(weights, split2(across)).reshape(CH, 16, CY)
-
-
 def vmem():
     return pl.BlockSpec(memory_space=pltpu.VMEM)
 
 
 def anywhere():
     return pl.BlockSpec(memory_space=pl.ANY)
+
+
+def hbm():
+    return pl.BlockSpec(memory_space=pltpu.HBM)
 
 
 def smem():
@@ -451,7 +478,7 @@
     ]
     outgoing = pl.pallas_call(
         outgoing_kernel,
-        in_specs=[anywhere()] * 4,
+        in_specs=[hbm()] * 4,
         out_shape=[struct(40, 128)] * 4,
         scratch_shapes=floe_scratch
         + [
@@ -459,7 +486,7 @@
             pltpu.VMEM((8, 128), i32),
             pltpu.SemaphoreType.DMA((4,)),
         ],
-        compiler_params=params(8),
+        compiler_params=params(60),
         cost_estimate=cost(1),
         name="outgoing",
     )(floe_position, floe_velocity, floe_radius, ghost_lists)
@@ -470,23 +497,15 @@
         lax.ppermute(outgoing[2], "gy", back(ny)),
     ]
 
-    near, far, sorted_tracers, source, rows, cols, edges, uv = pl.pallas_call(
+    packed, edges = pl.pallas_call(
         prepare_kernel,
-        in_specs=[anywhere()] * 7,
-        out_shape=[
-            struct(5, 64, 128),
-            struct(5, 64, 128),
-            struct(CH, F),
-            struct(32, 128, dtype=i32),
-            struct(1, F, dtype=i32),
-            struct(1, F, dtype=i32),
-            struct(16, 128, dtype=i32),
-            struct(2, 32, 128),
-        ],
+        in_specs=[hbm()] * 7,
+        out_shape=[struct(PACKED, 128), struct(16, 128, dtype=i32)],
         scratch_shapes=[
             pltpu.VMEM((64, F), bf16),
             pltpu.VMEM((128, F), bf16),
             pltpu.VMEM((32, 128), f32),
+            pltpu.VMEM((32, 128), i32),
         ]
         + floe_scratch
         + [
@@ -496,84 +515,79 @@
             pltpu.VMEM((32, 128), i32),
             pltpu.SemaphoreType.DMA((7,)),
         ],
-        compiler_params=params(16),
+        compiler_params=params(60),
         cost_estimate=cost(5),
         name="prepare",
     )(floe_position, floe_velocity, floe_radius, tracers, first, second, cells)
 
-    new_velocity, values_high, values_low, head_rows, tail_rows, head_ends, tail_ends = pl.pallas_call(
+    new_velocity, values_high, values_low, head_rows, tail_rows = pl.pallas_call(
         contact_kernel,
-        in_specs=[smem(), smem()] + [vmem()] * 15,
+        in_specs=[smem(), smem()] + [vmem()] * 9,
         out_shape=[
             struct(1, 1, 2, F),
             struct(CH, F),
             struct(CH, F),
             struct(CH, 16, CY),
             struct(CH, 16, CY),
-            struct(16, 512),
-            struct(16, 512),
         ],
-        scratch_shapes=[
-            pltpu.VMEM((192, NP), bf16),
-            pltpu.VMEM((128, NP), bf16),
-            pltpu.VMEM((32, 128), f32),
-        ],
+        scratch_shapes=[pltpu.VMEM((32, 128), f32)],
         compiler_params=params(20),
         cost_estimate=cost(5),
         name="contact",
     )(
-        pair_count, edges, near, far, first, second, *ghosts, radius, thickness, uv,
-        sorted_tracers, source, rows, cols,
+        pair_count, edges, packed, first, second, *ghosts, radius, thickness,
     )
-    ends_above = lax.ppermute(tail_ends, "gx", ring(nx))
-    ends_below = lax.ppermute(head_ends, "gx", back(nx))
     above = lax.ppermute(tail_rows, "gx", ring(nx))
     below = lax.ppermute(head_rows, "gx", back(nx))
 
-    field, sides = pl.pallas_call(
+    field, along, sides = pl.pallas_call(
         grid_kernel,
-        in_specs=[smem()] + [vmem()] * 4,
-        out_shape=[struct(CH, CX, CY), struct(CX, 512)],
-        compiler_params=params(16),
-        cost_estimate=cost(0.1),
+        in_specs=[smem()] + [vmem()] * 3,
+        out_specs=[anywhere(), vmem(), vmem()],
+        out_shape=[struct(CH, CX, CY), struct(CH, CX, CY), struct(CX, 512)],
+        scratch_shapes=[
+            pltpu.VMEM((CH, CX, CY), f32),
+            pltpu.VMEM((CX, 3 * CX), bf16),
+            pltpu.SemaphoreType.DMA,
+        ],
+        compiler_params=params(20),
+        cost_estimate=cost(10),
         name="to_grid",
-    )(edges, values_high, values_low, rows, cols)
-    sides = jnp.concatenate([ends_above, sides, ends_below], axis=0)
-    side_l = lax.ppermute(sides[:, 256:], "gy", ring(ny))
-    side_r = lax.ppermute(sides[:, :256], "gy", back(ny))
+    )(edges, values_high, values_low, packed)
+
+    top, low, head_cols, tail_cols = pl.pallas_call(
+        fix_kernel,
+        in_specs=[vmem()] * 4,
+        out_specs=[vmem()] * 4,
+        out_shape=[struct(CH, 16, CY)] * 2 + [struct(CX, 256)] * 2,
+        scratch_shapes=[pltpu.VMEM((16, 512), f32)],
+        compiler_params=params(12),
+        cost_estimate=cost(1),
+        name="fix_rows",
+    )(along, above, below, sides)
+    side_l = lax.ppermute(tail_cols, "gy", ring(ny))
+    side_r = lax.ppermute(head_cols, "gy", back(ny))
 
     own = pl.pallas_call(
-        own_filter_kernel,
-        in_specs=[vmem()],
+        own_y_kernel,
+        in_specs=[vmem()] * 3,
         out_specs=vmem(),
         out_shape=struct(CH, CX, CY),
-        scratch_shapes=[pltpu.VMEM((CX, 3 * CX), bf16), pltpu.VMEM((3 * CY, CY), bf16)],
+        scratch_shapes=[pltpu.VMEM((3 * CY, CY), bf16)],
         compiler_params=params(12),
-        cost_estimate=cost(0.1),
-        name="own_filter",
-    )(field)
+        cost_estimate=cost(4),
+        name="own_y",
+    )(along, top, low)
     smoothed = pl.pallas_call(
-        sides_kernel,
+        finish_kernel,
         in_specs=[vmem()] * 3,
         out_specs=anywhere(),
         out_shape=struct(CH, CX, CY),
         scratch_shapes=[pltpu.VMEM((CH, CX, CY), f32), pltpu.SemaphoreType.DMA((CH,))],
         compiler_params=params(14),
-        cost_estimate=cost(0.1),
-        name="add_sides",
+        cost_estimate=cost(1),
+        name="finish",
     )(own, side_l, side_r)
-    strip = pl.BlockSpec((CH, 16, CY), lambda g: (0, 15 * g, 0))
-    smoothed = pl.pallas_call(
-        ends_kernel,
-        grid=(2,),
-        in_specs=[pl.BlockSpec((CH, 16, CY), lambda g: (0, 0, 0))] * 2 + [strip],
-        out_specs=strip,
-        out_shape=struct(CH, CX, CY),
-        input_output_aliases={2: 0},
-        compiler_params=params(10),
-        cost_estimate=cost(1),
-        name="add_ends",
-    )(above, below, smoothed)
     return (new_velocity, field, smoothed)
 
 

time: 73.2 us -> 57.4 us (0.78)
  Pallas kernels: 38 us -> 27.6 us
  waiting for transfers between devices: 0.03 us -> 9.83 us
  local copies, waits for them, and re-layouts: 9.93 us -> 1.8 us
  starting transfers between devices: 23 us -> 16.3 us
    pallas_call x7, Pallas kernels: 38 us -> 27.6 us  [the longest x1 7.67 us: shards(): pl.pallas_call(prepare_kernel, in_specs=[hbm()] * 7, out_shape=[struct(PA...]
    unnamed x32 -> x12, local copies, waits for them, and re-layouts: 9.88 us -> 1.8 us
    ppermute x4 -> x2, waiting for transfers between devices: 0.01 us -> 6.9 us  [the longest x1 6.09 us: shards(): side_r = lax.ppermute(head_cols, 'gy', back(ny))]
    ppermute x4 -> x2, starting transfers between devices: 9.83 us -> 3.1 us  [the longest x1 3.1 us: shards(): side_l = lax.ppermute(tail_cols, 'gy', ring(ny))]
    ppermute x1, waiting for transfers between devices: 0.01 us -> 2.01 us  [shards(): below = lax.ppermute(head_rows, 'gx', back(nx))]
    ppermute x1, waiting for transfers between devices: 0.01 us -> 0.91 us  [shards(): above = lax.ppermute(tail_rows, 'gx', ring(nx))]
  transfers between devices with their start and end apart: 10 -> 8, of which waited for: 0 -> 4; matrix products, arithmetic and copies ran while one was open for 0% -> 0% of each run, Pallas kernels for 37% -> 31%
where the time goes in v2:
time: 57.4 us; the launch traced here: 57.1 us
  Pallas kernels  27.6 us (48%)
  starting transfers between devices  16.3 us (28%)
  waiting for transfers between devices  9.83 us (17%)
  local copies, waits for them, and re-layouts  1.8 us (3%)
  between operations  1.57 us (3%)
    pallas_call x1, Pallas kernels, shards(): pl.pallas_call(prepare_kernel, in_specs=[hbm()] * 7, out_shape=[struct(PA...  7.67 us
    pallas_call x1, Pallas kernels, shards(): pl.pallas_call(grid_kernel, in_specs=[smem()] + [vmem()] * 3, out_specs=[...  7.25 us
    ppermute x1, waiting for transfers between devices, shards(): side_r = lax.ppermute(head_cols, 'gy', back(ny))  6.09 us
    ppermute x1, starting transfers between devices, shards(): lax.ppermute(outgoing[0], 'gx', back(nx))  5.38 us
    pallas_call x1, Pallas kernels, shards(): pl.pallas_call(contact_kernel, in_specs=[smem(), smem()] + [vmem()] * 9,...  4.02 us
    ppermute x1, starting transfers between devices, shards(): below = lax.ppermute(head_rows, 'gx', back(nx))  3.57 us
    pallas_call x1, Pallas kernels, shards(): pl.pallas_call(finish_kernel, in_specs=[vmem()] * 3, out_specs=anywhere()...  3.19 us
    ppermute x1, starting transfers between devices, shards(): side_l = lax.ppermute(tail_cols, 'gy', ring(ny))  3.1 us
  transfers between devices with their start and end apart: 8, of which 4 were waited for; matrix products, arithmetic and copies ran while one was open for 0% of the time, Pallas kernels for 31%

profile of v2, /device:TPU:25, one launch (start us, length us, event | category | flops | bytes accessed | tf_op | source)
XLA Modules:
  0.0 57.1 jit_solution(5201604352065768148)
XLA Ops:
  0.6 2.2 %outgoing.1 = (f32[40,128]{1,0:T(8,128)}, f32[40,128]{1,0:T(8,128)}, f32[40,128]{1,0:T(8,128)}, f32[40,128]{1,0:T(8,128)}) custom-call(f32[1,1,2,4096]{3,2,1,0:T(2,128)} %pos_h.3, f32[1,1,2,4096]{3,2,1,0:T(2,128)} %vel_h.3, f32[1,1,4096]{2,1,0:T(1,128)} %rad_h.3, s32[1,1,4,1024]{3,2,1,0:T(4,128)} %lists_h.1), custom_call_target="tpu_custom_call" | custom-call | flops 1000000000 | bytes 1 | tf_op jit(solution)/shard_map/outgoing/pallas_call | solution.py:479
  2.8 1.3 %collective-permute-start = (f32[40,128]{1,0:T(8,128)}, f32[40,128]{1,0:T(8,128)S(1)}, u32[]{:S(2)}, u32[]{:S(2)}) collective-permute-start(f32[40,128]{1,0:T(8,128)} %get-tuple-element.23), channel_id=1, source_target_pairs={{0,16},{16,32},{32,48},{48,64},{64,80},{80,96},{96,112},{112,128},... | collective-permute-start | bytes 61448 | tf_op jit(solution)/shard_map/ppermute | solution.py:494
  4.1 5.4 %collective-permute-start.1 = (f32[40,128]{1,0:T(8,128)}, f32[40,128]{1,0:T(8,128)S(1)}, u32[]{:S(2)}, u32[]{:S(2)}) collective-permute-start(f32[40,128]{1,0:T(8,128)} %get-tuple-element.24), channel_id=1, source_target_pairs={{16,0},{32,16},{48,32},{64,48},{80,64},{96,80},{112,96},{128,112},... | collective-permute-start | bytes 61448 | tf_op jit(solution)/shard_map/ppermute | solution.py:495
  9.5 2.9 %collective-permute-start.2 = (f32[40,128]{1,0:T(8,128)}, f32[40,128]{1,0:T(8,128)S(1)}, u32[]{:S(2)}, u32[]{:S(2)}) collective-permute-start(f32[40,128]{1,0:T(8,128)} %get-tuple-element.25), channel_id=1, source_target_pairs={{0,1},{1,2},{2,3},{3,4},{4,5},{5,6},{6,7},{7,8},{8,9},{9,10},{10,1... | collective-permute-start | bytes 61448 | tf_op jit(solution)/shard_map/ppermute | solution.py:496
  12.4 0.0 collective-permute-start.3
  12.4 0.0 copy-start
  12.4 0.0 copy-start.1
  12.5 0.0 copy-start.2
  12.5 0.0 copy-start.3
  12.5 7.7 %prepare.1 = (f32[1312,128]{1,0:T(8,128)}, s32[16,128]{1,0:T(8,128)}) custom-call(f32[1,1,2,4096]{3,2,1,0:T(2,128)} %pos_h.3, f32[1,1,2,4096]{3,2,1,0:T(2,128)} %vel_h.3, f32[1,1,4096]{2,1,0:T(1,128)} %rad_h.3, f32[1,1,16,4096]{3,2,1,0:T(8,128)} %tracers_h.1, s32[64,128]{1,0:T(8,128)} %bitcast.5, s32[64,128]{1,0:T(8,128)} %bitcast.7, s32[32,128]{1,0:T(8,128)} %bitcast.11), custom_call_target="tpu_custom_call" | custom-call | flops 5000000000 | bytes 1 | tf_op jit(solution)/shard_map/prepare/pallas_call | solution.py:500
  20.8 0.0 collective-permute-done.ghost0
  20.8 0.0 collective-permute-done.1.ghost1
  20.8 0.0 collective-permute-done.2.ghost2
  20.8 0.0 collective-permute-done.3.ghost3
  20.8 0.0 copy-done
  20.8 0.0 copy-done.1
  20.9 0.0 copy-done.2
  20.9 0.0 copy-done.3
  20.9 0.0 copy-start.4
  20.9 1.1 %copy-done.4 = f32[1312,128]{1,0:T(8,128)S(1)} copy-done((f32[1312,128]{1,0:T(8,128)S(1)}, f32[1312,128]{1,0:T(8,128)}, u32[]{:S(2)}) %copy-start.4) | copy-done | bytes 671768
  22.0 0.0 copy-start.5
  22.0 0.7 %copy-done.5 = s32[16,128]{1,0:T(8,128)S(1)} copy-done((s32[16,128]{1,0:T(8,128)S(1)}, s32[16,128]{1,0:T(8,128)}, u32[]{:S(2)}) %copy-start.5) | copy-done | bytes 8216
  22.7 4.0 %contact.1 = (f32[1,1,2,4096]{3,2,1,0:T(2,128)}, f32[16,4096]{1,0:T(8,128)S(1)}, f32[16,4096]{1,0:T(8,128)S(1)}, f32[16,16,256]{2,1,0:T(8,128)S(1)}, f32[16,16,256]{2,1,0:T(8,128)S(1)}) custom-call(s32[1,1]{1,0:T(1,128)S(6)} %copy.13.count, s32[16,128]{1,0:T(8,128)S(1)} %copy-done.5, f32[1312,128]{1,0:T(8,128)S(1)} %copy-done.4, s32[64,128]{1,0:T(8,128)S(1)} %bitcast.6, ...), custom_call_target="tpu_custom_call" | custom-call | flops 5000000000 | bytes 1 | tf_op jit(solution)/shard_map/contact/pallas_call | solution.py:523
  26.7 0.0 collective-permute-start.4
  26.7 3.6 %collective-permute-start.5 = (f32[16,16,256]{2,1,0:T(8,128)S(1)}, f32[16,16,256]{2,1,0:T(8,128)S(1)}, u32[]{:S(2)}, u32[]{:S(2)}) collective-permute-start(f32[16,16,256]{2,1,0:T(8,128)S(1)} %get-tuple-element.33), channel_id=1, source_target_pairs={{16,0},{32,16},{48,32},{64,48},{80,64},{96,80},{112,96},{128,112},... | collective-permute-start | bytes 786440 | tf_op jit(solution)/shard_map/ppermute | solution.py:541
  30.3 7.3 %to_grid.1 = (f32[16,256,256]{2,1,0:T(8,128)}, f32[16,256,256]{2,1,0:T(8,128)S(1)}, f32[256,512]{1,0:T(8,128)S(1)}) custom-call(s32[16,128]{1,0:T(8,128)S(1)} %copy-done.5, f32[16,4096]{1,0:T(8,128)S(1)} %get-tuple-element.28.values_high, f32[16,4096]{1,0:T(8,128)S(1)} %get-tuple-element.29.values_low, f32[1312,128]{1,0:T(8,128)S(1)} %copy-done.4), custom_call_target="tpu_custom_call" | custom-call | flops 10000000000 | bytes 1 | tf_op jit(solution)/shard_map/to_grid/pallas_call | solution.py:543
  37.5 0.9 %collective-permute-done.4.above = f32[16,16,256]{2,1,0:T(8,128)S(1)} collective-permute-done((f32[16,16,256]{2,1,0:T(8,128)S(1)}, f32[16,16,256]{2,1,0:T(8,128)S(1)}, u32[]{:S(2)}, u32[]{:S(2)}) %collective-permute-start.4) | collective-permute-done | bytes 262176 | tf_op jit(solution)/shard_map/ppermute | solution.py:540
  38.4 2.0 %collective-permute-done.5.below = f32[16,16,256]{2,1,0:T(8,128)S(1)} collective-permute-done((f32[16,16,256]{2,1,0:T(8,128)S(1)}, f32[16,16,256]{2,1,0:T(8,128)S(1)}, u32[]{:S(2)}, u32[]{:S(2)}) %collective-permute-start.5) | collective-permute-done | bytes 262176 | tf_op jit(solution)/shard_map/ppermute | solution.py:541
  40.4 0.8 %fix_rows.1 = (f32[16,16,256]{2,1,0:T(8,128)S(1)}, f32[16,16,256]{2,1,0:T(8,128)S(1)}, f32[256,256]{1,0:T(8,128)S(1)}, f32[256,256]{1,0:T(8,128)S(1)}) custom-call(f32[16,256,256]{2,1,0:T(8,128)S(1)} %get-tuple-element.31.along, f32[16,16,256]{2,1,0:T(8,128)S(1)} %collective-permute-done.4.above, f32[16,16,256]{2,1,0:T(8,128)S(1)} %collective-permute-done.5.below, ...), custom_call_target="tpu_custom_call" | custom-call | flops 1000000000 | bytes 1 | tf_op jit(solution)/shard_map/fix_rows/pallas_call | solution.py:558
  41.2 3.1 %collective-permute-start.6 = (f32[256,256]{1,0:T(8,128)S(1)}, f32[256,256]{1,0:T(8,128)S(1)}, u32[]{:S(2)}, u32[]{:S(2)}) collective-permute-start(f32[256,256]{1,0:T(8,128)S(1)} %get-tuple-element.37), channel_id=1, source_target_pairs={{0,1},{1,2},{2,3},{3,4},{4,5},{5,6},{6,7},{7,8},{8,9},{9,10},{10,1... | collective-permute-start | bytes 786440 | tf_op jit(solution)/shard_map/ppermute | solution.py:568
  44.3 0.0 collective-permute-start.7
  44.3 2.5 %own_y.1.own = f32[16,256,256]{2,1,0:T(8,128)S(1)} custom-call(f32[16,256,256]{2,1,0:T(8,128)S(1)} %get-tuple-element.31.along, f32[16,16,256]{2,1,0:T(8,128)S(1)} %get-tuple-element.35.top, f32[16,16,256]{2,1,0:T(8,128)S(1)} %get-tuple-element.36.low), custom_call_target="tpu_custom_call" | custom-call | flops 4000000000 | bytes 1 | tf_op jit(solution)/shard_map/own_y/pallas_call | solution.py:571
  46.8 0.8 %collective-permute-done.6.side_l = f32[256,256]{1,0:T(8,128)S(1)} collective-permute-done((f32[256,256]{1,0:T(8,128)S(1)}, f32[256,256]{1,0:T(8,128)S(1)}, u32[]{:S(2)}, u32[]{:S(2)}) %collective-permute-start.6) | collective-permute-done | bytes 262176 | tf_op jit(solution)/shard_map/ppermute | solution.py:568
  47.6 6.1 %collective-permute-done.7.side_r = f32[256,256]{1,0:T(8,128)S(1)} collective-permute-done((f32[256,256]{1,0:T(8,128)S(1)}, f32[256,256]{1,0:T(8,128)S(1)}, u32[]{:S(2)}, u32[]{:S(2)}) %collective-permute-start.7) | collective-permute-done | bytes 262176 | tf_op jit(solution)/shard_map/ppermute | solution.py:569
  53.7 3.2 %finish.1 = f32[16,256,256]{2,1,0:T(8,128)} custom-call(f32[16,256,256]{2,1,0:T(8,128)S(1)} %own_y.1.own, f32[256,256]{1,0:T(8,128)S(1)} %collective-permute-done.6.side_l, f32[256,256]{1,0:T(8,128)S(1)} %collective-permute-done.7.side_r), custom_call_target="tpu_custom_call" | custom-call | flops 1000000000 | bytes 1 | tf_op jit(solution)/shard_map/finish/pallas_call | solution.py:581
Async XLA Ops:
  2.8 18.0 %collective-permute-start = (f32[40,128]{1,0:T(8,128)}, f32[40,128]{1,0:T(8,128)S(1)}, u32[]{:S(2)}, u32[]{:S(2)}) collective-permute-start(f32[40,128]{1,0:T(8,128)} %get-tuple-element.23), channel_id=1, source_target_pairs={{0,16},{16,32},{32,48},{48,64},{64,80},{80,96},{96,112},{112,128},... | collective-permute-start | bytes 61448 | tf_op jit(solution)/shard_map/ppermute | solution.py:494
  4.1 16.7 %collective-permute-start.1 = (f32[40,128]{1,0:T(8,128)}, f32[40,128]{1,0:T(8,128)S(1)}, u32[]{:S(2)}, u32[]{:S(2)}) collective-permute-start(f32[40,128]{1,0:T(8,128)} %get-tuple-element.24), channel_id=1, source_target_pairs={{16,0},{32,16},{48,32},{64,48},{80,64},{96,80},{112,96},{128,112},... | collective-permute-start | bytes 61448 | tf_op jit(solution)/shard_map/ppermute | solution.py:495
  9.5 11.3 %collective-permute-start.2 = (f32[40,128]{1,0:T(8,128)}, f32[40,128]{1,0:T(8,128)S(1)}, u32[]{:S(2)}, u32[]{:S(2)}) collective-permute-start(f32[40,128]{1,0:T(8,128)} %get-tuple-element.25), channel_id=1, source_target_pairs={{0,1},{1,2},{2,3},{3,4},{4,5},{5,6},{6,7},{7,8},{8,9},{9,10},{10,1... | collective-permute-start | bytes 61448 | tf_op jit(solution)/shard_map/ppermute | solution.py:496
  12.4 8.4 %collective-permute-start.3 = (f32[40,128]{1,0:T(8,128)}, f32[40,128]{1,0:T(8,128)S(1)}, u32[]{:S(2)}, u32[]{:S(2)}) collective-permute-start(f32[40,128]{1,0:T(8,128)} %get-tuple-element.26), channel_id=1, source_target_pairs={{1,0},{2,1},{3,2},{4,3},{5,4},{6,5},{7,6},{8,7},{9,8},{10,9},{11,1... | collective-permute-start | bytes 61448 | tf_op jit(solution)/shard_map/ppermute | solution.py:497
  12.4 8.4 %copy-start = (s32[1,1,8192]{2,1,0:T(1,128)S(1)}, s32[1,1,8192]{2,1,0:T(1,128)}, u32[]{:S(2)}) copy-start(s32[1,1,8192]{2,1,0:T(1,128)} %param.16) | copy-start | bytes 98308
  12.4 8.4 %copy-start.1 = (s32[1,1,8192]{2,1,0:T(1,128)S(1)}, s32[1,1,8192]{2,1,0:T(1,128)}, u32[]{:S(2)}) copy-start(s32[1,1,8192]{2,1,0:T(1,128)} %param.17) | copy-start | bytes 98308
  12.5 8.4 %copy-start.2 = (f32[1,1,4096]{2,1,0:T(1,128)S(1)}, f32[1,1,4096]{2,1,0:T(1,128)}, u32[]{:S(2)}) copy-start(f32[1,1,4096]{2,1,0:T(1,128)} %rad_h.3) | copy-start | bytes 49156
  12.5 8.4 %copy-start.3 = (f32[1,1,4096]{2,1,0:T(1,128)S(1)}, f32[1,1,4096]{2,1,0:T(1,128)}, u32[]{:S(2)}) copy-start(f32[1,1,4096]{2,1,0:T(1,128)} %param.13) | copy-start | bytes 49156
  20.9 1.1 %copy-start.4 = (f32[1312,128]{1,0:T(8,128)S(1)}, f32[1312,128]{1,0:T(8,128)}, u32[]{:S(2)}) copy-start(f32[1312,128]{1,0:T(8,128)} %get-tuple-element.22.packed) | copy-start | bytes 2015236
  22.0 0.7 %copy-start.5 = (s32[16,128]{1,0:T(8,128)S(1)}, s32[16,128]{1,0:T(8,128)}, u32[]{:S(2)}) copy-start(s32[16,128]{1,0:T(8,128)} %get-tuple-element.21.edges_s) | copy-start | bytes 24580
  26.7 11.7 %collective-permute-start.4 = (f32[16,16,256]{2,1,0:T(8,128)S(1)}, f32[16,16,256]{2,1,0:T(8,128)S(1)}, u32[]{:S(2)}, u32[]{:S(2)}) collective-permute-start(f32[16,16,256]{2,1,0:T(8,128)S(1)} %get-tuple-element.32), channel_id=1, source_target_pairs={{0,16},{16,32},{32,48},{48,64},{64,80},{80,96},{96,112},{112,128},... | collective-permute-start | bytes 786440 | tf_op jit(solution)/shard_map/ppermute | solution.py:540
  26.7 13.7 %collective-permute-start.5 = (f32[16,16,256]{2,1,0:T(8,128)S(1)}, f32[16,16,256]{2,1,0:T(8,128)S(1)}, u32[]{:S(2)}, u32[]{:S(2)}) collective-permute-start(f32[16,16,256]{2,1,0:T(8,128)S(1)} %get-tuple-element.33), channel_id=1, source_target_pairs={{16,0},{32,16},{48,32},{64,48},{80,64},{96,80},{112,96},{128,112},... | collective-permute-start | bytes 786440 | tf_op jit(solution)/shard_map/ppermute | solution.py:541
  41.2 6.4 %collective-permute-start.6 = (f32[256,256]{1,0:T(8,128)S(1)}, f32[256,256]{1,0:T(8,128)S(1)}, u32[]{:S(2)}, u32[]{:S(2)}) collective-permute-start(f32[256,256]{1,0:T(8,128)S(1)} %get-tuple-element.37), channel_id=1, source_target_pairs={{0,1},{1,2},{2,3},{3,4},{4,5},{5,6},{6,7},{7,8},{8,9},{9,10},{10,1... | collective-permute-start | bytes 786440 | tf_op jit(solution)/shard_map/ppermute | solution.py:568
  44.3 9.4 %collective-permute-start.7 = (f32[256,256]{1,0:T(8,128)S(1)}, f32[256,256]{1,0:T(8,128)S(1)}, u32[]{:S(2)}, u32[]{:S(2)}) collective-permute-start(f32[256,256]{1,0:T(8,128)S(1)} %get-tuple-element.38), channel_id=1, source_target_pairs={{1,0},{2,1},{3,2},{4,3},{5,4},{6,5},{7,6},{8,7},{9,8},{10,9},{11,1... | collective-permute-start | bytes 786440 | tf_op jit(solution)/shard_map/ppermute | solution.py:569

commit v3 on v2

--- a/solution.py
+++ b/solution.py
@@ -98,14 +98,36 @@
     copies = [pltpu.make_async_copy(a, b, sem.at[k]) for k, (a, b) in enumerate(pairs)]
     for copy in copies:
         copy.start()
-    for copy in copies:
+    for copy in copies[:-1]:
         copy.wait()
+    return copies[-1]
+
+
+def sorted_block(tracers, source):
+    index = jnp.broadcast_to(source, (8, 128))
+    high = lax.shift_right_logical(index, 7)
+    low = index & 127
+    parts = [jnp.zeros((8, 128), f32), jnp.zeros((8, 128), f32)]
+    for h in range(32):
+        here = high == h
+        for c in range(2):
+            block = tracers[0, 0, 8 * c : 8 * c + 8, 128 * h : 128 * h + 128]
+            got = jnp.take_along_axis(block, low, axis=1, mode="promise_in_bounds")
+            parts[c] = jnp.where(here, got, parts[c])
+    return jnp.concatenate(parts, axis=0)
+
+
+def store_values(values_high, values_low, at, tracer, pressure):
+    value = tracer * jnp.broadcast_to(pressure, (CH, 128))
+    top = value.astype(bf16).astype(f32)
+    values_high[:, at] = top
+    values_low[:, at] = (value - top).astype(bf16).astype(f32)
 
 
 def outgoing_kernel(pos_h, vel_h, rad_h, lists_h, *refs):
     outs = refs[:4]
     pos, vel, rad, lists, lines, sem = refs[4:]
-    fetch(((pos_h, pos), (vel_h, vel), (rad_h, rad), (lists_h, lists)), sem)
+    fetch(((pos_h, pos), (vel_h, vel), (rad_h, rad), (lists_h, lists)), sem).wait()
     row_of = floe_line(pos, vel, rad)
     for k in range(4):
         for s in range(8):
@@ -115,7 +137,8 @@
             outs[k][8 * r : 8 * r + 8, :] = got[r]
 
 
-NEAR, FAR, SOURCE, UV, TRACERS, ROWS, COLS, PACKED = 0, 320, 640, 672, 736, 1248, 1280, 1312
+NEAR, FAR, SOURCE, UV, TRACERS, ROWS, COLS, EDGES, PACKED = 0, 320, 640, 672, 736, 864, 896, 928, 944
+EARLY = (0, 1, 2, 3, 28, 29, 30, 31)
 
 
 def prepare_kernel(
@@ -123,10 +146,10 @@
     packed, edges,
     weighted, hot, cell_rows, source, pos, vel, rad, tracers, first, second, cells, sem,
 ):
-    fetch(
+    late = fetch(
         (
-            (pos_h, pos), (vel_h, vel), (rad_h, rad), (tracers_h, tracers),
-            (first_h, first), (second_h, second), (cells_h, cells),
+            (pos_h, pos), (vel_h, vel), (rad_h, rad), (first_h, first),
+            (second_h, second), (cells_h, cells), (tracers_h, tracers),
         ),
         sem,
     )
@@ -160,6 +183,7 @@
         at = slice(32 * b, 32 * b + 32)
         place = place + hots[b] * (ahead[at] + inside[at])
         edges[b : b + 1, :] = ahead[32 * b : 32 * b + 1].astype(i32)
+        packed[EDGES + b : EDGES + b + 1, :] = ahead[32 * b : 32 * b + 1]
     place = place.astype(i32)
     for q in range(32):
         at = slice(128 * q, 128 * q + 128)
@@ -180,22 +204,9 @@
         packed[ROWS + 8 * k : ROWS + 8 * k + 8, :] = lax.shift_right_logical(got, 8).astype(f32)
         packed[COLS + 8 * k : COLS + 8 * k + 8, :] = (got & 255).astype(f32)
 
-    def tracer_block(q, _):
-        index = jnp.broadcast_to(source[pl.ds(q, 1), :], (8, 128))
-        high = lax.shift_right_logical(index, 7)
-        low = index & 127
-        parts = [jnp.zeros((8, 128), f32), jnp.zeros((8, 128), f32)]
-        for h in range(32):
-            here = high == h
-            for c in range(2):
-                block = tracers[0, 0, 8 * c : 8 * c + 8, 128 * h : 128 * h + 128]
-                got = jnp.take_along_axis(block, low, axis=1, mode="promise_in_bounds")
-                parts[c] = jnp.where(here, got, parts[c])
-        for c in range(2):
-            packed[row_block(TRACERS + 16 * q + 8 * c, 8), :] = parts[c]
-        return 0
-
-    lax.fori_loop(0, 32, tracer_block, 0, unroll=8)
+    late.wait()
+    for t, q in enumerate(EARLY):
+        packed[TRACERS + 16 * t : TRACERS + 16 * t + 16, :] = sorted_block(tracers, source[q : q + 1, :])
 
 
 def pack_sides(cells, out, count, second):
@@ -234,14 +245,16 @@
 
 
 def contact_kernel(
-    count, edges_s,
-    packed, first, second, ghost0, ghost1, ghost2, ghost3, rad, thick,
-    new_velocity, values_high, values_low, head_rows, tail_rows,
+    count,
+    packed, first, second, ghost0, ghost1, ghost2, ghost3, rad, thick, tracers,
+    new_velocity, values_high, values_low, sorted_pressure, head_rows, tail_rows,
     pressure_rows,
 ):
     ghosts = (ghost0, ghost1, ghost2, ghost3)
     shift = ((0, -1.0), (0, 1.0), (1, -1.0), (1, 1.0))
     live_count = count[0, 0]
+    first_end = jnp.max(packed[EDGES + 1 : EDGES + 2, :]).astype(i32)
+    last_begin = jnp.max(packed[EDGES + 15 : EDGES + 16, :]).astype(i32)
 
     row = lax.axis_index("gy")
     inside = {2: row > 0, 3: row < lax.axis_size("gy") - 1}
@@ -302,19 +315,14 @@
             new_velocity[0, 0, r : r + 1, 128 * h : 128 * h + 128] = moved[h : h + 1, :]
     pressure_rows[...] = sums[2] / area
 
-    def value_block(k, _):
-        index = packed[row_block(SOURCE + 8 * k, 8), :].astype(i32)
+    for k in range(4):
+        index = packed[SOURCE + 8 * k : SOURCE + 8 * k + 8, :].astype(i32)
         got = lookup(lambda r, h: pressure_rows[h : h + 1, :], 1, 32, index)[0]
-        for s in range(8):
-            at = row_block(1024 * k + 128 * s, 128)
-            tracer = packed[row_block(TRACERS + 128 * k + 16 * s, 16), :]
-            value = tracer * jnp.broadcast_to(got[s : s + 1, :], (16, 128))
-            top = value.astype(bf16).astype(f32)
-            values_high[:, at] = top
-            values_low[:, at] = (value - top).astype(bf16).astype(f32)
-        return 0
-
-    lax.fori_loop(0, 4, value_block, 0, unroll=4)
+        sorted_pressure[8 * k : 8 * k + 8, :] = got
+    for t, q in enumerate(EARLY):
+        tracer = packed[TRACERS + 16 * t : TRACERS + 16 * t + 16, :]
+        at = slice(128 * q, 128 * q + 128)
+        store_values(values_high, values_low, at, tracer, sorted_pressure[q : q + 1, :])
 
     def both_ends(i):
         ends = ((head_rows, 0, i), (tail_rows, 15, 15 - i))
@@ -324,21 +332,35 @@
         out[...] = one + two
 
     def add_chunk(i, _):
+        for c in (i, 15 - i):
+            for q in (2 * c, 2 * c + 1):
+                tracer = sorted_block(tracers, packed[pl.ds(SOURCE + q, 1), :].astype(i32))
+                at = row_block(128 * q, 128)
+                store_values(values_high, values_low, at, tracer, sorted_pressure[pl.ds(q, 1), :])
         for out, got in both_ends(i):
             out[...] = out[...] + got
         return 0
 
     chunks = jnp.maximum(
-        lax.shift_right_logical(edges_s[1, 0] + 255, 8), 16 - lax.shift_right_logical(edges_s[15, 0], 8)
+        lax.shift_right_logical(first_end + 255, 8), 16 - lax.shift_right_logical(last_begin, 8)
     )
     lax.fori_loop(2, chunks, add_chunk, 0)
 
 
 def grid_kernel(
-    edges_s, values_high, values_low, packed,
+    edges_s, early_high, early_low, packed, tracers, sorted_pressure,
     field_h, along, sides,
-    field, left_x, sem,
+    field, left_x, values_high, values_low, sem,
 ):
+    for q in range(32):
+        at = slice(128 * q, 128 * q + 128)
+        if q in EARLY:
+            values_high[:, at] = early_high[:, at]
+            values_low[:, at] = early_low[:, at]
+        else:
+            tracer = sorted_block(tracers, packed[SOURCE + q : SOURCE + q + 1, :].astype(i32))
+            store_values(values_high, values_low, at, tracer, sorted_pressure[q : q + 1, :])
+
     def step(i, carry):
         b, c, fresh = carry
         got = scatter_step(b, c, values_high, values_low, packed)
@@ -520,13 +542,14 @@
         name="prepare",
     )(floe_position, floe_velocity, floe_radius, tracers, first, second, cells)
 
-    new_velocity, values_high, values_low, head_rows, tail_rows = pl.pallas_call(
+    new_velocity, values_high, values_low, sorted_pressure, head_rows, tail_rows = pl.pallas_call(
         contact_kernel,
-        in_specs=[smem(), smem()] + [vmem()] * 9,
+        in_specs=[smem()] + [vmem()] * 10,
         out_shape=[
             struct(1, 1, 2, F),
             struct(CH, F),
             struct(CH, F),
+            struct(32, 128),
             struct(CH, 16, CY),
             struct(CH, 16, CY),
         ],
@@ -535,25 +558,27 @@
         cost_estimate=cost(5),
         name="contact",
     )(
-        pair_count, edges, packed, first, second, *ghosts, radius, thickness,
+        pair_count, packed, first, second, *ghosts, radius, thickness, tracers,
     )
     above = lax.ppermute(tail_rows, "gx", ring(nx))
     below = lax.ppermute(head_rows, "gx", back(nx))
 
     field, along, sides = pl.pallas_call(
         grid_kernel,
-        in_specs=[smem()] + [vmem()] * 3,
+        in_specs=[smem()] + [vmem()] * 5,
         out_specs=[anywhere(), vmem(), vmem()],
         out_shape=[struct(CH, CX, CY), struct(CH, CX, CY), struct(CX, 512)],
         scratch_shapes=[
             pltpu.VMEM((CH, CX, CY), f32),
             pltpu.VMEM((CX, 3 * CX), bf16),
+            pltpu.VMEM((CH, F), f32),
+            pltpu.VMEM((CH, F), f32),
             pltpu.SemaphoreType.DMA,
         ],
         compiler_params=params(20),
         cost_estimate=cost(10),
         name="to_grid",
-    )(edges, values_high, values_low, packed)
+    )(edges, values_high, values_low, packed, tracers, sorted_pressure)
 
     top, low, head_cols, tail_cols = pl.pallas_call(
         fix_kernel,

time: 57.4 us -> 55.8 us (0.972)
  starting transfers between devices: 16.3 us -> 18.2 us
  waiting for transfers between devices: 9.83 us -> 7.97 us
  Pallas kernels: 27.6 us -> 26.7 us
  local copies, waits for them, and re-layouts: 1.8 us -> 1.05 us
    pallas_call x1, Pallas kernels: 7.67 us -> 5.51 us  [shards(): pl.pallas_call(prepare_kernel, in_specs=[hbm()] * 7, out_shape=[struct(PA...]
    ppermute x1, starting transfers between devices: 3.1 us -> 5.04 us  [shards(): side_l = lax.ppermute(tail_cols, 'gy', ring(ny))]
    ppermute x1, waiting for transfers between devices: 2.01 us -> 0.2 us  [shards(): below = lax.ppermute(head_rows, 'gx', back(nx))]
    pallas_call x2, Pallas kernels: 11.3 us -> 12.7 us  [the longest x1 9.29 us: shards(): pl.pallas_call(grid_kernel, in_specs=[smem()] + [vmem()] * 5, out_specs=[...]
    ppermute x1, waiting for transfers between devices: 0.91 us -> 0.01 us  [shards(): above = lax.ppermute(tail_rows, 'gx', ring(nx))]
    ppermute x1, waiting for transfers between devices: 0.01 us -> 0.8 us  [shards(): lax.ppermute(outgoing[2], 'gy', back(ny))]
    unnamed x12 -> x14, local copies, waits for them, and re-layouts: 1.8 us -> 1.05 us
where the time goes in v3:
time: 55.8 us; the launch traced here: 55.5 us
  Pallas kernels  26.7 us (48%)
  starting transfers between devices  18.2 us (33%)
  waiting for transfers between devices  7.97 us (14%)
  between operations  1.57 us (3%)
  local copies, waits for them, and re-layouts  1.05 us (2%)
    pallas_call x1, Pallas kernels, shards(): pl.pallas_call(grid_kernel, in_specs=[smem()] + [vmem()] * 5, out_specs=[...  9.29 us
    ppermute x1, waiting for transfers between devices, shards(): side_r = lax.ppermute(head_cols, 'gy', back(ny))  6.09 us
    pallas_call x1, Pallas kernels, shards(): pl.pallas_call(prepare_kernel, in_specs=[hbm()] * 7, out_shape=[struct(PA...  5.51 us
    ppermute x1, starting transfers between devices, shards(): lax.ppermute(outgoing[0], 'gx', back(nx))  5.38 us
    ppermute x1, starting transfers between devices, shards(): side_l = lax.ppermute(tail_cols, 'gy', ring(ny))  5.04 us
    ppermute x1, starting transfers between devices, shards(): below = lax.ppermute(head_rows, 'gx', back(nx))  3.57 us
    pallas_call x1, Pallas kernels, shards(): pl.pallas_call(contact_kernel, in_specs=[smem()] + [vmem()] * 10, out_sha...  3.37 us
    pallas_call x1, Pallas kernels, shards(): pl.pallas_call(finish_kernel, in_specs=[vmem()] * 3, out_specs=anywhere()...  3.16 us
  transfers between devices with their start and end apart: 8, of which 4 were waited for; matrix products, arithmetic and copies ran while one was open for 0% of the time, Pallas kernels for 31%

profile of v3, /device:TPU:25, one launch (start us, length us, event | category | flops | bytes accessed | tf_op | source)
XLA Modules:
  0.0 55.5 jit_solution(5016766058246811443)
XLA Ops:
  0.6 2.2 %outgoing.1 = (f32[40,128]{1,0:T(8,128)}, f32[40,128]{1,0:T(8,128)}, f32[40,128]{1,0:T(8,128)}, f32[40,128]{1,0:T(8,128)}) custom-call(f32[1,1,2,4096]{3,2,1,0:T(2,128)} %pos_h.3, f32[1,1,2,4096]{3,2,1,0:T(2,128)} %vel_h.3, f32[1,1,4096]{2,1,0:T(1,128)} %rad_h.3, s32[1,1,4,1024]{3,2,1,0:T(4,128)} %lists_h.1), custom_call_target="tpu_custom_call" | custom-call | flops 1000000000 | bytes 1 | tf_op jit(solution)/shard_map/outgoing/pallas_call | solution.py:501
  2.8 1.3 %collective-permute-start = (f32[40,128]{1,0:T(8,128)}, f32[40,128]{1,0:T(8,128)S(1)}, u32[]{:S(2)}, u32[]{:S(2)}) collective-permute-start(f32[40,128]{1,0:T(8,128)} %get-tuple-element.23), channel_id=1, source_target_pairs={{0,16},{16,32},{32,48},{48,64},{64,80},{80,96},{96,112},{112,128},... | collective-permute-start | bytes 61448 | tf_op jit(solution)/shard_map/ppermute | solution.py:516
  4.1 5.4 %collective-permute-start.1 = (f32[40,128]{1,0:T(8,128)}, f32[40,128]{1,0:T(8,128)S(1)}, u32[]{:S(2)}, u32[]{:S(2)}) collective-permute-start(f32[40,128]{1,0:T(8,128)} %get-tuple-element.24), channel_id=1, source_target_pairs={{16,0},{32,16},{48,32},{64,48},{80,64},{96,80},{112,96},{128,112},... | collective-permute-start | bytes 61448 | tf_op jit(solution)/shard_map/ppermute | solution.py:517
  9.5 2.9 %collective-permute-start.2 = (f32[40,128]{1,0:T(8,128)}, f32[40,128]{1,0:T(8,128)S(1)}, u32[]{:S(2)}, u32[]{:S(2)}) collective-permute-start(f32[40,128]{1,0:T(8,128)} %get-tuple-element.25), channel_id=1, source_target_pairs={{0,1},{1,2},{2,3},{3,4},{4,5},{5,6},{6,7},{7,8},{8,9},{9,10},{10,1... | collective-permute-start | bytes 61448 | tf_op jit(solution)/shard_map/ppermute | solution.py:518
  12.4 0.0 collective-permute-start.3
  12.4 0.0 copy-start
  12.4 0.0 copy-start.1
  12.4 0.0 copy-start.2
  12.5 0.0 copy-start.3
  12.5 0.0 copy-start.4
  12.5 5.5 %prepare.1 = (f32[944,128]{1,0:T(8,128)}, s32[16,128]{1,0:T(8,128)}) custom-call(f32[1,1,2,4096]{3,2,1,0:T(2,128)} %pos_h.3, f32[1,1,2,4096]{3,2,1,0:T(2,128)} %vel_h.3, f32[1,1,4096]{2,1,0:T(1,128)} %rad_h.3, f32[1,1,16,4096]{3,2,1,0:T(8,128)} %tracers.3, s32[64,128]{1,0:T(8,128)} %bitcast.5, s32[64,128]{1,0:T(8,128)} %bitcast.7, s32[32,128]{1,0:T(8,128)} %bitcast.11), custom_call_target="tpu_custom_call" | custom-call | flops 5000000000 | bytes 1 | tf_op jit(solution)/shard_map/prepare/pallas_call | solution.py:522
  18.6 0.0 collective-permute-done.ghost0
  18.7 0.0 collective-permute-done.1.ghost1
  18.7 0.0 collective-permute-done.2.ghost2
  18.7 0.8 %collective-permute-done.3.ghost3 = f32[40,128]{1,0:T(8,128)S(1)} collective-permute-done((f32[40,128]{1,0:T(8,128)}, f32[40,128]{1,0:T(8,128)S(1)}, u32[]{:S(2)}, u32[]{:S(2)}) %collective-permute-start.3) | collective-permute-done | bytes 20512 | tf_op jit(solution)/shard_map/ppermute | solution.py:519
  19.5 0.0 copy-done
  19.5 0.0 copy-done.1
  19.5 0.0 copy-done.2
  19.5 0.0 copy-done.3
  19.5 0.0 copy-done.4
  19.5 0.0 copy-start.5
  19.5 1.0 %copy-done.5 = f32[944,128]{1,0:T(8,128)S(1)} copy-done((f32[944,128]{1,0:T(8,128)S(1)}, f32[944,128]{1,0:T(8,128)}, u32[]{:S(2)}) %copy-start.5) | copy-done | bytes 483352
  20.5 0.0 copy-start.6
  20.5 3.4 %contact.1 = (f32[1,1,2,4096]{3,2,1,0:T(2,128)}, f32[16,4096]{1,0:T(8,128)S(1)}, f32[16,4096]{1,0:T(8,128)S(1)}, f32[32,128]{1,0:T(8,128)S(1)}, f32[16,16,256]{2,1,0:T(8,128)S(1)}, /*index=5*/f32[16,16,256]{2,1,0:T(8,128)S(1)}) custom-call(s32[1,1]{1,0:T(1,128)S(6)} %copy.13.count, f32[944,128]{1,0:T(8,128)S(1)} %copy-done.5, s32[64,128]{1,0:T(8,128)S(1)} %bitcast.6, ...), custom_call_target="tpu_custom_call" | custom-call | flops 5000000000 | bytes 1 | tf_op jit(solution)/shard_map/contact/pallas_call | solution.py:545
  23.9 0.0 collective-permute-start.4
  23.9 3.6 %collective-permute-start.5 = (f32[16,16,256]{2,1,0:T(8,128)S(1)}, f32[16,16,256]{2,1,0:T(8,128)S(1)}, u32[]{:S(2)}, u32[]{:S(2)}) collective-permute-start(f32[16,16,256]{2,1,0:T(8,128)S(1)} %get-tuple-element.35), channel_id=1, source_target_pairs={{16,0},{32,16},{48,32},{64,48},{80,64},{96,80},{112,96},{128,112},... | collective-permute-start | bytes 786440 | tf_op jit(solution)/shard_map/ppermute | solution.py:564
  27.5 0.0 copy-done.6
  27.5 9.3 %to_grid.1 = (f32[16,256,256]{2,1,0:T(8,128)}, f32[16,256,256]{2,1,0:T(8,128)S(1)}, f32[256,512]{1,0:T(8,128)S(1)}) custom-call(s32[16,128]{1,0:T(8,128)S(1)} %copy-done.6, f32[16,4096]{1,0:T(8,128)S(1)} %get-tuple-element.29.early_high, f32[16,4096]{1,0:T(8,128)S(1)} %get-tuple-element.30.early_low, f32[944,128]{1,0:T(8,128)S(1)} %copy-done.5, ...), custom_call_target="tpu_custom_call" | custom-call | flops 10000000000 | bytes 1 | tf_op jit(solution)/shard_map/to_grid/pallas_call | solution.py:566
  36.8 0.0 collective-permute-done.4.above
  36.8 0.2 collective-permute-done.5.below
  37.0 0.8 %fix_rows.1 = (f32[16,16,256]{2,1,0:T(8,128)S(1)}, f32[16,16,256]{2,1,0:T(8,128)S(1)}, f32[256,256]{1,0:T(8,128)S(1)}, f32[256,256]{1,0:T(8,128)S(1)}) custom-call(f32[16,256,256]{2,1,0:T(8,128)S(1)} %get-tuple-element.33.along, f32[16,16,256]{2,1,0:T(8,128)S(1)} %collective-permute-done.4.above, f32[16,16,256]{2,1,0:T(8,128)S(1)} %collective-permute-done.5.below, ...), custom_call_target="tpu_custom_call" | custom-call | flops 1000000000 | bytes 1 | tf_op jit(solution)/shard_map/fix_rows/pallas_call | solution.py:583
  37.8 5.0 %collective-permute-start.6 = (f32[256,256]{1,0:T(8,128)S(1)}, f32[256,256]{1,0:T(8,128)S(1)}, u32[]{:S(2)}, u32[]{:S(2)}) collective-permute-start(f32[256,256]{1,0:T(8,128)S(1)} %get-tuple-element.39), channel_id=1, source_target_pairs={{0,1},{1,2},{2,3},{3,4},{4,5},{5,6},{6,7},{7,8},{8,9},{9,10},{10,1... | collective-permute-start | bytes 786440 | tf_op jit(solution)/shard_map/ppermute | solution.py:593
  42.8 0.0 collective-permute-start.7
  42.8 2.4 %own_y.1.own = f32[16,256,256]{2,1,0:T(8,128)S(1)} custom-call(f32[16,256,256]{2,1,0:T(8,128)S(1)} %get-tuple-element.33.along, f32[16,16,256]{2,1,0:T(8,128)S(1)} %get-tuple-element.37.top, f32[16,16,256]{2,1,0:T(8,128)S(1)} %get-tuple-element.38.low), custom_call_target="tpu_custom_call" | custom-call | flops 4000000000 | bytes 1 | tf_op jit(solution)/shard_map/own_y/pallas_call | solution.py:596
  45.2 0.9 %collective-permute-done.6.side_l = f32[256,256]{1,0:T(8,128)S(1)} collective-permute-done((f32[256,256]{1,0:T(8,128)S(1)}, f32[256,256]{1,0:T(8,128)S(1)}, u32[]{:S(2)}, u32[]{:S(2)}) %collective-permute-start.6) | collective-permute-done | bytes 262176 | tf_op jit(solution)/shard_map/ppermute | solution.py:593
  46.1 6.1 %collective-permute-done.7.side_r = f32[256,256]{1,0:T(8,128)S(1)} collective-permute-done((f32[256,256]{1,0:T(8,128)S(1)}, f32[256,256]{1,0:T(8,128)S(1)}, u32[]{:S(2)}, u32[]{:S(2)}) %collective-permute-start.7) | collective-permute-done | bytes 262176 | tf_op jit(solution)/shard_map/ppermute | solution.py:594
  52.2 3.2 %finish.1 = f32[16,256,256]{2,1,0:T(8,128)} custom-call(f32[16,256,256]{2,1,0:T(8,128)S(1)} %own_y.1.own, f32[256,256]{1,0:T(8,128)S(1)} %collective-permute-done.6.side_l, f32[256,256]{1,0:T(8,128)S(1)} %collective-permute-done.7.side_r), custom_call_target="tpu_custom_call" | custom-call | flops 1000000000 | bytes 1 | tf_op jit(solution)/shard_map/finish/pallas_call | solution.py:606
Async XLA Ops:
  2.8 15.8 %collective-permute-start = (f32[40,128]{1,0:T(8,128)}, f32[40,128]{1,0:T(8,128)S(1)}, u32[]{:S(2)}, u32[]{:S(2)}) collective-permute-start(f32[40,128]{1,0:T(8,128)} %get-tuple-element.23), channel_id=1, source_target_pairs={{0,16},{16,32},{32,48},{48,64},{64,80},{80,96},{96,112},{112,128},... | collective-permute-start | bytes 61448 | tf_op jit(solution)/shard_map/ppermute | solution.py:516
  4.1 14.5 %collective-permute-start.1 = (f32[40,128]{1,0:T(8,128)}, f32[40,128]{1,0:T(8,128)S(1)}, u32[]{:S(2)}, u32[]{:S(2)}) collective-permute-start(f32[40,128]{1,0:T(8,128)} %get-tuple-element.24), channel_id=1, source_target_pairs={{16,0},{32,16},{48,32},{64,48},{80,64},{96,80},{112,96},{128,112},... | collective-permute-start | bytes 61448 | tf_op jit(solution)/shard_map/ppermute | solution.py:517
  9.5 9.2 %collective-permute-start.2 = (f32[40,128]{1,0:T(8,128)}, f32[40,128]{1,0:T(8,128)S(1)}, u32[]{:S(2)}, u32[]{:S(2)}) collective-permute-start(f32[40,128]{1,0:T(8,128)} %get-tuple-element.25), channel_id=1, source_target_pairs={{0,1},{1,2},{2,3},{3,4},{4,5},{5,6},{6,7},{7,8},{8,9},{9,10},{10,1... | collective-permute-start | bytes 61448 | tf_op jit(solution)/shard_map/ppermute | solution.py:518
  12.4 7.0 %collective-permute-start.3 = (f32[40,128]{1,0:T(8,128)}, f32[40,128]{1,0:T(8,128)S(1)}, u32[]{:S(2)}, u32[]{:S(2)}) collective-permute-start(f32[40,128]{1,0:T(8,128)} %get-tuple-element.26), channel_id=1, source_target_pairs={{1,0},{2,1},{3,2},{4,3},{5,4},{6,5},{7,6},{8,7},{9,8},{10,9},{11,1... | collective-permute-start | bytes 61448 | tf_op jit(solution)/shard_map/ppermute | solution.py:519
  12.4 7.0 %copy-start = (f32[1,1,16,4096]{3,2,1,0:T(8,128)S(1)}, f32[1,1,16,4096]{3,2,1,0:T(8,128)}, u32[]{:S(2)}) copy-start(f32[1,1,16,4096]{3,2,1,0:T(8,128)} %tracers.3) | copy-start | bytes 786436
  12.4 7.0 %copy-start.1 = (s32[1,1,8192]{2,1,0:T(1,128)S(1)}, s32[1,1,8192]{2,1,0:T(1,128)}, u32[]{:S(2)}) copy-start(s32[1,1,8192]{2,1,0:T(1,128)} %param.16) | copy-start | bytes 98308
  12.4 7.0 %copy-start.2 = (s32[1,1,8192]{2,1,0:T(1,128)S(1)}, s32[1,1,8192]{2,1,0:T(1,128)}, u32[]{:S(2)}) copy-start(s32[1,1,8192]{2,1,0:T(1,128)} %param.17) | copy-start | bytes 98308
  12.5 7.0 %copy-start.3 = (f32[1,1,4096]{2,1,0:T(1,128)S(1)}, f32[1,1,4096]{2,1,0:T(1,128)}, u32[]{:S(2)}) copy-start(f32[1,1,4096]{2,1,0:T(1,128)} %rad_h.3) | copy-start | bytes 49156
  12.5 7.0 %copy-start.4 = (f32[1,1,4096]{2,1,0:T(1,128)S(1)}, f32[1,1,4096]{2,1,0:T(1,128)}, u32[]{:S(2)}) copy-start(f32[1,1,4096]{2,1,0:T(1,128)} %param.13) | copy-start | bytes 49156
  19.5 1.0 %copy-start.5 = (f32[944,128]{1,0:T(8,128)S(1)}, f32[944,128]{1,0:T(8,128)}, u32[]{:S(2)}) copy-start(f32[944,128]{1,0:T(8,128)} %get-tuple-element.22.packed) | copy-start | bytes 1449988
  20.5 6.9 %copy-start.6 = (s32[16,128]{1,0:T(8,128)S(1)}, s32[16,128]{1,0:T(8,128)}, u32[]{:S(2)}) copy-start(s32[16,128]{1,0:T(8,128)} %get-tuple-element.28.edges_s) | copy-start | bytes 24580
  23.9 12.9 %collective-permute-start.4 = (f32[16,16,256]{2,1,0:T(8,128)S(1)}, f32[16,16,256]{2,1,0:T(8,128)S(1)}, u32[]{:S(2)}, u32[]{:S(2)}) collective-permute-start(f32[16,16,256]{2,1,0:T(8,128)S(1)} %get-tuple-element.34), channel_id=1, source_target_pairs={{0,16},{16,32},{32,48},{48,64},{64,80},{80,96},{96,112},{112,128},... | collective-permute-start | bytes 786440 | tf_op jit(solution)/shard_map/ppermute | solution.py:563
  23.9 13.1 %collective-permute-start.5 = (f32[16,16,256]{2,1,0:T(8,128)S(1)}, f32[16,16,256]{2,1,0:T(8,128)S(1)}, u32[]{:S(2)}, u32[]{:S(2)}) collective-permute-start(f32[16,16,256]{2,1,0:T(8,128)S(1)} %get-tuple-element.35), channel_id=1, source_target_pairs={{16,0},{32,16},{48,32},{64,48},{80,64},{96,80},{112,96},{128,112},... | collective-permute-start | bytes 786440 | tf_op jit(solution)/shard_map/ppermute | solution.py:564
  37.8 8.4 %collective-permute-start.6 = (f32[256,256]{1,0:T(8,128)S(1)}, f32[256,256]{1,0:T(8,128)S(1)}, u32[]{:S(2)}, u32[]{:S(2)}) collective-permute-start(f32[256,256]{1,0:T(8,128)S(1)} %get-tuple-element.39), channel_id=1, source_target_pairs={{0,1},{1,2},{2,3},{3,4},{4,5},{5,6},{6,7},{7,8},{8,9},{9,10},{10,1... | collective-permute-start | bytes 786440 | tf_op jit(solution)/shard_map/ppermute | solution.py:593
  42.8 9.4 %collective-permute-start.7 = (f32[256,256]{1,0:T(8,128)S(1)}, f32[256,256]{1,0:T(8,128)S(1)}, u32[]{:S(2)}, u32[]{:S(2)}) collective-permute-start(f32[256,256]{1,0:T(8,128)S(1)} %get-tuple-element.40), channel_id=1, source_target_pairs={{1,0},{2,1},{3,2},{4,3},{5,4},{6,5},{7,6},{8,7},{9,8},{10,9},{11,1... | collective-permute-start | bytes 786440 | tf_op jit(solution)/shard_map/ppermute | solution.py:594

commit v4 on v3

--- a/solution.py
+++ b/solution.py
@@ -209,7 +209,7 @@
         packed[TRACERS + 16 * t : TRACERS + 16 * t + 16, :] = sorted_block(tracers, source[q : q + 1, :])
 
 
-def pack_sides(cells, out, count, second):
+def pack_sides(cells, heads, tails, begin, count):
     lane = iota((count, 128), 1)
     for g in range(2):
         head = jnp.zeros((count, 128), f32)
@@ -221,8 +221,8 @@
             head = jnp.where(mine, pltpu.roll(left, 16 * k, 1) if k else left, head)
             turn = (16 * k + 16) % 128
             tail = jnp.where(mine, pltpu.roll(right, turn, 1) if turn else right, tail)
-        out[:, 128 * g : 128 * g + 128] = head
-        out[:, second + 128 * g : second + 128 * g + 128] = tail
+        heads[begin : begin + count, 128 * g : 128 * g + 128] = head
+        tails[begin : begin + count, 128 * g : 128 * g + 128] = tail
 
 
 def lines_at(ref, base, c):
@@ -349,8 +349,8 @@
 
 def grid_kernel(
     edges_s, early_high, early_low, packed, tracers, sorted_pressure,
-    field_h, along, sides,
-    field, left_x, values_high, values_low, sem,
+    field, head_cols, tail_cols,
+    values_high, values_low,
 ):
     for q in range(32):
         at = slice(128 * q, 128 * q + 128)
@@ -378,18 +378,7 @@
     carry = (jnp.int32(0), jnp.int32(0), jnp.int32(1))
     for i in range(31):
         carry = step(i, carry)
-    keep = pltpu.make_async_copy(field, field_h, sem)
-    keep.start()
-    left_x[...] = left3(taps_at(iota((CX, CX), 1) - iota((CX, CX), 0)))
-
-    def some(k, _):
-        for c in range(4):
-            along[4 * k + c] = dot_nn(left_x[...], right3(field[4 * k + c]))
-        return 0
-
-    lax.fori_loop(0, CH // 4, some, 0)
-    pack_sides(along, sides, CX, 256)
-    keep.wait()
+    pack_sides(field, head_cols, tail_cols, 0, CX)
 
 
 def blocks_of_16(reach):
@@ -398,37 +387,50 @@
     return jnp.where(same, taps_at(delta + reach), 0.0)
 
 
-def fix_kernel(along, above, below, sides, top, low, head_cols, tail_cols, ends):
-    for ref, reach, begin, out in ((above, -16, 0, top), (below, 16, CX - 16, low)):
-        more = dot3(blocks_of_16(reach).T, ref[...].reshape(256, CY)).reshape(CH, 16, CY)
-        out[...] = along[:, begin : begin + 16, :] + more
-        pack_sides(out, ends, 16, 256)
-        head_cols[begin : begin + 16, :] = ends[:, :256]
-        tail_cols[begin : begin + 16, :] = ends[:, 256:]
-    head_cols[16 : CX - 16, :] = sides[16 : CX - 16, :256]
-    tail_cols[16 : CX - 16, :] = sides[16 : CX - 16, 256:]
-
-
-def own_y_kernel(along, top, low, out, right_y):
-    right_y[...] = right3(taps_at(iota((CY, CY), 1) - iota((CY, CY), 0)))
+def corners_kernel(above, below, heads, tails):
+    pack_sides(above, heads, tails, 0, 16)
+    pack_sides(below, heads, tails, 16, 16)
+
+
+def own_kernel(field, above, below, after, out, field_h, left_x, right_y, more, sem):
+    keep = pltpu.make_async_copy(field, field_h, sem)
+    keep.start()
+    band = taps_at(iota((CX, CX), 1) - iota((CX, CX), 0))
+    left_x[...] = left3(band)
+    right_y[...] = right3(band)
+    for k, (ref, reach) in enumerate(((above, -16), (below, 16))):
+        got = dot3(blocks_of_16(reach).T, ref[...].reshape(256, CY))
+        more[k] = got.reshape(CH, 16, CY)
 
     def some(k, _):
         for c in range(4):
             ch = 4 * k + c
-            rows = jnp.concatenate([top[ch], along[ch, 16 : CX - 16, :], low[ch]], axis=0)
+            along = dot_nn(left_x[...], right3(field[ch]))
+            top = along[0:16] + more[0, ch]
+            low = along[CX - 16 :] + more[1, ch]
+            rows = jnp.concatenate([top, along[16 : CX - 16], low], axis=0)
             out[ch] = dot_nn(left3(rows), right_y[...])
         return 0
 
     lax.fori_loop(0, CH // 4, some, 0)
-
-
-def finish_kernel(own, side_l, side_r, out_h, work, sem):
+    keep.wait()
+
+
+def finish_kernel(own, side_l, side_r, corner_l, corner_r, out_h, work, sem):
     row = lax.axis_index("gy")
     ok_l, ok_r = row > 0, row < lax.axis_size("gy") - 1
+    band = left3(taps_at(iota((CX, CX), 1) - iota((CX, CX), 0)))
+    edge_up = taps_at(iota((16, 16), 1) - 16 - iota((16, 16), 0))
+    edge_down = taps_at(iota((16, 16), 1) + 16 - iota((16, 16), 0))
     parts = []
-    for ref, ok, reach in ((side_l, ok_l, -16), (side_r, ok_r, 16)):
+    for ref, corner, ok, reach in ((side_l, corner_l, ok_l, -16), (side_r, corner_r, ok_r, 16)):
         columns = jnp.where(jnp.full((CX, 256), ok), ref[...], 0.0)
-        parts.append(dot3(columns, blocks_of_16(reach)))
+        ends = jnp.where(jnp.full((32, 256), ok), corner[...], 0.0)
+        mid = dot_nn(band, right3(columns))
+        top = mid[0:16] + dot3(edge_up, ends[0:16])
+        low = mid[CX - 16 :] + dot3(edge_down, ends[16:32])
+        along = jnp.concatenate([top, mid[16 : CX - 16], low], axis=0)
+        parts.append(dot3(along, blocks_of_16(reach)))
     lane = iota((CX, 128), 1)
     copies = []
     for ch in range(CH):
@@ -563,56 +565,56 @@
     above = lax.ppermute(tail_rows, "gx", ring(nx))
     below = lax.ppermute(head_rows, "gx", back(nx))
 
-    field, along, sides = pl.pallas_call(
+    field, head_cols, tail_cols = pl.pallas_call(
         grid_kernel,
         in_specs=[smem()] + [vmem()] * 5,
-        out_specs=[anywhere(), vmem(), vmem()],
-        out_shape=[struct(CH, CX, CY), struct(CH, CX, CY), struct(CX, 512)],
+        out_specs=[vmem()] * 3,
+        out_shape=[struct(CH, CX, CY), struct(CX, 256), struct(CX, 256)],
+        scratch_shapes=[pltpu.VMEM((CH, F), f32), pltpu.VMEM((CH, F), f32)],
+        compiler_params=params(16),
+        cost_estimate=cost(8),
+        name="to_grid",
+    )(edges, values_high, values_low, packed, tracers, sorted_pressure)
+    side_l = lax.ppermute(tail_cols, "gy", ring(ny))
+    side_r = lax.ppermute(head_cols, "gy", back(ny))
+
+    corner_heads, corner_tails = pl.pallas_call(
+        corners_kernel,
+        in_specs=[vmem()] * 2,
+        out_specs=[vmem()] * 2,
+        out_shape=[struct(32, 256)] * 2,
+        compiler_params=params(4),
+        cost_estimate=cost(0.2),
+        name="corners",
+    )(above, below)
+    corner_l = lax.ppermute(corner_tails, "gy", ring(ny))
+    corner_r = lax.ppermute(corner_heads, "gy", back(ny))
+
+    own, field = pl.pallas_call(
+        own_kernel,
+        in_specs=[vmem()] * 4,
+        out_specs=[vmem(), hbm()],
+        out_shape=[struct(CH, CX, CY)] * 2,
         scratch_shapes=[
-            pltpu.VMEM((CH, CX, CY), f32),
             pltpu.VMEM((CX, 3 * CX), bf16),
-            pltpu.VMEM((CH, F), f32),
-            pltpu.VMEM((CH, F), f32),
+            pltpu.VMEM((3 * CY, CY), bf16),
+            pltpu.VMEM((2, CH, 16, CY), f32),
             pltpu.SemaphoreType.DMA,
         ],
-        compiler_params=params(20),
-        cost_estimate=cost(10),
-        name="to_grid",
-    )(edges, values_high, values_low, packed, tracers, sorted_pressure)
-
-    top, low, head_cols, tail_cols = pl.pallas_call(
-        fix_kernel,
-        in_specs=[vmem()] * 4,
-        out_specs=[vmem()] * 4,
-        out_shape=[struct(CH, 16, CY)] * 2 + [struct(CX, 256)] * 2,
-        scratch_shapes=[pltpu.VMEM((16, 512), f32)],
         compiler_params=params(12),
-        cost_estimate=cost(1),
-        name="fix_rows",
-    )(along, above, below, sides)
-    side_l = lax.ppermute(tail_cols, "gy", ring(ny))
-    side_r = lax.ppermute(head_cols, "gy", back(ny))
-
-    own = pl.pallas_call(
-        own_y_kernel,
-        in_specs=[vmem()] * 3,
-        out_specs=vmem(),
-        out_shape=struct(CH, CX, CY),
-        scratch_shapes=[pltpu.VMEM((3 * CY, CY), bf16)],
-        compiler_params=params(12),
-        cost_estimate=cost(4),
-        name="own_y",
-    )(along, top, low)
+        cost_estimate=cost(6),
+        name="own_filters",
+    )(field, above, below, corner_heads)
     smoothed = pl.pallas_call(
         finish_kernel,
-        in_specs=[vmem()] * 3,
+        in_specs=[vmem()] * 5,
         out_specs=anywhere(),
         out_shape=struct(CH, CX, CY),
         scratch_shapes=[pltpu.VMEM((CH, CX, CY), f32), pltpu.SemaphoreType.DMA((CH,))],
         compiler_params=params(14),
         cost_estimate=cost(1),
         name="finish",
-    )(own, side_l, side_r)
+    )(own, side_l, side_r, corner_l, corner_r)
     return (new_velocity, field, smoothed)
 
 

time: 55.8 us -> 57.1 us (1.023)
  the two profiles are of different devices: /device:TPU:25 before, /device:TPU:4 now
where the time goes in v4:
time: 57.1 us; the launch traced here: 56.9 us
  Pallas kernels  27.2 us (48%)
  starting transfers between devices  27 us (47%)
  between operations  1.62 us (3%)
  local copies, waits for them, and re-layouts  1.05 us (2%)
    pallas_call x1, Pallas kernels, shards(): pl.pallas_call(grid_kernel, in_specs=[smem()] + [vmem()] * 5, out_specs=[...  6.28 us
    pallas_call x1, Pallas kernels, shards(): pl.pallas_call(own_kernel, in_specs=[vmem()] * 4, out_specs=[vmem(), hbm(...  5.61 us
    pallas_call x1, Pallas kernels, shards(): pl.pallas_call(prepare_kernel, in_specs=[hbm()] * 7, out_shape=[struct(PA...  5.51 us
    ppermute x1, starting transfers between devices, shards(): lax.ppermute(outgoing[0], 'gx', back(nx))  5.38 us
    ppermute x1, starting transfers between devices, shards(): lax.ppermute(outgoing[2], 'gy', back(ny))  5.36 us
    ppermute x1, starting transfers between devices, shards(): side_r = lax.ppermute(head_cols, 'gy', back(ny))  5.35 us
    ppermute x1, starting transfers between devices, shards(): corner_r = lax.ppermute(corner_heads, 'gy', back(ny))  5.35 us
    ppermute x1, starting transfers between devices, shards(): below = lax.ppermute(head_rows, 'gx', back(nx))  4.13 us
  transfers between devices with their start and end apart: 10, of which 0 were waited for; matrix products, arithmetic and copies ran while one was open for 0% of the time, Pallas kernels for 31%

profile of v4, /device:TPU:4, one launch (start us, length us, event | category | flops | bytes accessed | tf_op | source)
XLA Modules:
  0.0 56.9 jit_solution(4784260856985623574)
XLA Ops:
  0.6 2.2 %outgoing.1 = (f32[40,128]{1,0:T(8,128)}, f32[40,128]{1,0:T(8,128)}, f32[40,128]{1,0:T(8,128)}, f32[40,128]{1,0:T(8,128)}) custom-call(f32[1,1,2,4096]{3,2,1,0:T(2,128)} %pos_h.3, f32[1,1,2,4096]{3,2,1,0:T(2,128)} %vel_h.3, f32[1,1,4096]{2,1,0:T(1,128)} %rad_h.3, s32[1,1,4,1024]{3,2,1,0:T(4,128)} %lists_h.1), custom_call_target="tpu_custom_call" | custom-call | flops 1000000000 | bytes 1 | tf_op jit(solution)/shard_map/outgoing/pallas_call | solution.py:503
  2.8 1.3 %collective-permute-start = (f32[40,128]{1,0:T(8,128)}, f32[40,128]{1,0:T(8,128)S(1)}, u32[]{:S(2)}, u32[]{:S(2)}) collective-permute-start(f32[40,128]{1,0:T(8,128)} %get-tuple-element.23), channel_id=1, source_target_pairs={{0,16},{16,32},{32,48},{48,64},{64,80},{80,96},{96,112},{112,128},... | collective-permute-start | bytes 61448 | tf_op jit(solution)/shard_map/ppermute | solution.py:518
  4.1 5.4 %collective-permute-start.1 = (f32[40,128]{1,0:T(8,128)}, f32[40,128]{1,0:T(8,128)S(1)}, u32[]{:S(2)}, u32[]{:S(2)}) collective-permute-start(f32[40,128]{1,0:T(8,128)} %get-tuple-element.24), channel_id=1, source_target_pairs={{16,0},{32,16},{48,32},{64,48},{80,64},{96,80},{112,96},{128,112},... | collective-permute-start | bytes 61448 | tf_op jit(solution)/shard_map/ppermute | solution.py:519
  9.5 0.0 collective-permute-start.2
  9.5 5.4 %collective-permute-start.3 = (f32[40,128]{1,0:T(8,128)}, f32[40,128]{1,0:T(8,128)S(1)}, u32[]{:S(2)}, u32[]{:S(2)}) collective-permute-start(f32[40,128]{1,0:T(8,128)} %get-tuple-element.26), channel_id=1, source_target_pairs={{1,0},{2,1},{3,2},{4,3},{5,4},{6,5},{7,6},{8,7},{9,8},{10,9},{11,1... | collective-permute-start | bytes 61448 | tf_op jit(solution)/shard_map/ppermute | solution.py:521
  14.8 0.0 copy-start
  14.8 0.0 copy-start.1
  14.8 0.0 copy-start.2
  14.8 0.0 copy-start.3
  14.8 0.0 copy-start.4
  14.9 5.5 %prepare.1 = (f32[944,128]{1,0:T(8,128)}, s32[16,128]{1,0:T(8,128)}) custom-call(f32[1,1,2,4096]{3,2,1,0:T(2,128)} %pos_h.3, f32[1,1,2,4096]{3,2,1,0:T(2,128)} %vel_h.3, f32[1,1,4096]{2,1,0:T(1,128)} %rad_h.3, f32[1,1,16,4096]{3,2,1,0:T(8,128)} %tracers.3, s32[64,128]{1,0:T(8,128)} %bitcast.5, s32[64,128]{1,0:T(8,128)} %bitcast.7, s32[32,128]{1,0:T(8,128)} %bitcast.11), custom_call_target="tpu_custom_call" | custom-call | flops 5000000000 | bytes 1 | tf_op jit(solution)/shard_map/prepare/pallas_call | solution.py:524
  21.0 0.0 collective-permute-done.ghost0
  21.0 0.0 collective-permute-done.1.ghost1
  21.1 0.0 collective-permute-done.2.ghost2
  21.1 0.0 collective-permute-done.3.ghost3
  21.1 0.0 copy-done
  21.1 0.0 copy-done.1
  21.1 0.0 copy-done.2
  21.1 0.0 copy-done.3
  21.1 0.0 copy-done.4
  21.1 0.0 copy-start.5
  21.1 1.0 %copy-done.5 = f32[944,128]{1,0:T(8,128)S(1)} copy-done((f32[944,128]{1,0:T(8,128)S(1)}, f32[944,128]{1,0:T(8,128)}, u32[]{:S(2)}) %copy-start.5) | copy-done | bytes 483352
  22.2 0.0 copy-start.6
  22.2 3.4 %contact.1 = (f32[1,1,2,4096]{3,2,1,0:T(2,128)}, f32[16,4096]{1,0:T(8,128)S(1)}, f32[16,4096]{1,0:T(8,128)S(1)}, f32[32,128]{1,0:T(8,128)S(1)}, f32[16,16,256]{2,1,0:T(8,128)S(1)}, /*index=5*/f32[16,16,256]{2,1,0:T(8,128)S(1)}) custom-call(s32[1,1]{1,0:T(1,128)S(6)} %copy.13.count, f32[944,128]{1,0:T(8,128)S(1)} %copy-done.5, s32[64,128]{1,0:T(8,128)S(1)} %bitcast.6, ...), custom_call_target="tpu_custom_call" | custom-call | flops 5000000000 | bytes 1 | tf_op jit(solution)/shard_map/contact/pallas_call | solution.py:547
  25.5 0.0 collective-permute-start.4
  25.5 4.1 %collective-permute-start.5 = (f32[16,16,256]{2,1,0:T(8,128)S(1)}, f32[16,16,256]{2,1,0:T(8,128)S(1)}, u32[]{:S(2)}, u32[]{:S(2)}) collective-permute-start(f32[16,16,256]{2,1,0:T(8,128)S(1)} %get-tuple-element.34), channel_id=1, source_target_pairs={{16,0},{32,16},{48,32},{64,48},{80,64},{96,80},{112,96},{128,112},... | collective-permute-start | bytes 786440 | tf_op jit(solution)/shard_map/ppermute | solution.py:566
  29.7 0.0 copy-done.6
  29.7 6.3 %to_grid.1 = (f32[16,256,256]{2,1,0:T(8,128)S(1)}, f32[256,256]{1,0:T(8,128)S(1)}, f32[256,256]{1,0:T(8,128)S(1)}) custom-call(s32[16,128]{1,0:T(8,128)S(1)} %copy-done.6, f32[16,4096]{1,0:T(8,128)S(1)} %get-tuple-element.29.early_high, f32[16,4096]{1,0:T(8,128)S(1)} %get-tuple-element.30.early_low, f32[944,128]{1,0:T(8,128)S(1)} %copy-done.5, ...), custom_call_target="tpu_custom_call" | custom-call | flops 8000000000 | bytes 1 | tf_op jit(solution)/shard_map/to_grid/pallas_call | solution.py:568
  36.0 0.1 collective-permute-start.6
  36.0 5.3 %collective-permute-start.7 = (f32[256,256]{1,0:T(8,128)S(1)}, f32[256,256]{1,0:T(8,128)S(1)}, u32[]{:S(2)}, u32[]{:S(2)}) collective-permute-start(f32[256,256]{1,0:T(8,128)S(1)} %get-tuple-element.39), channel_id=1, source_target_pairs={{1,0},{2,1},{3,2},{4,3},{5,4},{6,5},{7,6},{8,7},{9,8},{10,9},{11,1... | collective-permute-start | bytes 786440 | tf_op jit(solution)/shard_map/ppermute | solution.py:579
  41.4 0.0 collective-permute-done.4.above
  41.4 0.0 collective-permute-done.5.below
  41.4 0.2 corners.1
  41.6 0.1 collective-permute-start.8
  41.7 5.3 %collective-permute-start.9 = (f32[32,256]{1,0:T(8,128)S(1)}, f32[32,256]{1,0:T(8,128)S(1)}, u32[]{:S(2)}, u32[]{:S(2)}) collective-permute-start(f32[32,256]{1,0:T(8,128)S(1)} %get-tuple-element.35.after), channel_id=1, source_target_pairs={{1,0},{2,1},{3,2},{4,3},{5,4},{6,5},{7,6},{8,7},{9,8},{10,9},{11,1... | collective-permute-start | bytes 98312 | tf_op jit(solution)/shard_map/ppermute | solution.py:591
  47.0 5.6 %own_filters.1 = (f32[16,256,256]{2,1,0:T(8,128)S(1)}, f32[16,256,256]{2,1,0:T(8,128)}) custom-call(f32[16,256,256]{2,1,0:T(8,128)S(1)} %get-tuple-element.32.field, f32[16,16,256]{2,1,0:T(8,128)S(1)} %collective-permute-done.4.above, f32[16,16,256]{2,1,0:T(8,128)S(1)} %collective-permute-done.5.below, f32[32,256]{1,0:T(8,128)S(1)} %get-tuple-element.35.after), custom_call_target="tpu_custom_call" | custom-call | flops 6000000000 | bytes 1 | tf_op jit(solution)/shard_map/own_filters/pallas_call | solution.py:593
  52.6 0.0 collective-permute-done.6.side_l
  52.6 0.0 collective-permute-done.7.side_r
  52.7 0.0 collective-permute-done.8.corner_l
  52.7 0.0 collective-permute-done.9.corner_r
  52.7 4.0 %finish.1 = f32[16,256,256]{2,1,0:T(8,128)} custom-call(f32[16,256,256]{2,1,0:T(8,128)S(1)} %get-tuple-element.37.own, f32[256,256]{1,0:T(8,128)S(1)} %collective-permute-done.6.side_l, f32[256,256]{1,0:T(8,128)S(1)} %collective-permute-done.7.side_r, f32[32,256]{1,0:T(8,128)S(1)} %collective-permute-done.8.corner_l, ...), custom_call_target="tpu_custom_call" | custom-call | flops 1000000000 | bytes 1 | tf_op jit(solution)/shard_map/finish/pallas_call | solution.py:608
Async XLA Ops:
  2.8 18.2 %collective-permute-start = (f32[40,128]{1,0:T(8,128)}, f32[40,128]{1,0:T(8,128)S(1)}, u32[]{:S(2)}, u32[]{:S(2)}) collective-permute-start(f32[40,128]{1,0:T(8,128)} %get-tuple-element.23), channel_id=1, source_target_pairs={{0,16},{16,32},{32,48},{48,64},{64,80},{80,96},{96,112},{112,128},... | collective-permute-start | bytes 61448 | tf_op jit(solution)/shard_map/ppermute | solution.py:518
  4.1 16.9 %collective-permute-start.1 = (f32[40,128]{1,0:T(8,128)}, f32[40,128]{1,0:T(8,128)S(1)}, u32[]{:S(2)}, u32[]{:S(2)}) collective-permute-start(f32[40,128]{1,0:T(8,128)} %get-tuple-element.24), channel_id=1, source_target_pairs={{16,0},{32,16},{48,32},{64,48},{80,64},{96,80},{112,96},{128,112},... | collective-permute-start | bytes 61448 | tf_op jit(solution)/shard_map/ppermute | solution.py:519
  9.5 11.6 %collective-permute-start.2 = (f32[40,128]{1,0:T(8,128)}, f32[40,128]{1,0:T(8,128)S(1)}, u32[]{:S(2)}, u32[]{:S(2)}) collective-permute-start(f32[40,128]{1,0:T(8,128)} %get-tuple-element.25), channel_id=1, source_target_pairs={{0,1},{1,2},{2,3},{3,4},{4,5},{5,6},{6,7},{7,8},{8,9},{9,10},{10,1... | collective-permute-start | bytes 61448 | tf_op jit(solution)/shard_map/ppermute | solution.py:520
  9.5 11.6 %collective-permute-start.3 = (f32[40,128]{1,0:T(8,128)}, f32[40,128]{1,0:T(8,128)S(1)}, u32[]{:S(2)}, u32[]{:S(2)}) collective-permute-start(f32[40,128]{1,0:T(8,128)} %get-tuple-element.26), channel_id=1, source_target_pairs={{1,0},{2,1},{3,2},{4,3},{5,4},{6,5},{7,6},{8,7},{9,8},{10,9},{11,1... | collective-permute-start | bytes 61448 | tf_op jit(solution)/shard_map/ppermute | solution.py:521
  14.8 6.2 %copy-start = (f32[1,1,16,4096]{3,2,1,0:T(8,128)S(1)}, f32[1,1,16,4096]{3,2,1,0:T(8,128)}, u32[]{:S(2)}) copy-start(f32[1,1,16,4096]{3,2,1,0:T(8,128)} %tracers.3) | copy-start | bytes 786436
  14.8 6.2 %copy-start.1 = (s32[1,1,8192]{2,1,0:T(1,128)S(1)}, s32[1,1,8192]{2,1,0:T(1,128)}, u32[]{:S(2)}) copy-start(s32[1,1,8192]{2,1,0:T(1,128)} %param.16) | copy-start | bytes 98308
  14.8 6.3 %copy-start.2 = (s32[1,1,8192]{2,1,0:T(1,128)S(1)}, s32[1,1,8192]{2,1,0:T(1,128)}, u32[]{:S(2)}) copy-start(s32[1,1,8192]{2,1,0:T(1,128)} %param.17) | copy-start | bytes 98308
  14.8 6.3 %copy-start.3 = (f32[1,1,4096]{2,1,0:T(1,128)S(1)}, f32[1,1,4096]{2,1,0:T(1,128)}, u32[]{:S(2)}) copy-start(f32[1,1,4096]{2,1,0:T(1,128)} %rad_h.3) | copy-start | bytes 49156
  14.8 6.3 %copy-start.4 = (f32[1,1,4096]{2,1,0:T(1,128)S(1)}, f32[1,1,4096]{2,1,0:T(1,128)}, u32[]{:S(2)}) copy-start(f32[1,1,4096]{2,1,0:T(1,128)} %param.13) | copy-start | bytes 49156
  21.1 1.0 %copy-start.5 = (f32[944,128]{1,0:T(8,128)S(1)}, f32[944,128]{1,0:T(8,128)}, u32[]{:S(2)}) copy-start(f32[944,128]{1,0:T(8,128)} %get-tuple-element.22.packed) | copy-start | bytes 1449988
  22.2 7.5 %copy-start.6 = (s32[16,128]{1,0:T(8,128)S(1)}, s32[16,128]{1,0:T(8,128)}, u32[]{:S(2)}) copy-start(s32[16,128]{1,0:T(8,128)} %get-tuple-element.28.edges_s) | copy-start | bytes 24580
  25.5 15.9 %collective-permute-start.4 = (f32[16,16,256]{2,1,0:T(8,128)S(1)}, f32[16,16,256]{2,1,0:T(8,128)S(1)}, u32[]{:S(2)}, u32[]{:S(2)}) collective-permute-start(f32[16,16,256]{2,1,0:T(8,128)S(1)} %get-tuple-element.33), channel_id=1, source_target_pairs={{0,16},{16,32},{32,48},{48,64},{64,80},{80,96},{96,112},{112,128},... | collective-permute-start | bytes 786440 | tf_op jit(solution)/shard_map/ppermute | solution.py:565
  25.5 15.9 %collective-permute-start.5 = (f32[16,16,256]{2,1,0:T(8,128)S(1)}, f32[16,16,256]{2,1,0:T(8,128)S(1)}, u32[]{:S(2)}, u32[]{:S(2)}) collective-permute-start(f32[16,16,256]{2,1,0:T(8,128)S(1)} %get-tuple-element.34), channel_id=1, source_target_pairs={{16,0},{32,16},{48,32},{64,48},{80,64},{96,80},{112,96},{128,112},... | collective-permute-start | bytes 786440 | tf_op jit(solution)/shard_map/ppermute | solution.py:566
  36.0 16.7 %collective-permute-start.6 = (f32[256,256]{1,0:T(8,128)S(1)}, f32[256,256]{1,0:T(8,128)S(1)}, u32[]{:S(2)}, u32[]{:S(2)}) collective-permute-start(f32[256,256]{1,0:T(8,128)S(1)} %get-tuple-element.38), channel_id=1, source_target_pairs={{0,1},{1,2},{2,3},{3,4},{4,5},{5,6},{6,7},{7,8},{8,9},{9,10},{10,1... | collective-permute-start | bytes 786440 | tf_op jit(solution)/shard_map/ppermute | solution.py:578
  36.0 16.6 %collective-permute-start.7 = (f32[256,256]{1,0:T(8,128)S(1)}, f32[256,256]{1,0:T(8,128)S(1)}, u32[]{:S(2)}, u32[]{:S(2)}) collective-permute-start(f32[256,256]{1,0:T(8,128)S(1)} %get-tuple-element.39), channel_id=1, source_target_pairs={{1,0},{2,1},{3,2},{4,3},{5,4},{6,5},{7,6},{8,7},{9,8},{10,9},{11,1... | collective-permute-start | bytes 786440 | tf_op jit(solution)/shard_map/ppermute | solution.py:579
  41.6 11.1 %collective-permute-start.8 = (f32[32,256]{1,0:T(8,128)S(1)}, f32[32,256]{1,0:T(8,128)S(1)}, u32[]{:S(2)}, u32[]{:S(2)}) collective-permute-start(f32[32,256]{1,0:T(8,128)S(1)} %get-tuple-element.40), channel_id=1, source_target_pairs={{0,1},{1,2},{2,3},{3,4},{4,5},{5,6},{6,7},{7,8},{8,9},{9,10},{10,1... | collective-permute-start | bytes 98312 | tf_op jit(solution)/shard_map/ppermute | solution.py:590
  41.7 11.0 %collective-permute-start.9 = (f32[32,256]{1,0:T(8,128)S(1)}, f32[32,256]{1,0:T(8,128)S(1)}, u32[]{:S(2)}, u32[]{:S(2)}) collective-permute-start(f32[32,256]{1,0:T(8,128)S(1)} %get-tuple-element.35.after), channel_id=1, source_target_pairs={{1,0},{2,1},{3,2},{4,3},{5,4},{6,5},{7,6},{8,7},{9,8},{10,9},{11,1... | collective-permute-start | bytes 98312 | tf_op jit(solution)/shard_map/ppermute | solution.py:591

commit v5 on v3

--- a/solution.py
+++ b/solution.py
@@ -246,7 +246,7 @@
 
 def contact_kernel(
     count,
-    packed, first, second, ghost0, ghost1, ghost2, ghost3, rad, thick, tracers,
+    packed, first, second, ghost2, ghost3, ghost0, ghost1, rad, thick, tracers,
     new_velocity, values_high, values_low, sorted_pressure, head_rows, tail_rows,
     pressure_rows,
 ):
@@ -512,12 +512,11 @@
         cost_estimate=cost(1),
         name="outgoing",
     )(floe_position, floe_velocity, floe_radius, ghost_lists)
-    ghosts = [
-        lax.ppermute(outgoing[1], "gx", ring(nx)),
-        lax.ppermute(outgoing[0], "gx", back(nx)),
-        lax.ppermute(outgoing[3], "gy", ring(ny)),
-        lax.ppermute(outgoing[2], "gy", back(ny)),
-    ]
+    from_below = lax.ppermute(outgoing[3], "gy", ring(ny))
+    from_above = lax.ppermute(outgoing[2], "gy", back(ny))
+    from_left = lax.ppermute(outgoing[1], "gx", ring(nx))
+    from_right = lax.ppermute(outgoing[0], "gx", back(nx))
+    ghosts = [from_below, from_above, from_left, from_right]
 
     packed, edges = pl.pallas_call(
         prepare_kernel,

time: 55.8 us -> 55.7 us (level)
  waiting for transfers between devices: 7.97 us -> 6.99 us
  starting transfers between devices: 18.2 us -> 19.1 us
    ppermute x1, starting transfers between devices: 5.04 us -> 6.86 us  [shards(): side_l = lax.ppermute(tail_cols, 'gy', ring(ny))]
    ppermute x4, starting transfers between devices: 9.62 us -> 8.65 us  [the longest x1 5.3 us: shards(): from_right = lax.ppermute(outgoing[0], 'gx', back(nx))]
    ppermute x4, waiting for transfers between devices: 0.8 us -> 0.01 us  [the longest x1 0.01 us: shards(): from_above = lax.ppermute(outgoing[2], 'gy', back(ny))]
  transfers between devices with their start and end apart: 8 -> 8, of which waited for: 4 -> 2; matrix products, arithmetic and copies ran while one was open for 0% -> 0% of each run, Pallas kernels for 31% -> 31%
where the time goes in v5:
time: 55.7 us; the launch traced here: 55.4 us
  Pallas kernels  26.7 us (48%)
  starting transfers between devices  19.1 us (34%)
  waiting for transfers between devices  6.99 us (13%)
  between operations  1.59 us (3%)
  local copies, waits for them, and re-layouts  1.05 us (2%)
    pallas_call x1, Pallas kernels, shards(): pl.pallas_call(grid_kernel, in_specs=[smem()] + [vmem()] * 5, out_specs=[...  9.3 us
    ppermute x1, starting transfers between devices, shards(): side_l = lax.ppermute(tail_cols, 'gy', ring(ny))  6.86 us
    ppermute x1, waiting for transfers between devices, shards(): side_r = lax.ppermute(head_cols, 'gy', back(ny))  6.09 us
    pallas_call x1, Pallas kernels, shards(): pl.pallas_call(prepare_kernel, in_specs=[hbm()] * 7, out_shape=[struct(PA...  5.51 us
    ppermute x1, starting transfers between devices, shards(): from_right = lax.ppermute(outgoing[0], 'gx', back(nx))  5.3 us
    ppermute x1, starting transfers between devices, shards(): below = lax.ppermute(head_rows, 'gx', back(nx))  3.57 us
    pallas_call x1, Pallas kernels, shards(): pl.pallas_call(contact_kernel, in_specs=[smem()] + [vmem()] * 10, out_sha...  3.38 us
    pallas_call x1, Pallas kernels, shards(): pl.pallas_call(finish_kernel, in_specs=[vmem()] * 3, out_specs=anywhere()...  3.16 us
  transfers between devices with their start and end apart: 8, of which 2 were waited for; matrix products, arithmetic and copies ran while one was open for 0% of the time, Pallas kernels for 31%

profile of v5, /device:TPU:25, one launch (start us, length us, event | category | flops | bytes accessed | tf_op | source)
XLA Modules:
  0.0 55.4 jit_solution(13195240766076703647)
XLA Ops:
  0.6 2.2 %outgoing.1 = (f32[40,128]{1,0:T(8,128)}, f32[40,128]{1,0:T(8,128)}, f32[40,128]{1,0:T(8,128)}, f32[40,128]{1,0:T(8,128)}) custom-call(f32[1,1,2,4096]{3,2,1,0:T(2,128)} %pos_h.3, f32[1,1,2,4096]{3,2,1,0:T(2,128)} %vel_h.3, f32[1,1,4096]{2,1,0:T(1,128)} %rad_h.3, s32[1,1,4,1024]{3,2,1,0:T(4,128)} %lists_h.1), custom_call_target="tpu_custom_call" | custom-call | flops 1000000000 | bytes 1 | tf_op jit(solution)/shard_map/outgoing/pallas_call | solution.py:501
  2.8 3.0 %collective-permute-start = (f32[40,128]{1,0:T(8,128)}, f32[40,128]{1,0:T(8,128)S(1)}, u32[]{:S(2)}, u32[]{:S(2)}) collective-permute-start(f32[40,128]{1,0:T(8,128)} %get-tuple-element.23), channel_id=1, source_target_pairs={{0,1},{1,2},{2,3},{3,4},{4,5},{5,6},{6,7},{7,8},{8,9},{9,10},{10,1... | collective-permute-start | bytes 61448 | tf_op jit(solution)/shard_map/ppermute | solution.py:515
  5.9 0.0 collective-permute-start.1
  5.9 0.3 collective-permute-start.2
  6.2 5.3 %collective-permute-start.3 = (f32[40,128]{1,0:T(8,128)}, f32[40,128]{1,0:T(8,128)S(1)}, u32[]{:S(2)}, u32[]{:S(2)}) collective-permute-start(f32[40,128]{1,0:T(8,128)} %get-tuple-element.26), channel_id=1, source_target_pairs={{16,0},{32,16},{48,32},{64,48},{80,64},{96,80},{112,96},{128,112},... | collective-permute-start | bytes 61448 | tf_op jit(solution)/shard_map/ppermute | solution.py:518
  11.5 0.0 copy-start
  11.5 0.0 copy-start.1
  11.5 0.0 copy-start.2
  11.5 0.0 copy-start.3
  11.5 0.0 copy-start.4
  11.5 5.5 %prepare.1 = (f32[944,128]{1,0:T(8,128)}, s32[16,128]{1,0:T(8,128)}) custom-call(f32[1,1,2,4096]{3,2,1,0:T(2,128)} %pos_h.3, f32[1,1,2,4096]{3,2,1,0:T(2,128)} %vel_h.3, f32[1,1,4096]{2,1,0:T(1,128)} %rad_h.3, f32[1,1,16,4096]{3,2,1,0:T(8,128)} %tracers.3, s32[64,128]{1,0:T(8,128)} %bitcast.5, s32[64,128]{1,0:T(8,128)} %bitcast.7, s32[32,128]{1,0:T(8,128)} %bitcast.11), custom_call_target="tpu_custom_call" | custom-call | flops 5000000000 | bytes 1 | tf_op jit(solution)/shard_map/prepare/pallas_call | solution.py:521
  17.7 0.0 collective-permute-done.ghost2
  17.7 0.0 collective-permute-done.1.ghost3
  17.7 0.0 collective-permute-done.2.ghost0
  17.7 0.0 collective-permute-done.3.ghost1
  17.7 0.0 copy-done
  17.7 0.0 copy-done.1
  17.7 0.0 copy-done.2
  17.7 0.0 copy-done.3
  17.7 0.0 copy-done.4
  17.8 0.0 copy-start.5
  17.8 1.0 %copy-done.5 = f32[944,128]{1,0:T(8,128)S(1)} copy-done((f32[944,128]{1,0:T(8,128)S(1)}, f32[944,128]{1,0:T(8,128)}, u32[]{:S(2)}) %copy-start.5) | copy-done | bytes 483352
  18.8 0.0 copy-start.6
  18.8 3.4 %contact.1 = (f32[1,1,2,4096]{3,2,1,0:T(2,128)}, f32[16,4096]{1,0:T(8,128)S(1)}, f32[16,4096]{1,0:T(8,128)S(1)}, f32[32,128]{1,0:T(8,128)S(1)}, f32[16,16,256]{2,1,0:T(8,128)S(1)}, /*index=5*/f32[16,16,256]{2,1,0:T(8,128)S(1)}) custom-call(s32[1,1]{1,0:T(1,128)S(6)} %copy.13.count, f32[944,128]{1,0:T(8,128)S(1)} %copy-done.5, s32[64,128]{1,0:T(8,128)S(1)} %bitcast.6, ...), custom_call_target="tpu_custom_call" | custom-call | flops 5000000000 | bytes 1 | tf_op jit(solution)/shard_map/contact/pallas_call | solution.py:544
  22.2 0.0 collective-permute-start.4
  22.2 3.6 %collective-permute-start.5 = (f32[16,16,256]{2,1,0:T(8,128)S(1)}, f32[16,16,256]{2,1,0:T(8,128)S(1)}, u32[]{:S(2)}, u32[]{:S(2)}) collective-permute-start(f32[16,16,256]{2,1,0:T(8,128)S(1)} %get-tuple-element.35), channel_id=1, source_target_pairs={{16,0},{32,16},{48,32},{64,48},{80,64},{96,80},{112,96},{128,112},... | collective-permute-start | bytes 786440 | tf_op jit(solution)/shard_map/ppermute | solution.py:563
  25.7 0.0 copy-done.6
  25.7 9.3 %to_grid.1 = (f32[16,256,256]{2,1,0:T(8,128)}, f32[16,256,256]{2,1,0:T(8,128)S(1)}, f32[256,512]{1,0:T(8,128)S(1)}) custom-call(s32[16,128]{1,0:T(8,128)S(1)} %copy-done.6, f32[16,4096]{1,0:T(8,128)S(1)} %get-tuple-element.29.early_high, f32[16,4096]{1,0:T(8,128)S(1)} %get-tuple-element.30.early_low, f32[944,128]{1,0:T(8,128)S(1)} %copy-done.5, ...), custom_call_target="tpu_custom_call" | custom-call | flops 10000000000 | bytes 1 | tf_op jit(solution)/shard_map/to_grid/pallas_call | solution.py:565
  35.1 0.0 collective-permute-done.4.above
  35.1 0.0 collective-permute-done.5.below
  35.1 0.8 %fix_rows.1 = (f32[16,16,256]{2,1,0:T(8,128)S(1)}, f32[16,16,256]{2,1,0:T(8,128)S(1)}, f32[256,256]{1,0:T(8,128)S(1)}, f32[256,256]{1,0:T(8,128)S(1)}) custom-call(f32[16,256,256]{2,1,0:T(8,128)S(1)} %get-tuple-element.33.along, f32[16,16,256]{2,1,0:T(8,128)S(1)} %collective-permute-done.4.above, f32[16,16,256]{2,1,0:T(8,128)S(1)} %collective-permute-done.5.below, ...), custom_call_target="tpu_custom_call" | custom-call | flops 1000000000 | bytes 1 | tf_op jit(solution)/shard_map/fix_rows/pallas_call | solution.py:582
  35.9 6.9 %collective-permute-start.6 = (f32[256,256]{1,0:T(8,128)S(1)}, f32[256,256]{1,0:T(8,128)S(1)}, u32[]{:S(2)}, u32[]{:S(2)}) collective-permute-start(f32[256,256]{1,0:T(8,128)S(1)} %get-tuple-element.39), channel_id=1, source_target_pairs={{0,1},{1,2},{2,3},{3,4},{4,5},{5,6},{6,7},{7,8},{8,9},{9,10},{10,1... | collective-permute-start | bytes 786440 | tf_op jit(solution)/shard_map/ppermute | solution.py:592
  42.7 0.0 collective-permute-start.7
  42.7 2.4 %own_y.1.own = f32[16,256,256]{2,1,0:T(8,128)S(1)} custom-call(f32[16,256,256]{2,1,0:T(8,128)S(1)} %get-tuple-element.33.along, f32[16,16,256]{2,1,0:T(8,128)S(1)} %get-tuple-element.37.top, f32[16,16,256]{2,1,0:T(8,128)S(1)} %get-tuple-element.38.low), custom_call_target="tpu_custom_call" | custom-call | flops 4000000000 | bytes 1 | tf_op jit(solution)/shard_map/own_y/pallas_call | solution.py:595
  45.2 0.9 %collective-permute-done.6.side_l = f32[256,256]{1,0:T(8,128)S(1)} collective-permute-done((f32[256,256]{1,0:T(8,128)S(1)}, f32[256,256]{1,0:T(8,128)S(1)}, u32[]{:S(2)}, u32[]{:S(2)}) %collective-permute-start.6) | collective-permute-done | bytes 262176 | tf_op jit(solution)/shard_map/ppermute | solution.py:592
  46.0 6.1 %collective-permute-done.7.side_r = f32[256,256]{1,0:T(8,128)S(1)} collective-permute-done((f32[256,256]{1,0:T(8,128)S(1)}, f32[256,256]{1,0:T(8,128)S(1)}, u32[]{:S(2)}, u32[]{:S(2)}) %collective-permute-start.7) | collective-permute-done | bytes 262176 | tf_op jit(solution)/shard_map/ppermute | solution.py:593
  52.1 3.2 %finish.1 = f32[16,256,256]{2,1,0:T(8,128)} custom-call(f32[16,256,256]{2,1,0:T(8,128)S(1)} %own_y.1.own, f32[256,256]{1,0:T(8,128)S(1)} %collective-permute-done.6.side_l, f32[256,256]{1,0:T(8,128)S(1)} %collective-permute-done.7.side_r), custom_call_target="tpu_custom_call" | custom-call | flops 1000000000 | bytes 1 | tf_op jit(solution)/shard_map/finish/pallas_call | solution.py:605
Async XLA Ops:
  2.8 14.8 %collective-permute-start = (f32[40,128]{1,0:T(8,128)}, f32[40,128]{1,0:T(8,128)S(1)}, u32[]{:S(2)}, u32[]{:S(2)}) collective-permute-start(f32[40,128]{1,0:T(8,128)} %get-tuple-element.23), channel_id=1, source_target_pairs={{0,1},{1,2},{2,3},{3,4},{4,5},{5,6},{6,7},{7,8},{8,9},{9,10},{10,1... | collective-permute-start | bytes 61448 | tf_op jit(solution)/shard_map/ppermute | solution.py:515
  5.9 11.8 %collective-permute-start.1 = (f32[40,128]{1,0:T(8,128)}, f32[40,128]{1,0:T(8,128)S(1)}, u32[]{:S(2)}, u32[]{:S(2)}) collective-permute-start(f32[40,128]{1,0:T(8,128)} %get-tuple-element.24), channel_id=1, source_target_pairs={{1,0},{2,1},{3,2},{4,3},{5,4},{6,5},{7,6},{8,7},{9,8},{10,9},{11,1... | collective-permute-start | bytes 61448 | tf_op jit(solution)/shard_map/ppermute | solution.py:516
  5.9 11.8 %collective-permute-start.2 = (f32[40,128]{1,0:T(8,128)}, f32[40,128]{1,0:T(8,128)S(1)}, u32[]{:S(2)}, u32[]{:S(2)}) collective-permute-start(f32[40,128]{1,0:T(8,128)} %get-tuple-element.25), channel_id=1, source_target_pairs={{0,16},{16,32},{32,48},{48,64},{64,80},{80,96},{96,112},{112,128},... | collective-permute-start | bytes 61448 | tf_op jit(solution)/shard_map/ppermute | solution.py:517
  6.2 11.5 %collective-permute-start.3 = (f32[40,128]{1,0:T(8,128)}, f32[40,128]{1,0:T(8,128)S(1)}, u32[]{:S(2)}, u32[]{:S(2)}) collective-permute-start(f32[40,128]{1,0:T(8,128)} %get-tuple-element.26), channel_id=1, source_target_pairs={{16,0},{32,16},{48,32},{64,48},{80,64},{96,80},{112,96},{128,112},... | collective-permute-start | bytes 61448 | tf_op jit(solution)/shard_map/ppermute | solution.py:518
  11.5 6.2 %copy-start = (f32[1,1,16,4096]{3,2,1,0:T(8,128)S(1)}, f32[1,1,16,4096]{3,2,1,0:T(8,128)}, u32[]{:S(2)}) copy-start(f32[1,1,16,4096]{3,2,1,0:T(8,128)} %tracers.3) | copy-start | bytes 786436
  11.5 6.2 %copy-start.1 = (s32[1,1,8192]{2,1,0:T(1,128)S(1)}, s32[1,1,8192]{2,1,0:T(1,128)}, u32[]{:S(2)}) copy-start(s32[1,1,8192]{2,1,0:T(1,128)} %param.16) | copy-start | bytes 98308
  11.5 6.3 %copy-start.2 = (s32[1,1,8192]{2,1,0:T(1,128)S(1)}, s32[1,1,8192]{2,1,0:T(1,128)}, u32[]{:S(2)}) copy-start(s32[1,1,8192]{2,1,0:T(1,128)} %param.17) | copy-start | bytes 98308
  11.5 6.3 %copy-start.3 = (f32[1,1,4096]{2,1,0:T(1,128)S(1)}, f32[1,1,4096]{2,1,0:T(1,128)}, u32[]{:S(2)}) copy-start(f32[1,1,4096]{2,1,0:T(1,128)} %rad_h.3) | copy-start | bytes 49156
  11.5 6.3 %copy-start.4 = (f32[1,1,4096]{2,1,0:T(1,128)S(1)}, f32[1,1,4096]{2,1,0:T(1,128)}, u32[]{:S(2)}) copy-start(f32[1,1,4096]{2,1,0:T(1,128)} %param.13) | copy-start | bytes 49156
  17.8 1.0 %copy-start.5 = (f32[944,128]{1,0:T(8,128)S(1)}, f32[944,128]{1,0:T(8,128)}, u32[]{:S(2)}) copy-start(f32[944,128]{1,0:T(8,128)} %get-tuple-element.22.packed) | copy-start | bytes 1449988
  18.8 7.0 %copy-start.6 = (s32[16,128]{1,0:T(8,128)S(1)}, s32[16,128]{1,0:T(8,128)}, u32[]{:S(2)}) copy-start(s32[16,128]{1,0:T(8,128)} %get-tuple-element.28.edges_s) | copy-start | bytes 24580
  22.2 12.9 %collective-permute-start.4 = (f32[16,16,256]{2,1,0:T(8,128)S(1)}, f32[16,16,256]{2,1,0:T(8,128)S(1)}, u32[]{:S(2)}, u32[]{:S(2)}) collective-permute-start(f32[16,16,256]{2,1,0:T(8,128)S(1)} %get-tuple-element.34), channel_id=1, source_target_pairs={{0,16},{16,32},{32,48},{48,64},{64,80},{80,96},{96,112},{112,128},... | collective-permute-start | bytes 786440 | tf_op jit(solution)/shard_map/ppermute | solution.py:562
  22.2 12.9 %collective-permute-start.5 = (f32[16,16,256]{2,1,0:T(8,128)S(1)}, f32[16,16,256]{2,1,0:T(8,128)S(1)}, u32[]{:S(2)}, u32[]{:S(2)}) collective-permute-start(f32[16,16,256]{2,1,0:T(8,128)S(1)} %get-tuple-element.35), channel_id=1, source_target_pairs={{16,0},{32,16},{48,32},{64,48},{80,64},{96,80},{112,96},{128,112},... | collective-permute-start | bytes 786440 | tf_op jit(solution)/shard_map/ppermute | solution.py:563
  35.9 10.2 %collective-permute-start.6 = (f32[256,256]{1,0:T(8,128)S(1)}, f32[256,256]{1,0:T(8,128)S(1)}, u32[]{:S(2)}, u32[]{:S(2)}) collective-permute-start(f32[256,256]{1,0:T(8,128)S(1)} %get-tuple-element.39), channel_id=1, source_target_pairs={{0,1},{1,2},{2,3},{3,4},{4,5},{5,6},{6,7},{7,8},{8,9},{9,10},{10,1... | collective-permute-start | bytes 786440 | tf_op jit(solution)/shard_map/ppermute | solution.py:592
  42.7 9.4 %collective-permute-start.7 = (f32[256,256]{1,0:T(8,128)S(1)}, f32[256,256]{1,0:T(8,128)S(1)}, u32[]{:S(2)}, u32[]{:S(2)}) collective-permute-start(f32[256,256]{1,0:T(8,128)S(1)} %get-tuple-element.40), channel_id=1, source_target_pairs={{1,0},{2,1},{3,2},{4,3},{5,4},{6,5},{7,6},{8,7},{9,8},{10,9},{11,1... | collective-permute-start | bytes 786440 | tf_op jit(solution)/shard_map/ppermute | solution.py:593
